TPU v7x, 32 devices: a whole 2x2x4 slice. The times are simulated.
32 devices in a mesh: dp: 2 (over y), seq: 16 (over z, x, core).
Axes of the slice: x: 2, y: 2, z: 4, core: 2. Of those that a mesh axis runs over, the one named last changes fastest.
Arguments:
- atoms: float32 [4, 4096, 128], P('dp', 'seq'), may hold values from -6 to 6
- single_cond: float32 [4, 4096, 128], P('dp', 'seq'), may hold values from -6 to 6
- pair_block: float32 [4, 128, 16, 32, 128], P('dp', 'seq'), may hold values from -6 to 6
- atom_count: int32 [4], P('dp'), may hold values from 2048 to 4096, as said below
- s_gain1: float32 [128], replicated, may hold values from 0.5 to 1.5
- w_scale1: float32 [128, 128], replicated, may hold values from -0.5 to 0.5
- b_scale1: float32 [128], replicated, may hold values from -6 to 6
- w_shift1: float32 [128, 128], replicated, may hold values from -0.5 to 0.5
- w_query: float32 [128, 128], replicated, may hold values from -0.5 to 0.5
- b_query: float32 [128], replicated, may hold values from -3 to 3
- w_key: float32 [128, 128], replicated, may hold values from -0.5 to 0.5
- w_value: float32 [128, 128], replicated, may hold values from -0.5 to 0.5
- w_gate: float32 [128, 128], replicated, may hold values from -0.5 to 0.5
- pair_gain: float32 [16], replicated, may hold values from 0.5 to 1.5
- w_pair: float32 [16, 4], replicated, may hold values from -1.5 to 1.5
- w_out: float32 [128, 128], replicated, may hold values from -8 to 8
- w_zero1: float32 [128, 128], replicated, may hold values from -0.5 to 0.5
- b_zero1: float32 [128], replicated, may hold values from -6 to 6
- s_gain2: float32 [128], replicated, may hold values from 0.5 to 1.5
- w_scale2: float32 [128, 128], replicated, may hold values from -0.5 to 0.5
- b_scale2: float32 [128], replicated, may hold values from -6 to 6
- w_shift2: float32 [128, 128], replicated, may hold values from -0.5 to 0.5
- w_hidden_gate: float32 [128, 256], replicated, may hold values from -0.5 to 0.5
- w_hidden_up: float32 [128, 256], replicated, may hold values from -0.5 to 0.5
- w_down: float32 [256, 128], replicated, may hold values from -1.5 to 1.5
- w_zero2: float32 [128, 128], replicated, may hold values from -0.5 to 0.5
- b_zero2: float32 [128], replicated, may hold values from -6 to 6
- cotangent: float32 [4, 4096, 128], P('dp', 'seq'), may hold values from -6 to 6
Outputs:
- block_out: float32 [4, 4096, 128], P('dp', 'seq')
- grad_atoms: float32 [4, 4096, 128], P('dp', 'seq')
- grad_single: float32 [4, 4096, 128], P('dp', 'seq')
- grad_pair: float32 [4, 128, 16, 32, 128], P('dp', 'seq')
- grad_s_gain1: float32 [128], replicated
- grad_w_scale1: float32 [128, 128], replicated
- grad_b_scale1: float32 [128], replicated
- grad_w_shift1: float32 [128, 128], replicated
- grad_w_query: float32 [128, 128], replicated
- grad_b_query: float32 [128], replicated
- grad_w_key: float32 [128, 128], replicated
- grad_w_value: float32 [128, 128], replicated
- grad_w_gate: float32 [128, 128], replicated
- grad_pair_gain: float32 [16], replicated
- grad_w_pair: float32 [16, 4], replicated
- grad_w_out: float32 [128, 128], replicated
- grad_w_zero1: float32 [128, 128], replicated
- grad_b_zero1: float32 [128], replicated
- grad_s_gain2: float32 [128], replicated
- grad_w_scale2: float32 [128, 128], replicated
- grad_b_scale2: float32 [128], replicated
- grad_w_shift2: float32 [128, 128], replicated
- grad_w_hidden_gate: float32 [128, 256], replicated
- grad_w_hidden_up: float32 [128, 256], replicated
- grad_w_down: float32 [256, 128], replicated
- grad_w_zero2: float32 [128, 128], replicated
- grad_b_zero2: float32 [128], replicated
Inputs may be any that keep to these rules, and one draw needn't show every extreme that they name: `atom_count`: each sample's real atoms come first and the rest is padding; among the 2 samples of each dp index one, drawn from the seed, is full.
All inputs are finite; a program needn't handle non-finite values.
Results may differ from a plain program's by a relative error of at most 0.0003.
Values sent between devices are 32-bit elements; how exact they have to be, the bound alone decides.
A program may use at most 128 MiB of HBM per device.

v0:
```python
import math

import jax
import jax.numpy as jnp
from jax import lax
from jax.sharding import PartitionSpec as P

WQ = 32
KW = 128
HALO = 48


def with_halo(shard, sides, width):
    for axis, dim in sides:
        devices, length = (lax.axis_size(axis), shard.shape[dim])
        up = [(i, (i + 1) % devices) for i in range(devices - 1)]
        down = [(j, i) for i, j in up]
        last = lax.slice_in_dim(shard, length - width, length, axis=dim)
        initial = lax.slice_in_dim(shard, 0, width, axis=dim)
        before = lax.ppermute(last, axis, up)
        after = lax.ppermute(initial, axis, down)
        shard = jnp.concatenate([before, shard, after], axis=dim)
    return shard


def norm_rows(x):
    mean = jnp.mean(x, axis=-1, keepdims=True)
    cent = x - mean
    var = jnp.mean(cent * cent, axis=-1, keepdims=True)
    return cent * lax.rsqrt(var + 1e-05)


def matmul(x, w):
    return jnp.dot(x, w, precision=lax.Precision.HIGHEST, preferred_element_type=jnp.float32)


def window_blocks(ext, nwin, wq, reps):
    blocks = ext.reshape(nwin + reps - 1, wq, ext.shape[1])
    return jnp.concatenate([blocks[i : i + nwin] for i in range(reps)], axis=1)


def attend_core(query, keys, values, pair, pair_gain, w_pair, valid):
    nwin, wq, width = query.shape
    heads = w_pair.shape[1]
    size = width // heads
    kwid = keys.shape[1]
    q_four = query.reshape(nwin, wq, heads, size)
    k_four = keys.reshape(nwin, kwid, heads, size)
    v_four = values.reshape(nwin, kwid, heads, size)
    mean = jnp.mean(pair, axis=1, keepdims=True)
    cent = pair - mean
    var = jnp.mean(cent * cent, axis=1, keepdims=True)
    pair_norm = cent * lax.rsqrt(jnp.maximum(var, 0.25)) * pair_gain[None, :, None, None]
    bias = jnp.einsum("wpij,ph->whij", pair_norm, w_pair, precision=lax.Precision.HIGHEST)
    scores = (
        jnp.einsum("wihd,wjhd->whij", q_four, k_four, precision=lax.Precision.HIGHEST)
        / math.sqrt(size)
        + bias
    )
    scores = jnp.where(valid[:, None], scores, -1000000000.0)
    top = jnp.max(scores, axis=-1, keepdims=True)
    expo = jnp.exp(scores - top)
    weights = expo / jnp.sum(expo, axis=-1, keepdims=True)
    mixed = jnp.einsum("whij,wjhd->wihd", weights, v_four, precision=lax.Precision.HIGHEST)
    return mixed.reshape(nwin, wq, width)


def prepare(params, atoms, single):
    cond = norm_rows(single) * params[0]
    normed = jax.nn.sigmoid(matmul(cond, params[1]) + params[2]) * norm_rows(atoms) + matmul(
        cond, params[3]
    )
    query = matmul(normed, params[4]) + params[5]
    key_value = matmul(normed, jnp.concatenate([params[6], params[7]], axis=1))
    gate = jax.nn.sigmoid(matmul(normed, params[8]))
    return (query, key_value, gate)


def finish(params, atoms, single, pair, query, gate, kv_ext, valid):
    rows, width = query.shape
    nwin = rows // WQ
    reps = KW // WQ
    keys = window_blocks(kv_ext[:, :width], nwin, WQ, reps)
    values = window_blocks(kv_ext[:, width:], nwin, WQ, reps)
    mixed = jax.checkpoint(attend_core)(
        query.reshape(nwin, WQ, width), keys, values, pair, params[9], params[10], valid
    )
    gated = gate * mixed.reshape(rows, width)
    first = atoms + jax.nn.sigmoid(matmul(single, params[12]) + params[13]) * matmul(
        gated, params[11]
    )
    cond = norm_rows(single) * params[14]
    normed = jax.nn.sigmoid(matmul(cond, params[15]) + params[16]) * norm_rows(first) + matmul(
        cond, params[17]
    )
    hidden = jax.nn.silu(matmul(normed, params[18])) * matmul(normed, params[19])
    return first + jax.nn.sigmoid(matmul(single, params[21]) + params[22]) * matmul(
        hidden, params[20]
    )


def shards(
    atoms,
    single_cond,
    pair_block,
    atom_count,
    s_gain1,
    w_scale1,
    b_scale1,
    w_shift1,
    w_query,
    b_query,
    w_key,
    w_value,
    w_gate,
    pair_gain,
    w_pair,
    w_out,
    w_zero1,
    b_zero1,
    s_gain2,
    w_scale2,
    b_scale2,
    w_shift2,
    w_hidden_gate,
    w_hidden_up,
    w_down,
    w_zero2,
    b_zero2,
    cotangent,
):
    params = (
        s_gain1,
        w_scale1,
        b_scale1,
        w_shift1,
        w_query,
        b_query,
        w_key,
        w_value,
        w_gate,
        pair_gain,
        w_pair,
        w_out,
        w_zero1,
        b_zero1,
        s_gain2,
        w_scale2,
        b_scale2,
        w_shift2,
        w_hidden_gate,
        w_hidden_up,
        w_down,
        w_zero2,
        b_zero2,
    )
    samples = atoms.shape[0]
    rows = atoms.shape[1]
    nwin = rows // WQ
    start = lax.axis_index("seq") * rows
    qpos = (
        start
        + jnp.arange(nwin, dtype=jnp.int32)[:, None] * WQ
        + jnp.arange(WQ, dtype=jnp.int32)[None, :]
    )
    kpos = (
        start
        - HALO
        + jnp.arange(nwin, dtype=jnp.int32)[:, None] * WQ
        + jnp.arange(KW, dtype=jnp.int32)[None, :]
    )
    total = jax.tree.map(jnp.zeros_like, params)
    outs, grad_rows, grad_conds, grad_pairs = ([], [], [], [])
    for sample in range(samples):
        count = atom_count[sample]
        inside = (kpos >= 0) & (kpos < count)
        valid = inside[:, None, :] | (kpos[:, None, :] == qpos[:, :, None])
        pre_out, pre_back = jax.vjp(prepare, params, atoms[sample], single_cond[sample])
        query, key_value, gate = pre_out
        kv_ext = with_halo(key_value, (("seq", 0),), HALO)

        def closing(params, atoms_s, single_s, pair_s, query, gate, kv_ext):
            return finish(params, atoms_s, single_s, pair_s, query, gate, kv_ext, valid)

        result, post_back = jax.vjp(
            closing,
            params,
            atoms[sample],
            single_cond[sample],
            pair_block[sample],
            query,
            gate,
            kv_ext,
        )
        g_params, g_atoms, g_single, g_pair, g_query, g_gate, g_ext = post_back(cotangent[sample])
        rims = jnp.concatenate([g_ext[:HALO], g_ext[-HALO:]], axis=0)
        rims_ext = with_halo(rims, (("seq", 0),), HALO)
        g_kv = g_ext[HALO:-HALO]
        g_kv = g_kv.at[:HALO].add(rims_ext[:HALO])
        g_kv = g_kv.at[-HALO:].add(rims_ext[-HALO:])
        g_params_pre, g_atoms_pre, g_single_pre = pre_back((g_query, g_kv, g_gate))
        sample_grads = jax.tree.map(jnp.add, g_params, g_params_pre)
        total = jax.tree.map(jnp.add, total, tuple(sample_grads))
        outs.append(result)
        grad_rows.append(g_atoms + g_atoms_pre)
        grad_conds.append(g_single + g_single_pre)
        grad_pairs.append(g_pair)
    total = lax.psum(tuple(total), ("dp", "seq"))
    return (
        jnp.stack(outs),
        jnp.stack(grad_rows),
        jnp.stack(grad_conds),
        jnp.stack(grad_pairs),
    ) + tuple(total)


def solution(mesh):
    return jax.shard_map(
        shards,
        mesh=mesh,
        in_specs=(
            P("dp", "seq", None),
            P("dp", "seq", None),
            P("dp", "seq", None, None, None),
            P("dp"),
            P(),
            P(),
            P(),
            P(),
            P(),
            P(),
            P(),
            P(),
            P(),
            P(),
            P(),
            P(),
            P(),
            P(),
            P(),
            P(),
            P(),
            P(),
            P(),
            P(),
            P(),
            P(),
            P(),
            P("dp", "seq", None),
        ),
        out_specs=(
            P("dp", "seq", None),
            P("dp", "seq", None),
            P("dp", "seq", None),
            P("dp", "seq", None, None, None),
            P(),
            P(),
            P(),
            P(),
            P(),
            P(),
            P(),
            P(),
            P(),
            P(),
            P(),
            P(),
            P(),
            P(),
            P(),
            P(),
            P(),
            P(),
            P(),
            P(),
            P(),
            P(),
            P(),
        ),
        check_vma=False,
    )
```

profile of v0, /device:TPU:0, one launch (start us, length us, event | category | flops | bytes accessed | tf_op | source)
XLA Modules:
  0.0 596.8 jit_solution(17454970744067988900)
XLA Ops:
  16.4 3.0 collective-permute-start
  22.9 5.1 collective-permute-start.2
  36.0 4.6 copy_bitcast_fusion
  40.6 5.4 multiply_reduce_fusion.4
  53.1 5.3 fusion.5
  58.4 4.0 fusion.2
  63.4 2.0 fusion.320
  72.3 2.3 fusion.222
  76.5 2.0 copy.143
  80.6 2.1 copy.144
  84.6 2.1 copy.145
  92.6 2.0 copy.139
  96.6 2.0 copy.140
  100.6 2.0 copy.141
  106.7 3.0 fusion.424
  119.1 2.4 fusion.216
  123.5 2.1 copy.162
  127.6 2.1 copy.163
  135.7 2.0 copy.165
  138.8 2.0 copy.158
  142.8 2.1 copy.159
  146.8 2.0 copy.160
  152.8 3.1 fusion.427
  187.9 2.2 multiply_reduce_fusion.3
  195.0 3.0 fusion.14
  198.0 2.8 fusion.406
  214.5 2.1 convert_reduce_fusion.1
  232.8 2.2 fusion.382
  244.5 2.1 copy.203
  249.1 2.8 fusion.411
  265.5 2.2 convert_reduce_fusion
  282.9 2.5 fusion.430
  285.4 2.6 fusion.431
  289.9 2.0 copy.195
  297.6 2.0 fusion.259
  305.4 3.4 fusion.78
  308.8 4.4 multiply_reduce_fusion.1
  320.4 4.2 collective-permute-start.4
  324.7 3.7 collective-permute-start.6
  328.4 2.1 copy.217
  338.8 2.0 convolution_add_fusion.30
  340.8 2.0 convolution_add_fusion.31
  345.0 2.4 multiply_reduce_fusion
  347.5 2.9 fusion.84
  357.0 2.4 pad_maximum_fusion
  359.7 5.7 copy.236
  382.0 44.0 %all-reduce.20 = (f32[128]{0:T(128)}, f32[128]{0:T(128)}, f32[128]{0:T(128)}, f32[16]{0:T(128)}, f32[16,4]{0,1:T(4,128)}, /*index=5*/f32[128]{0:T(128)}, f32[128]{0:T(128)}, f32[128]{0:T(128)}, f32[128]{0:T(128)}) all-reduce(f32[128]{0:T(128)S(1)} %add.547, f32[128]{0:T(128)S(1)} %add.549, ...), channel_id=1, replica_groups=mesh['dp'=2,'seq'=16] {'dp','seq'}, use_global_device_ids=true, to_apply=%region_56.57 | all-reduce | flops 976 | bytes 7808 | tf_op jit(solution)/shard_map/psum | solution.py:208
  428.0 141.3 %all-reduce.24.cloned.1.call-done = (f32[128,128]{1,0:T(8,128)}, f32[128,128]{1,0:T(8,128)}, f32[128,128]{1,0:T(8,128)}, f32[128,128]{1,0:T(8,128)}, f32[128,128...) async-done(((f32[128,128]{1,0:T(8,128)}, ...) | async-done | bytes 1114128 | tf_op jit(solution)/shard_map/psum | solution.py:208
  (806 shorter events, 264.4 us)
Async XLA Ops:
  7.2 58.3 %copy-start = (f32[256,128]{1,0:T(8,128)S(1)}, f32[256,128]{1,0:T(8,128)}, u32[]{:S(2)}) copy-start(f32[256,128]{1,0:T(8,128)} %param.60) | copy-start | bytes 393220
  7.2 13.5 %copy-start.181 = (f32[128,128]{1,0:T(8,128)S(1)}, f32[128,128]{1,0:T(8,128)}, u32[]{:S(2)}) copy-start(f32[128,128]{1,0:T(8,128)} %param.41) | copy-start | bytes 196612
  7.3 13.5 %copy-start.255 = (f32[128]{0:T(128)S(1)}, f32[128]{0:T(128)}, u32[]{:S(2)}) copy-start(f32[128]{0:T(128)} %param.42) | copy-start | bytes 1540
  7.3 562.0 %all-reduce.24.cloned.1.call-start = ((), (), s32[]{:S(2)}) async-start(), calls=%async_computation | async-start | bytes 2228224 | tf_op jit(solution)/shard_map/psum | solution.py:208
  8.5 157.6 %copy-start.198 = (f32[256]{0:T(256)}, f32[256]{0:T(256)S(1)}, u32[]{:S(2)}) copy-start(f32[256]{0:T(256)S(1)} %get-tuple-element.398) | copy-start | bytes 3076
  8.5 159.5 %copy-start.196 = (f32[256]{0:T(256)}, f32[256]{0:T(256)S(1)}, u32[]{:S(2)}) copy-start(f32[256]{0:T(256)S(1)} %get-tuple-element.397) | copy-start | bytes 3076
  10.4 155.8 %copy-start.200 = (f32[256]{0:T(256)}, f32[256]{0:T(256)S(1)}, u32[]{:S(2)}) copy-start(f32[256]{0:T(256)S(1)} %fusion.327) | copy-start | bytes 3076
  13.4 16.2 %copy-start.127 = (f32[128,128]{1,0:T(8,128)S(1)}, f32[128,128]{1,0:T(8,128)}, u32[]{:S(2)}) copy-start(f32[128,128]{1,0:T(8,128)} %param.44) | copy-start | bytes 196612
  13.4 16.2 %copy-start.247 = (f32[128]{0:T(128)S(1)}, f32[128]{0:T(128)}, u32[]{:S(2)}) copy-start(f32[128]{0:T(128)} %param.45) | copy-start | bytes 1540
  14.9 16.8 %copy-start.183 = (f32[128,128]{1,0:T(8,128)S(1)}, f32[128,128]{1,0:T(8,128)}, u32[]{:S(2)}) copy-start(f32[128,128]{1,0:T(8,128)} %param.55) | copy-start | bytes 196612
  14.9 16.8 %copy-start.215 = (f32[128]{0:T(128)S(1)}, f32[128]{0:T(128)}, u32[]{:S(2)}) copy-start(f32[128]{0:T(128)} %param.54) | copy-start | bytes 1540
  14.9 16.8 %copy-start.256 = (f32[128]{0:T(128)S(1)}, f32[128]{0:T(128)}, u32[]{:S(2)}) copy-start(f32[128]{0:T(128)} %param.56) | copy-start | bytes 1540
  16.4 55.9 %collective-permute-start = (f32[48,256]{1,0:T(8,128)}, f32[48,256]{1,0:T(8,128)}, u32[]{:S(2)}, u32[]{:S(2)}) collective-permute-start(f32[48,256]{1,0:T(8,128)} %get-tuple-element.332), channel_id=1, source_target_pairs={{0,1},{1,2},{2,3},{3,4},{4,5},{5,6},{6,7},{7,8},{8,9},{9,10},{10,1... | collective-permute-start | bytes 147464 | tf_op jit(solution)/shard_map/ppermute | solution.py:20
  19.4 52.9 %collective-permute-start.1 = (f32[48,256]{1,0:T(8,128)}, f32[48,256]{1,0:T(8,128)}, u32[]{:S(2)}, u32[]{:S(2)}) collective-permute-start(f32[48,256]{1,0:T(8,128)} %get-tuple-element.333), channel_id=1, source_target_pairs={{1,0},{2,1},{3,2},{4,3},{5,4},{6,5},{7,6},{8,7},{9,8},{10,9},{11,1... | collective-permute-start | bytes 147464 | tf_op jit(solution)/shard_map/ppermute | solution.py:21
  20.7 147.3 %copy-start.202 = (f32[256]{0:T(256)}, f32[256]{0:T(256)S(1)}, u32[]{:S(2)}) copy-start(f32[256]{0:T(256)S(1)} %fusion.330) | copy-start | bytes 3076
  21.2 13.6 %copy-start.111 = (f32[256,128]{0,1:T(8,128)}, f32[256,128]{0,1:T(8,128)S(1)}, u32[]{:S(2)}) copy-start(f32[256,128]{0,1:T(8,128)S(1)} %fusion.65) | copy-start | bytes 393220
  21.2 12.6 %copy-start.186 = (f32[128,128]{1,0:T(8,128)S(1)}, f32[128,128]{1,0:T(8,128)}, u32[]{:S(2)}) copy-start(f32[128,128]{1,0:T(8,128)} %param.61) | copy-start | bytes 196612
  21.2 12.6 %copy-start.257 = (f32[128]{0:T(128)S(1)}, f32[128]{0:T(128)}, u32[]{:S(2)}) copy-start(f32[128]{0:T(128)} %param.62) | copy-start | bytes 1540
  21.3 142.8 %copy-start.25 = (f32[1,256,128]{1,2,0:T(8,128)}, f32[1,256,128]{1,2,0:T(8,128)S(1)}, u32[]{:S(2)}) copy-start(f32[1,256,128]{1,2,0:T(8,128)S(1)} %copy.274) | copy-start | bytes 393220
  21.4 13.8 %copy-start.234 = (f32[256]{0:T(256)}, f32[256]{0:T(256)S(1)}, u32[]{:S(2)}) copy-start(f32[256]{0:T(256)S(1)} %multiply_reduce_fusion.21) | copy-start | bytes 3076
  21.4 13.8 %copy-start.227 = (f32[256]{0:T(256)}, f32[256]{0:T(256)S(1)}, u32[]{:S(2)}) copy-start(f32[256]{0:T(256)S(1)} %fusion.331) | copy-start | bytes 3076
  21.4 13.8 %copy-start.30 = (f32[2,8,16,32,128]{4,3,2,1,0:T(8,128)S(1)}, f32[2,8,16,32,128]{4,3,2,1,0:T(8,128)}, u32[]{:S(2)}) copy-start(f32[2,8,16,32,128]{4,3,2,1,0:T(8,128)} %param.38) | copy-start | bytes 12582916
  22.3 13.6 %copy-start.73 = (f32[256,256]{1,0:T(8,128)}, f32[256,256]{1,0:T(8,128)S(1)}, u32[]{:S(2)}) copy-start(f32[256,256]{1,0:T(8,128)S(1)} %fusion.439) | copy-start | bytes 786436
  22.9 96.2 %collective-permute-start.2 = (f32[48,256]{1,0:T(8,128)}, f32[48,256]{1,0:T(8,128)}, u32[]{:S(2)}, u32[]{:S(2)}) collective-permute-start(f32[48,256]{1,0:T(8,128)} %get-tuple-element.339), channel_id=1, source_target_pairs={{0,1},{1,2},{2,3},{3,4},{4,5},{5,6},{6,7},{7,8},{8,9},{9,10},{10,1... | collective-permute-start | bytes 147464 | tf_op jit(solution)/shard_map/ppermute | solution.py:20
  28.1 91.1 %collective-permute-start.3 = (f32[48,256]{1,0:T(8,128)}, f32[48,256]{1,0:T(8,128)}, u32[]{:S(2)}, u32[]{:S(2)}) collective-permute-start(f32[48,256]{1,0:T(8,128)} %get-tuple-element.340), channel_id=1, source_target_pairs={{1,0},{2,1},{3,2},{4,3},{5,4},{6,5},{7,6},{8,7},{9,8},{10,9},{11,1... | collective-permute-start | bytes 147464 | tf_op jit(solution)/shard_map/ppermute | solution.py:21
  35.2 31.4 %copy-start.139 = (f32[256,128]{0,1:T(8,128)}, f32[256,128]{0,1:T(8,128)S(1)}, u32[]{:S(2)}) copy-start(f32[256,128]{0,1:T(8,128)S(1)} %fusion.67) | copy-start | bytes 393220
  52.0 13.4 %copy-start.52 = (f32[1,256,128]{1,2,0:T(8,128)}, f32[1,256,128]{1,2,0:T(8,128)S(1)}, u32[]{:S(2)}) copy-start(f32[1,256,128]{1,2,0:T(8,128)S(1)} %copy.276) | copy-start | bytes 393220
  114.3 66.0 %copy-start.71 = (f32[256,128]{0,1:T(8,128)}, f32[256,128]{0,1:T(8,128)S(1)}, u32[]{:S(2)}) copy-start(f32[256,128]{0,1:T(8,128)S(1)} %get-tuple-element.363) | copy-start | bytes 393220
  288.9 14.6 %copy-start.14 = (f32[8,4,32,128]{3,2,1,0:T(8,128)S(1)}, f32[8,4,32,128]{3,2,1,0:T(8,128)}, u32[]{:S(2)}) copy-start(f32[8,4,32,128]{3,2,1,0:T(8,128)} %copy-done.13) | copy-start | bytes 1572868
  293.8 11.6 %copy-start.2 = (f32[8,16,32,128]{3,1,2,0:T(8,128)S(1)}, f32[8,16,32,128]{3,1,2,0:T(8,128)}, u32[]{:S(2)}) copy-start(f32[8,16,32,128]{3,1,2,0:T(8,128)} %get-tuple-element.96) | copy-start | bytes 6291460
  293.8 11.6 %copy-start.32 = (f32[8,32,128]{2,1,0:T(8,128)S(1)}, f32[8,32,128]{2,1,0:T(8,128)}, u32[]{:S(2)}) copy-start(f32[8,32,128]{2,1,0:T(8,128)} %copy-done.31) | copy-start | bytes 393220
  293.8 11.6 %copy-start.210 = (f32[16]{0:T(128)S(1)}, f32[16]{0:T(128)}, u32[]{:S(2)}) copy-start(f32[16]{0:T(128)} %param.49) | copy-start | bytes 196
  320.4 45.9 %collective-permute-start.4 = (f32[48,256]{1,0:T(8,128)}, f32[48,256]{1,0:T(8,128)}, u32[]{:S(2)}, u32[]{:S(2)}) collective-permute-start(f32[48,256]{1,0:T(8,128)} %fusion.306), channel_id=1, source_target_pairs={{0,1},{1,2},{2,3},{3,4},{4,5},{5,6},{6,7},{7,8},{8,9},{9,10},{10,1... | collective-permute-start | bytes 147464 | tf_op jit(solution)/shard_map/ppermute | solution.py:20
  324.7 44.1 %collective-permute-start.6 = (f32[48,256]{1,0:T(8,128)}, f32[48,256]{1,0:T(8,128)}, u32[]{:S(2)}, u32[]{:S(2)}) collective-permute-start(f32[48,256]{1,0:T(8,128)} %fusion.310), channel_id=1, source_target_pairs={{0,1},{1,2},{2,3},{3,4},{4,5},{5,6},{6,7},{7,8},{8,9},{9,10},{10,1... | collective-permute-start | bytes 147464 | tf_op jit(solution)/shard_map/ppermute | solution.py:20
  328.4 15.6 %copy-start.16 = (f32[8,4,32,128]{3,2,1,0:T(8,128)S(1)}, f32[8,4,32,128]{3,2,1,0:T(8,128)}, u32[]{:S(2)}) copy-start(f32[8,4,32,128]{3,2,1,0:T(8,128)} %copy-done.15) | copy-start | bytes 1572868
  328.4 15.6 %copy-start.170 = (f32[8,4,32]{2,1,0:T(4,128)S(1)}, f32[8,4,32]{2,1,0:T(4,128)}, u32[]{:S(2)}) copy-start(f32[8,4,32]{2,1,0:T(4,128)} %copy-done.168) | copy-start | bytes 12292
  332.4 11.6 %copy-start.29 = (f32[4,8,32,128]{3,0,2,1:T(4,128)S(1)}, f32[4,8,32,128]{3,0,2,1:T(4,128)}, u32[]{:S(2)}) copy-start(f32[4,8,32,128]{3,0,2,1:T(4,128)} %copy-done.28) | copy-start | bytes 1572868
  332.4 11.6 %copy-start.70 = (f32[8,4,32,128]{3,2,1,0:T(8,128)S(1)}, f32[8,4,32,128]{3,2,1,0:T(8,128)}, u32[]{:S(2)}) copy-start(f32[8,4,32,128]{3,2,1,0:T(8,128)} %get-tuple-element.382) | copy-start | bytes 1572868
  332.4 11.6 %copy-start.78 = (pred[8,32,128]{2,1,0:T(8,128)(4,1)S(1)}, pred[8,32,128]{2,1,0:T(8,128)(4,1)}, u32[]{:S(2)}) copy-start(pred[8,32,128]{2,1,0:T(8,128)(4,1)} %get-tuple-element.100) | copy-start | bytes 98308
  332.4 11.6 %copy-start.175 = (f32[4,8,32]{2,1,0:T(8,128)S(1)}, f32[4,8,32]{2,1,0:T(8,128)}, u32[]{:S(2)}) copy-start(f32[4,8,32]{2,1,0:T(8,128)} %copy-done.173) | copy-start | bytes 12292
  332.4 11.6 %copy-start.180 = (f32[8,4,32]{2,1,0:T(4,128)S(1)}, f32[8,4,32]{2,1,0:T(4,128)}, u32[]{:S(2)}) copy-start(f32[8,4,32]{2,1,0:T(4,128)} %copy-done.178) | copy-start | bytes 12292
  332.4 11.6 %copy-start.212 = (f32[4,8,32]{2,0,1:T(4,128)S(1)}, f32[4,8,32]{2,0,1:T(4,128)}, u32[]{:S(2)}) copy-start(f32[4,8,32]{2,0,1:T(4,128)} %get-tuple-element.352) | copy-start | bytes 12292
  367.5 3.5 collective-permute-start.5
  369.6 3.8 collective-permute-start.7
  379.9 46.2 %copy-start.103 = (f32[256,128]{0,1:T(8,128)S(1)}, f32[256,128]{0,1:T(8,128)}, u32[]{:S(2)}) copy-start(f32[256,128]{0,1:T(8,128)} %get-tuple-element.224) | copy-start | bytes 393220
  379.9 46.2 %copy-start.128 = (f32[128,128]{1,0:T(8,128)S(1)}, f32[128,128]{1,0:T(8,128)}, u32[]{:S(2)}) copy-start(f32[128,128]{1,0:T(8,128)} %param.52) | copy-start | bytes 196612
  426.0 163.4 %copy-start.1 = (f32[256,128]{1,0:T(8,128)S(1)}, f32[256,128]{1,0:T(8,128)}, u32[]{:S(2)}) copy-start(f32[256,128]{1,0:T(8,128)} %param.60) | copy-start | bytes 393220
  569.2 19.6 %copy-start.194 = (f32[256,128]{1,0:T(8,128)S(1)}, f32[256,128]{1,0:T(8,128)}, u32[]{:S(2)}) copy-start(f32[256,128]{1,0:T(8,128)} %get-tuple-element.429) | copy-start | bytes 393220
  (221 other events, 1068.9 us)
Sparse Core Ops, SparseCore 0:
  426.2 143.0 all-reduce.23
where the time goes:
time: 604 us; the launch traced here: 597 us
  local copies, waits for them, and re-layouts  175 us (29%)
  waiting for transfers between devices  142 us (24%)
  matrix products  133 us (22%)
  other arithmetic  62.7 us (10%)
  blocking collectives  44 us (7%)
  starting transfers between devices  21.4 us (4%)
  between operations  18.3 us (3%)
    psum x1, waiting for transfers between devices, shards(): total = lax.psum(tuple(total), ('dp', 'seq'))  141 us
    dot_general x78, matrix products, matmul(): jnp.dot(x, w, precision=lax.Precision.HIGHEST, preferred_element_type=jnp...  78 us
    unnamed x558, local copies, waits for them, and re-layouts  65.7 us
    concatenate x32, local copies, waits for them, and re-layouts, window_blocks(): return jnp.concatenate([blocks[i:i + nwin] for i in range(reps)], axis=1)  63.3 us
    psum x1, blocking collectives, shards(): total = lax.psum(tuple(total), ('dp', 'seq'))  44 us
    dot_general x8, matrix products, attend_core(): jnp.einsum('wpij,ph->whij', pair_norm, w_pair, precision=lax.Precision.HI...  26.7 us
    dot_general x8, matrix products, attend_core(): jnp.einsum('wihd,wjhd->whij', q_four, k_four, precision=lax.Precision.HIG...  18.3 us
    ppermute x4, starting transfers between devices, with_halo(): before = lax.ppermute(last, axis, up)  16 us
  transfers between devices with their start and end apart: 9, of which 2 were waited for; matrix products, arithmetic and copies ran while one was open for 22% of the time, Pallas kernels for 0%

commit v1 on v0

v1 whole, which is shorter than its diff:
```python
import functools
import math

import jax
import jax.numpy as jnp
from jax import lax
from jax.experimental import pallas as pl
from jax.experimental.pallas import tpu as pltpu
from jax.sharding import PartitionSpec as P

WQ = 32
KW = 128
HALO = 48
LANES = 128
MESH = pl.DeviceIdType.MESH
F32 = jnp.float32
HIGH = lax.Precision.HIGH

MATRICES = (
    ("w_down", 2, 1),
    ("w_hidden_gate", 1, 2),
    ("w_hidden_up", 1, 2),
    ("w_zero2", 1, 1),
    ("w_scale2", 1, 1),
    ("w_shift2", 1, 1),
    ("w_out", 1, 1),
    ("w_zero1", 1, 1),
    ("w_query", 1, 1),
    ("w_key", 1, 1),
    ("w_value", 1, 1),
    ("w_gate", 1, 1),
    ("w_scale1", 1, 1),
    ("w_shift1", 1, 1),
)
VECTORS = ("b_scale1", "b_query", "b_scale2", "b_zero1", "b_zero2", "s_gain1", "s_gain2", "pair_gain")
PARAMS = (
    "s_gain1",
    "w_scale1",
    "b_scale1",
    "w_shift1",
    "w_query",
    "b_query",
    "w_key",
    "w_value",
    "w_gate",
    "pair_gain",
    "w_pair",
    "w_out",
    "w_zero1",
    "b_zero1",
    "s_gain2",
    "w_scale2",
    "b_scale2",
    "w_shift2",
    "w_hidden_gate",
    "w_hidden_up",
    "w_down",
    "w_zero2",
    "b_zero2",
)


def offsets():
    place, row = {}, 0
    for name, rows, columns in MATRICES:
        place[name] = row
        row += rows * columns * LANES
    place["vectors"] = row
    place["w_pair"] = row + 8
    return place, row + 16


PLACE, USED = offsets()


def nn(a, b):
    return lax.dot_general(a, b, (((1,), (0,)), ((), ())), precision=HIGH, preferred_element_type=F32)


def nt(a, b):
    return lax.dot_general(a, b, (((1,), (1,)), ((), ())), precision=HIGH, preferred_element_type=F32)


def tn(a, b):
    return lax.dot_general(a, b, (((0,), (0,)), ((), ())), precision=HIGH, preferred_element_type=F32)


def norm(x):
    mean = jnp.mean(x, axis=-1, keepdims=True)
    cent = x - mean
    var = jnp.mean(cent * cent, axis=-1, keepdims=True)
    inv = lax.rsqrt(var + 1e-05)
    return cent * inv, inv


def norm_back(d, xhat, inv):
    mean = jnp.mean(d, axis=-1, keepdims=True)
    along = jnp.mean(d * xhat, axis=-1, keepdims=True)
    return (d - mean - xhat * along) * inv


def sigmoid(x):
    return 1.0 / (1.0 + jnp.exp(-x))


def column_sum(x):
    return jnp.sum(x, axis=0, keepdims=True)


def block_kernel(sizes, *refs):
    samples, rows, dpn, seqn, packed = sizes
    nwin = rows // WQ
    nz = 4
    nx = seqn // (2 * nz)
    nxy = dpn * nx
    half = packed // 2
    part = half // nxy
    chunk = part // nz
    (
        count,
        gain_s,
        wpair_s,
        atoms,
        single,
        cot,
        p_s_gain1,
        p_w_scale1,
        p_b_scale1,
        p_w_shift1,
        p_w_query,
        p_b_query,
        p_w_key,
        p_w_value,
        p_w_gate,
        p_pair_gain,
        p_w_pair,
        p_w_out,
        p_w_zero1,
        p_b_zero1,
        p_s_gain2,
        p_w_scale2,
        p_b_scale2,
        p_w_shift2,
        p_w_hidden_gate,
        p_w_hidden_up,
        p_w_down,
        p_w_zero2,
        p_b_zero2,
        pair_hbm,
        out,
        g_atoms,
        g_single,
        g_pair_hbm,
        res,
        pair,
        bias,
        pmean,
        prs,
        prob,
        ds,
        kv,
        dkv,
        dhalo,
        q_s,
        gate_s,
        mixed_s,
        cond1_s,
        cond2_s,
        ns_s,
        na_s,
        n1_s,
        sc1_s,
        sc2_s,
        sh2_s,
        z1_s,
        z2_s,
        rs_s,
        ra_s,
        dq_s,
        dfirst_s,
        dz1_s,
        dz2_s,
        dn2_s,
        dsc2_s,
        gpre_s,
        gacc,
        acc,
        recv_c,
        recv_xy,
        recv_z,
        pair_sem,
        gp_sem,
        h_send,
        h_recv,
        c_send,
        c_recv,
        xy_send,
        xy_recv,
        z_send,
        z_recv,
    ) = refs
    dp = lax.axis_index("dp")
    me = lax.axis_index("seq")
    core = lax.rem(me, 2)
    x = lax.rem(me // 2, nx)
    z = me // (2 * nx)
    k = dp * nx + x
    left = (dp, lax.rem(me + seqn - 1, seqn))
    right = (dp, lax.rem(me + 1, seqn))
    other = (dp, me + 1 - 2 * core)

    def xy_peer(o):
        kk = lax.rem(k + o, nxy)
        return kk, (kk // nx, (z * nx + lax.rem(kk, nx)) * 2 + core)

    def z_peer(o):
        zz = lax.rem(z + o, nz)
        return zz, (dp, (zz * nx + x) * 2 + core)

    for s in range(samples):
        pltpu.make_async_copy(pair_hbm.at[s], pair.at[s], pair_sem.at[s]).start()

    barrier = pltpu.get_barrier_semaphore()
    greeted = [left, right, other]
    greeted += [xy_peer(o)[1] for o in range(1, nxy)]
    greeted += [z_peer(o)[1] for o in range(1, nz)]
    for device in greeted:
        pl.semaphore_signal(barrier, inc=1, device_id=device, device_id_type=MESH)

    def three(ref):
        return ref[...].reshape(samples * rows, ref.shape[-1])

    ns, rs = norm(single[...])
    na, ra = norm(atoms[...])
    ns_s[...] = ns
    na_s[...] = na
    rs_s[...] = rs
    ra_s[...] = ra
    cond1 = ns * p_s_gain1[...]
    cond1_s[...] = cond1
    sc1 = sigmoid(nn(cond1, p_w_scale1[...]) + p_b_scale1[...])
    sc1_s[...] = sc1
    n1 = sc1 * na + nn(cond1, p_w_shift1[...])
    n1_s[...] = n1
    keys = nn(n1, p_w_key[...])
    values = nn(n1, p_w_value[...])
    for s in range(samples):
        kv[s, HALO : HALO + rows, 0:LANES] = keys[s * rows : (s + 1) * rows]
        kv[s, HALO : HALO + rows, LANES : 2 * LANES] = values[s * rows : (s + 1) * rows]

    pl.semaphore_wait(barrier, len(greeted))
    to_right = pltpu.make_async_remote_copy(
        src_ref=kv.at[:, rows : rows + HALO],
        dst_ref=kv.at[:, 0:HALO],
        send_sem=h_send.at[0],
        recv_sem=h_recv.at[0],
        device_id=right,
        device_id_type=MESH,
    )
    to_left = pltpu.make_async_remote_copy(
        src_ref=kv.at[:, HALO : 2 * HALO],
        dst_ref=kv.at[:, HALO + rows : 2 * HALO + rows],
        send_sem=h_send.at[1],
        recv_sem=h_recv.at[1],
        device_id=left,
        device_id_type=MESH,
    )
    to_right.start()
    to_left.start()

    scale = 1.0 / math.sqrt(32)
    q_s[...] = (nn(n1, p_w_query[...]) + p_b_query[...]) * scale
    gate_s[...] = sigmoid(nn(n1, p_w_gate[...]))
    cond2 = ns * p_s_gain2[...]
    cond2_s[...] = cond2
    sc2_s[...] = sigmoid(nn(cond2, p_w_scale2[...]) + p_b_scale2[...])
    sh2_s[...] = nn(cond2, p_w_shift2[...])
    z1_s[...] = sigmoid(nn(single[...], p_w_zero1[...]) + p_b_zero1[...])
    z2_s[...] = sigmoid(nn(single[...], p_w_zero2[...]) + p_b_zero2[...])

    channels = gain_s.shape[0]
    heads = wpair_s.shape[0]
    wg = [[gain_s[p] * wpair_s[h, p] for h in range(heads)] for p in range(channels)]
    wsum = [functools.reduce(lambda a, b: a + b, [wg[p][h] for p in range(channels)]) for h in range(heads)]

    for s in range(samples):
        pltpu.make_async_copy(pair_hbm.at[s], pair.at[s], pair_sem.at[s]).wait()

    def pair_bias(t, carry):
        s, w = t // nwin, lax.rem(t, nwin)
        first = pair[s, w, 0]
        total, square = first, first * first
        b = [first * wg[0][h] for h in range(heads)]
        for p in range(1, channels):
            v = pair[s, w, p]
            total = total + v
            square = square + v * v
            b = [b[h] + v * wg[p][h] for h in range(heads)]
        mean = total * (1.0 / channels)
        var = square * (1.0 / channels) - mean * mean
        inv = lax.rsqrt(jnp.maximum(var, 0.25))
        pmean[t] = mean
        live = jnp.where(var > 0.25, 1.0, jnp.where(var == 0.25, 0.5, 0.0))
        prs[t, 0] = inv
        prs[t, 1] = inv * inv * live * (1.0 / channels)
        for h in range(heads):
            bias[t, h * WQ : (h + 1) * WQ] = inv * (b[h] - mean * wsum[h])
        return carry

    lax.fori_loop(0, samples * nwin, pair_bias, 0)

    to_right.wait()
    to_left.wait()
    for s in range(samples):
        kv[s, 0:HALO] = jnp.where(me == 0, 0.0, kv[s, 0:HALO])
        kv[s, HALO + rows :] = jnp.where(me == seqn - 1, 0.0, kv[s, HALO + rows :])

    lane = lax.broadcasted_iota(jnp.int32, (heads * WQ, LANES), 1)
    row = lax.broadcasted_iota(jnp.int32, (heads * WQ, LANES), 0)
    own = (lane // 32 == row // WQ).astype(F32)
    same = lane == lax.rem(row, WQ) + HALO

    def window(t):
        s, w = t // nwin, lax.rem(t, nwin)
        return s, w, pl.multiple_of(s * rows + w * WQ, WQ), pl.multiple_of(w * WQ, WQ)

    def heads_in(v):
        return jnp.concatenate([v] * heads, axis=0) * own

    def heads_out(v):
        v = v * own
        return (v[0:WQ] + v[WQ : 2 * WQ]) + (v[2 * WQ : 3 * WQ] + v[3 * WQ : 4 * WQ])

    def attend(t, carry):
        s, w, at, key_at = window(t)
        queries = heads_in(q_s[pl.ds(at, WQ), :])
        key = kv[s, pl.ds(key_at, KW), 0:LANES]
        value = kv[s, pl.ds(key_at, KW), LANES : 2 * LANES]
        scores = nt(queries, key) + bias[t]
        begin = me * rows + w * WQ - HALO
        inside = (lane >= -begin) & (lane < count[s] - begin)
        scores = jnp.where(inside | same, scores, -1e9)
        top = jnp.max(scores, axis=-1, keepdims=True)
        expo = jnp.exp(scores - top)
        weights = expo / jnp.sum(expo, axis=-1, keepdims=True)
        prob[t] = weights
        mixed_s[pl.ds(at, WQ), :] = heads_out(nn(weights, value))
        return carry

    lax.fori_loop(0, samples * nwin, attend, 0)

    gated = gate_s[...] * mixed_s[...]
    projected = nn(gated, p_w_out[...])
    first = atoms[...] + z1_s[...] * projected
    nf, rf = norm(first)
    n2 = sc2_s[...] * nf + sh2_s[...]
    hg = nn(n2, p_w_hidden_gate[...])
    hu = nn(n2, p_w_hidden_up[...])
    sg = sigmoid(hg)
    silu = hg * sg
    hidden = silu * hu
    down = nn(hidden, p_w_down[...])
    z2 = z2_s[...]
    g = cot[...]
    out[...] = first + z2 * down

    def put(name, value):
        base = PLACE[name]
        for b in range(value.shape[1] // LANES):
            at = base + b * value.shape[0]
            acc[at : at + value.shape[0]] = value[:, b * LANES : (b + 1) * LANES]

    d_down = g * z2
    dz2 = g * down * z2 * (1.0 - z2)
    dz2_s[...] = dz2
    put("w_down", tn(hidden, d_down))
    d_hidden = nt(d_down, p_w_down[...])
    d_hg = d_hidden * hu * (sg * (1.0 + hg * (1.0 - sg)))
    d_hu = d_hidden * silu
    put("w_hidden_gate", tn(n2, d_hg))
    put("w_hidden_up", tn(n2, d_hu))
    put("w_zero2", tn(single[...], dz2))
    d_n2 = nt(d_hg, p_w_hidden_gate[...]) + nt(d_hu, p_w_hidden_up[...])
    dn2_s[...] = d_n2
    sc2 = sc2_s[...]
    dsc2 = d_n2 * nf * sc2 * (1.0 - sc2)
    dsc2_s[...] = dsc2
    put("w_scale2", tn(cond2_s[...], dsc2))
    put("w_shift2", tn(cond2_s[...], d_n2))
    d_first = g + norm_back(d_n2 * sc2, nf, rf)
    dfirst_s[...] = d_first
    z1 = z1_s[...]
    d_proj = d_first * z1
    dz1 = d_first * projected * z1 * (1.0 - z1)
    dz1_s[...] = dz1
    put("w_out", tn(gated, d_proj))
    put("w_zero1", tn(single[...], dz1))
    d_gated = nt(d_proj, p_w_out[...])
    gate = gate_s[...]
    mixed = mixed_s[...]
    gpre_s[...] = d_gated * mixed * gate * (1.0 - gate)
    mixed_s[...] = d_gated * gate

    dkv[...] = jnp.zeros_like(dkv)

    def attend_back(t, carry):
        s, w, at, key_at = window(t)
        queries = heads_in(q_s[pl.ds(at, WQ), :])
        d_mixed = heads_in(mixed_s[pl.ds(at, WQ), :])
        key = kv[s, pl.ds(key_at, KW), 0:LANES]
        value = kv[s, pl.ds(key_at, KW), LANES : 2 * LANES]
        weights = prob[t]
        d_weights = nt(d_mixed, value)
        d_scores = weights * (d_weights - jnp.sum(weights * d_weights, axis=-1, keepdims=True))
        ds[t] = d_scores
        dq_s[pl.ds(at, WQ), :] = heads_out(nn(d_scores, key)) * scale
        dkv[s, pl.ds(key_at, KW), 0:LANES] += tn(d_scores, queries)
        dkv[s, pl.ds(key_at, KW), LANES : 2 * LANES] += tn(weights, d_mixed)
        return carry

    lax.fori_loop(0, samples * nwin, attend_back, 0)

    back_left = pltpu.make_async_remote_copy(
        src_ref=dkv.at[:, 0:HALO],
        dst_ref=dhalo.at[1],
        send_sem=h_send.at[2],
        recv_sem=h_recv.at[2],
        device_id=left,
        device_id_type=MESH,
    )
    back_right = pltpu.make_async_remote_copy(
        src_ref=dkv.at[:, HALO + rows : 2 * HALO + rows],
        dst_ref=dhalo.at[0],
        send_sem=h_send.at[3],
        recv_sem=h_recv.at[3],
        device_id=right,
        device_id_type=MESH,
    )
    back_left.start()
    back_right.start()

    gacc[...] = jnp.zeros_like(gacc)

    def pair_back(t, carry):
        s, w = t // nwin, lax.rem(t, nwin)
        inv, live = prs[t, 0], prs[t, 1]
        mean = pmean[t]
        u, along, level = [], None, None
        for h in range(heads):
            d = ds[t, h * WQ : (h + 1) * WQ]
            u.append(d * inv)
            a = d * bias[t, h * WQ : (h + 1) * WQ]
            b = u[h] * (wsum[h] * (1.0 / channels))
            along = a if along is None else along + a
            level = b if level is None else level + b
        c1 = along * live
        c0 = mean * c1 - level
        mu = [mean * u[h] for h in range(heads)]
        for p in range(channels):
            v = pair[s, w, p]
            d = c0 - v * c1
            for h in range(heads):
                d = d + u[h] * wg[p][h]
                product = v * u[h] - mu[h]
                gacc[h * channels + p] += (product[0:8] + product[8:16]) + (product[16:24] + product[24:32])
            pair[s, w, p] = d
        return carry

    lax.fori_loop(0, samples * nwin, pair_back, 0)

    for s in range(samples):
        pltpu.make_async_copy(pair.at[s], g_pair_hbm.at[s], gp_sem.at[s]).start()

    back_left.wait()
    back_right.wait()
    for s in range(samples):
        dkv[s, HALO : 2 * HALO] += dhalo[0, s]
        dkv[s, rows : rows + HALO] += dhalo[1, s]

    n1 = n1_s[...]
    dq = dq_s[...]
    d_keys = jnp.concatenate([dkv[s, HALO : HALO + rows, 0:LANES] for s in range(samples)], axis=0)
    d_values = jnp.concatenate([dkv[s, HALO : HALO + rows, LANES : 2 * LANES] for s in range(samples)], axis=0)
    d_gate = gpre_s[...]
    put("w_query", tn(n1, dq))
    put("w_key", tn(n1, d_keys))
    put("w_value", tn(n1, d_values))
    put("w_gate", tn(n1, d_gate))
    d_n1 = (nt(dq, p_w_query[...]) + nt(d_keys, p_w_key[...])) + (
        nt(d_values, p_w_value[...]) + nt(d_gate, p_w_gate[...])
    )
    na = na_s[...]
    sc1 = sc1_s[...]
    dsc1 = d_n1 * na * sc1 * (1.0 - sc1)
    put("w_scale1", tn(cond1_s[...], dsc1))
    put("w_shift1", tn(cond1_s[...], d_n1))
    g_atoms[...] = dfirst_s[...] + norm_back(d_n1 * sc1, na, ra_s[...])
    ns = ns_s[...]
    d_cond1 = nt(dsc1, p_w_scale1[...]) + nt(d_n1, p_w_shift1[...])
    d_cond2 = nt(dsc2_s[...], p_w_scale2[...]) + nt(dn2_s[...], p_w_shift2[...])
    d_ns = d_cond1 * p_s_gain1[...] + d_cond2 * p_s_gain2[...]
    g_single[...] = norm_back(d_ns, ns, rs_s[...]) + (
        nt(dz1_s[...], p_w_zero1[...]) + nt(dz2_s[...], p_w_zero2[...])
    )

    eye = (
        lax.broadcasted_iota(jnp.int32, (channels, LANES), 0) == lax.broadcasted_iota(jnp.int32, (channels, LANES), 1)
    ).astype(F32)
    gsum = jnp.sum(jnp.sum(gacc[...], axis=1), axis=-1, keepdims=True)
    rows_g = [column_sum(gsum[h * channels : (h + 1) * channels] * eye) for h in range(heads)]
    blank = jnp.zeros((1, LANES - channels), F32)
    gain_row = jnp.concatenate([p_pair_gain[...], blank], axis=1)
    pair_row = jnp.zeros((1, LANES), F32)
    for h in range(heads):
        pair_row = pair_row + rows_g[h] * jnp.concatenate([p_w_pair[h : h + 1, :], blank], axis=1)
    pair_grad = jnp.concatenate([v * gain_row for v in rows_g] + [jnp.zeros((8 - heads, LANES), F32)], axis=0)
    small = {
        "b_scale1": column_sum(dsc1),
        "b_query": column_sum(dq),
        "b_scale2": column_sum(dsc2_s[...]),
        "b_zero1": column_sum(dz1_s[...]),
        "b_zero2": column_sum(dz2_s[...]),
        "s_gain1": column_sum(d_cond1 * ns),
        "s_gain2": column_sum(d_cond2 * ns),
        "pair_gain": pair_row,
    }
    acc[PLACE["vectors"] : PLACE["vectors"] + 8] = jnp.concatenate([small[name] for name in VECTORS], axis=0)
    acc[PLACE["w_pair"] : PLACE["w_pair"] + 8] = pair_grad
    acc[USED:] = jnp.zeros((packed - USED, LANES), F32)

    def remote(src, dst, send, recv, device):
        return pltpu.make_async_remote_copy(
            src_ref=src, dst_ref=dst, send_sem=send, recv_sem=recv, device_id=device, device_id_type=MESH
        )

    def span(start, size):
        return pl.ds(pl.multiple_of(start, 8), size)

    mine = core * half
    copy = remote(acc.at[span((1 - core) * half, half)], recv_c, c_send.at[0], c_recv.at[0], other)
    copy.start()
    copy.wait()
    acc[span(mine, half), :] += recv_c[...]

    copies = []
    for o in range(1, nxy):
        kk, device = xy_peer(o)
        copies.append(
            remote(
                acc.at[span(mine + kk * part, part)], recv_xy.at[o - 1], xy_send.at[o - 1], xy_recv.at[o - 1], device
            )
        )
    for copy in copies:
        copy.start()
    for copy in copies:
        copy.wait()
    mine_xy = mine + k * part
    value = acc[span(mine_xy, part), :]
    for o in range(1, nxy):
        value = value + recv_xy[o - 1]
    acc[span(mine_xy, part), :] = value

    copies = []
    for o in range(1, nz):
        zz, device = z_peer(o)
        copies.append(
            remote(
                acc.at[span(mine_xy + zz * chunk, chunk)], recv_z.at[o - 1], z_send.at[o - 1], z_recv.at[o - 1], device
            )
        )
    for copy in copies:
        copy.start()
    for copy in copies:
        copy.wait()
    mine_z = mine_xy + z * chunk
    value = acc[span(mine_z, chunk), :]
    for o in range(1, nz):
        value = value + recv_z[o - 1]
    res[span(mine_z, chunk), :] = value

    def gather(src, peers, send, recv):
        copies = []
        for i, device in enumerate(peers):
            copies.append(remote(res.at[src], res.at[src], send.at[i], recv.at[i], device))
        for copy in copies:
            copy.start()
        for copy in copies:
            copy.wait()

    gather(span(mine_z, chunk), [z_peer(o)[1] for o in range(1, nz)], z_send.at[pl.ds(nz - 1, nz - 1)], z_recv.at[pl.ds(nz - 1, nz - 1)])
    gather(
        span(mine_xy, part),
        [xy_peer(o)[1] for o in range(1, nxy)],
        xy_send.at[pl.ds(nxy - 1, nxy - 1)],
        xy_recv.at[pl.ds(nxy - 1, nxy - 1)],
    )
    gather(span(mine, half), [other], c_send.at[pl.ds(1, 1)], c_recv.at[pl.ds(1, 1)])
    for s in range(samples):
        pltpu.make_async_copy(pair.at[s], g_pair_hbm.at[s], gp_sem.at[s]).wait()


def unpack_kernel(pieces, *refs):
    n, v = len(pieces), len(VECTORS)
    packed, big_in, refs = refs[0], refs[1:5], refs[5:]
    big_out, mats, rows, wp = refs[:4], refs[4 : 4 + n], refs[4 + n : 4 + n + v], refs[4 + n + v]
    stage, in_sems, out_sems, sems = refs[5 + n + v :][:4], *refs[-3:]
    moves = []
    for a, mid, b in zip(big_in, stage, big_out):
        for c in range(a.shape[0]):
            i = len(moves)
            moves.append(
                (
                    pltpu.make_async_copy(a.at[c], mid.at[c], in_sems.at[i]),
                    pltpu.make_async_copy(mid.at[c], b.at[c], out_sems.at[i]),
                )
            )
    for load, _ in moves:
        load.start()
    copies = []
    for name, ref in zip(pieces, mats):
        base = PLACE[name]
        height, width = ref.shape
        for b in range(width // LANES):
            copies.append(
                pltpu.make_async_copy(
                    packed.at[pl.ds(base + b * height, height)],
                    ref.at[:, pl.ds(b * LANES, LANES)],
                    sems.at[len(copies)],
                )
            )
    for copy in copies:
        copy.start()
    base = PLACE["vectors"]
    for i, ref in enumerate(rows):
        ref[...] = packed[base + i : base + i + 1, 0 : ref.shape[1]]
    base = PLACE["w_pair"]
    wp[...] = packed[base : base + wp.shape[0], 0 : wp.shape[1]]
    for load, store in moves:
        load.wait()
        store.start()
    for copy in copies:
        copy.wait()
    for _, store in moves:
        store.wait()


def shards(dpn, seqn, atoms, single_cond, pair_block, atom_count, *rest):
    params, cotangent = dict(zip(PARAMS, rest[:-1])), rest[-1]
    params["w_pair"] = params["w_pair"].T
    samples, rows, width = atoms.shape
    nwin, channels = pair_block.shape[1:3]
    heads = params["w_pair"].shape[0]
    flat = samples * rows
    grain = 8 * dpn * seqn
    packed = -(-USED // grain) * grain
    nz, nx = 4, seqn // 8
    nxy = dpn * nx
    half = packed // 2
    part = half // nxy
    chunk = part // nz
    windows = samples * nwin

    def row(v):
        return v.reshape(1, -1) if v.ndim == 1 else v

    vmem = pl.BlockSpec(memory_space=pltpu.VMEM)
    smem = pl.BlockSpec(memory_space=pltpu.SMEM)
    anyw = pl.BlockSpec(memory_space=pl.ANY)

    def buf(*shape):
        return pltpu.VMEM(shape, F32)

    tall = (flat, width)
    scratch = [
        buf(*pair_block.shape),
        buf(windows, heads * WQ, KW),
        buf(windows, WQ, KW),
        buf(windows, 2, WQ, KW),
        buf(windows, heads * WQ, KW),
        buf(windows, heads * WQ, KW),
        buf(samples, rows + 2 * HALO, 2 * width),
        buf(samples, rows + 2 * HALO, 2 * width),
        buf(2, samples, HALO, 2 * width),
    ]
    scratch += [buf(*tall) for _ in range(13)]
    scratch += [buf(flat, 1), buf(flat, 1)]
    scratch += [buf(*tall) for _ in range(7)]
    scratch += [
        buf(heads * channels, 8, KW),
        buf(packed, LANES),
        buf(half, LANES),
        buf(nxy - 1, part, LANES),
        buf(nz - 1, chunk, LANES),
        pltpu.SemaphoreType.DMA((samples,)),
        pltpu.SemaphoreType.DMA((samples,)),
        pltpu.SemaphoreType.DMA((4,)),
        pltpu.SemaphoreType.DMA((4,)),
        pltpu.SemaphoreType.DMA((2,)),
        pltpu.SemaphoreType.DMA((2,)),
        pltpu.SemaphoreType.DMA((2 * (nxy - 1),)),
        pltpu.SemaphoreType.DMA((2 * (nxy - 1),)),
        pltpu.SemaphoreType.DMA((2 * (nz - 1),)),
        pltpu.SemaphoreType.DMA((2 * (nz - 1),)),
    ]
    sizes = (samples, rows, dpn, seqn, packed)
    out, g_atoms, g_single, g_pair, res = pl.pallas_call(
        functools.partial(block_kernel, sizes),
        out_shape=[
            jax.ShapeDtypeStruct(tall, F32),
            jax.ShapeDtypeStruct(tall, F32),
            jax.ShapeDtypeStruct(tall, F32),
            jax.ShapeDtypeStruct(pair_block.shape, F32),
            jax.ShapeDtypeStruct((packed, LANES), F32),
        ],
        in_specs=[smem] * 3 + [vmem] * (3 + len(PARAMS)) + [anyw],
        out_specs=[vmem, vmem, vmem, anyw, vmem],
        scratch_shapes=scratch,
        compiler_params=pltpu.CompilerParams(
            collective_id=0, has_side_effects=True, vmem_limit_bytes=56 * 2**20
        ),
        name="block",
    )(
        atom_count,
        params["pair_gain"],
        params["w_pair"],
        atoms.reshape(tall),
        single_cond.reshape(tall),
        cotangent.reshape(tall),
        *[row(params[name]) for name in PARAMS],
        pair_block,
    )

    pieces = tuple(name for name, _, _ in MATRICES)
    mats = [jax.ShapeDtypeStruct(params[name].shape, F32) for name in pieces]
    vecs = [jax.ShapeDtypeStruct((1, params[name].shape[0]), F32) for name in VECTORS]
    big = [out.reshape(atoms.shape), g_atoms.reshape(atoms.shape), g_single.reshape(atoms.shape)]
    big.append(g_pair.reshape((windows,) + pair_block.shape[2:]))
    moves = sum(v.shape[0] for v in big)
    copies = sum(columns for _, _, columns in MATRICES)
    hbm = pl.BlockSpec(memory_space=pltpu.HBM)
    results = pl.pallas_call(
        functools.partial(unpack_kernel, pieces),
        out_shape=[jax.ShapeDtypeStruct(v.shape, F32) for v in big]
        + mats
        + vecs
        + [jax.ShapeDtypeStruct((heads, channels), F32)],
        in_specs=[vmem] + [hbm] * 4,
        out_specs=[hbm] * (4 + len(mats)) + [vmem] * (len(vecs) + 1),
        scratch_shapes=[buf(*v.shape) for v in big]
        + [
            pltpu.SemaphoreType.DMA((moves,)),
            pltpu.SemaphoreType.DMA((moves,)),
            pltpu.SemaphoreType.DMA((copies,)),
        ],
        compiler_params=pltpu.CompilerParams(vmem_limit_bytes=32 * 2**20),
        name="unpack",
    )(res, *big)
    grads = dict(zip(pieces, results[4:]))
    for name, value in zip(VECTORS, results[4 + len(mats) :]):
        grads[name] = value.reshape(-1)
    grads["w_pair"] = results[-1].T
    out, g_atoms, g_single, g_pair = results[:4]
    return (out, g_atoms, g_single, g_pair.reshape(pair_block.shape)) + tuple(grads[name] for name in PARAMS)


def solution(mesh):
    data = P("dp", "seq", None)
    pairs = P("dp", "seq", None, None, None)
    return jax.shard_map(
        functools.partial(shards, mesh.shape["dp"], mesh.shape["seq"]),
        mesh=mesh,
        in_specs=(data, data, pairs, P("dp")) + (P(),) * len(PARAMS) + (data,),
        out_specs=(data, data, data, pairs) + (P(),) * len(PARAMS),
        check_vma=False,
    )
```

time: 604 us -> 82.2 us (0.14); the launches traced: 597 us -> 81.8 us
  local copies, waits for them, and re-layouts: 175 us -> 6.3 us
  waiting for transfers between devices: 142 us -> 0 us
  matrix products: 133 us -> 0 us
  Pallas kernels: 0 us -> 74.8 us
  other arithmetic: 62.7 us -> 0 us
  blocking collectives: 44 us -> 0 us
  starting transfers between devices: 21.4 us -> 0 us
  between operations: 18.3 us -> 0.7 us
    psum x1 -> x0, waiting for transfers between devices: 141 us -> none  [shards(): total = lax.psum(tuple(total), ('dp', 'seq'))]
    dot_general x100 -> x0, matrix products: 133 us -> none  [the longest x78 78 us: matmul(): jnp.dot(x, w, precision=lax.Precision.HIGHEST, preferred_element_type=jnp...]
    pallas_call x0 -> x2, Pallas kernels: none -> 74.8 us  [the longest x1 69.9 us: shards(): pl.pallas_call(functools.partial(block_kernel, sizes), out_shape=[jax.Sha...]
    concatenate x33 -> x0, local copies, waits for them, and re-layouts: 64.1 us -> none  [the longest x32 63.3 us: window_blocks(): return jnp.concatenate([blocks[i:i + nwin] for i in range(reps)], axis=1)]
    unnamed x558 -> x10, local copies, waits for them, and re-layouts: 65.7 us -> 6.3 us
    psum x1 -> x0, blocking collectives: 44 us -> none  [shards(): total = lax.psum(tuple(total), ('dp', 'seq'))]
    reduce_sum x26 -> x0, other arithmetic: 24.1 us -> none  [the longest x3 8.25 us: attend_core(): var = jnp.mean(cent * cent, axis=1, keepdims=True)]
    ppermute x8 -> x0, starting transfers between devices: 21.4 us -> none  [the longest x4 16 us: with_halo(): before = lax.ppermute(last, axis, up)]
  transfers between devices with their start and end apart: 9 -> 0, of which waited for: 2 -> 0; matrix products, arithmetic and copies ran while one was open for 22% -> 0% of each run, Pallas kernels for 0% -> 0%
where the time goes in v1:
time: 82.2 us; the launch traced here: 81.8 us
  Pallas kernels  74.8 us (91%)
  local copies, waits for them, and re-layouts  6.3 us (8%)
    pallas_call x1, Pallas kernels, shards(): pl.pallas_call(functools.partial(block_kernel, sizes), out_shape=[jax.Sha...  69.9 us
    unnamed x10, local copies, waits for them, and re-layouts  6.3 us
    pallas_call x1, Pallas kernels, shards(): pl.pallas_call(functools.partial(unpack_kernel, pieces), out_shape=[jax.S...  4.99 us

profile of v1, /device:TPU:0, one launch (start us, length us, event | category | flops | bytes accessed | tf_op | source)
XLA Modules:
  0.0 81.8 jit_solution(17584978805438019812)
XLA Ops:
  0.7 69.9 %block.1 = (f32[512,128]{1,0:T(8,128)}, f32[512,128]{1,0:T(8,128)}, f32[512,128]{1,0:T(8,128)}, f32[2,8,16,32,128]{4,3,2,1,0:T(8,128)}, f32[2304,128]{1,0:T(8,128)}) custom-call(s32[2]{0:T(128)} %refs_0_.1, f32[16]{0:T(128)} %refs_1_.1, f32[4,16]{1,0:T(4,128)} %bitcast.33, f32[512,128]{1,0:T(8,128)} %bitcast.30, f32[512,128]{1,0:T(8,128)} %bitcast.31, ...), custom_call_target="tpu_custom_call" | custom-call | tf_op jit(solution)/shard_map/block/pallas_call | solution.py:706
  70.5 0.0 copy-start
  70.6 2.2 %copy-done = f32[2,8,16,32,128]{4,3,2,1,0:T(8,128)S(1)} copy-done((f32[2,8,16,32,128]{4,3,2,1,0:T(8,128)S(1)}, f32[2,8,16,32,128]{4,3,2,1,0:T(8,128)}, u32[]{:S(2)}) %copy-start) | copy-done | bytes 4194328
  72.7 0.0 copy-start.1
  72.7 1.3 %copy-done.1 = f32[2304,128]{1,0:T(8,128)S(1)} copy-done((f32[2304,128]{1,0:T(8,128)S(1)}, f32[2304,128]{1,0:T(8,128)}, u32[]{:S(2)}) %copy-start.1) | copy-done | bytes 1179672
  74.0 0.0 copy-start.2
  74.0 0.9 %copy-done.2 = f32[512,128]{1,0:T(8,128)S(1)} copy-done((f32[512,128]{1,0:T(8,128)S(1)}, f32[512,128]{1,0:T(8,128)}, u32[]{:S(2)}) %copy-start.2) | copy-done | bytes 262168
  75.0 0.0 copy-start.3
  75.0 0.9 %copy-done.3 = f32[512,128]{1,0:T(8,128)S(1)} copy-done((f32[512,128]{1,0:T(8,128)S(1)}, f32[512,128]{1,0:T(8,128)}, u32[]{:S(2)}) %copy-start.3) | copy-done | bytes 262168
  75.9 0.0 copy-start.4
  75.9 0.9 %copy-done.4 = f32[512,128]{1,0:T(8,128)S(1)} copy-done((f32[512,128]{1,0:T(8,128)S(1)}, f32[512,128]{1,0:T(8,128)}, u32[]{:S(2)}) %copy-start.4) | copy-done | bytes 262168
  76.9 5.0 %unpack.1 = (f32[2,256,128]{2,1,0:T(8,128)}, f32[2,256,128]{2,1,0:T(8,128)}, f32[2,256,128]{2,1,0:T(8,128)}, f32[16,16,32,128]{3,2,1,0:T(8,128)}, f32[256,128]{1...) custom-call(f32[2304,128]{1,0:T(8,128)S(1)} %copy-done.1, ...), custom_call_target="tpu_custom_call" | custom-call | tf_op jit(solution)/shard_map/unpack/pallas_call | solution.py:741
Async XLA Ops:
  70.5 2.2 %copy-start = (f32[2,8,16,32,128]{4,3,2,1,0:T(8,128)S(1)}, f32[2,8,16,32,128]{4,3,2,1,0:T(8,128)}, u32[]{:S(2)}) copy-start(f32[2,8,16,32,128]{4,3,2,1,0:T(8,128)} %get-tuple-element.63) | copy-start | bytes 12582916
  72.7 1.3 %copy-start.1 = (f32[2304,128]{1,0:T(8,128)S(1)}, f32[2304,128]{1,0:T(8,128)}, u32[]{:S(2)}) copy-start(f32[2304,128]{1,0:T(8,128)} %get-tuple-element.59.refs_0_) | copy-start | bytes 3538948
  74.0 0.9 %copy-start.2 = (f32[512,128]{1,0:T(8,128)S(1)}, f32[512,128]{1,0:T(8,128)}, u32[]{:S(2)}) copy-start(f32[512,128]{1,0:T(8,128)} %get-tuple-element.60) | copy-start | bytes 786436
  75.0 0.9 %copy-start.3 = (f32[512,128]{1,0:T(8,128)S(1)}, f32[512,128]{1,0:T(8,128)}, u32[]{:S(2)}) copy-start(f32[512,128]{1,0:T(8,128)} %get-tuple-element.61) | copy-start | bytes 786436
  75.9 0.9 %copy-start.4 = (f32[512,128]{1,0:T(8,128)S(1)}, f32[512,128]{1,0:T(8,128)}, u32[]{:S(2)}) copy-start(f32[512,128]{1,0:T(8,128)} %get-tuple-element.62) | copy-start | bytes 786436

commit v2 on v1

v2 whole, which is shorter than its diff:
```python
import functools
import math

import jax
import jax.numpy as jnp
from jax import lax
from jax.experimental import pallas as pl
from jax.experimental.pallas import tpu as pltpu
from jax.sharding import PartitionSpec as P

WQ = 32
KW = 128
HALO = 48
LANES = 128
MESH = pl.DeviceIdType.MESH
F32 = jnp.float32

EARLY = (
    ("w_down", 2, 1),
    ("w_hidden_gate", 1, 2),
    ("w_hidden_up", 1, 2),
    ("w_zero2", 1, 1),
    ("w_scale2", 1, 1),
    ("w_shift2", 1, 1),
    ("w_out", 1, 1),
    ("w_zero1", 1, 1),
    ("w_gate", 1, 1),
)
LATE = (
    ("w_query", 1, 1),
    ("w_key", 1, 1),
    ("w_value", 1, 1),
    ("w_scale1", 1, 1),
    ("w_shift1", 1, 1),
)
VECTORS = ("b_scale1", "b_query", "b_scale2", "b_zero1", "b_zero2", "s_gain1", "s_gain2", "pair_gain")
PARAMS = (
    "s_gain1",
    "w_scale1",
    "b_scale1",
    "w_shift1",
    "w_query",
    "b_query",
    "w_key",
    "w_value",
    "w_gate",
    "pair_gain",
    "w_pair",
    "w_out",
    "w_zero1",
    "b_zero1",
    "s_gain2",
    "w_scale2",
    "b_scale2",
    "w_shift2",
    "w_hidden_gate",
    "w_hidden_up",
    "w_down",
    "w_zero2",
    "b_zero2",
)


def offsets():
    place, used = {}, []
    for group in (EARLY, LATE):
        row = 0
        for name, rows, columns in group:
            place[name] = row
            row += rows * columns * LANES
        used.append(row)
    place["vectors"] = used[1]
    place["w_pair"] = used[1] + 8
    return place, used[0], used[1] + 16


PLACE, EARLY_ROWS, LATE_ROWS = offsets()
BF16 = jnp.bfloat16
NN = (((1,), (0,)), ((), ()))
NT = (((1,), (1,)), ((), ()))
TN = (((0,), (0,)), ((), ()))


def dot(a, b, dims):
    return lax.dot_general(a, b, dims, preferred_element_type=F32)


def cat(parts, axis):
    return jnp.concatenate(parts, axis=axis)


def split(x):
    high = x.astype(BF16)
    return high, (x - high.astype(F32)).astype(BF16)


def product(a, b, dims):
    (ah, al), (bh, bl) = a, b
    (ka,), (kb,) = dims[0]
    return dot(cat([ah, al, ah], ka), cat([bh, bh, bl], kb), dims)


def nn(a, b):
    return product(a, b, NN)


def nt(a, b):
    return product(a, b, NT)


def tn(a, b):
    return product(a, b, TN)


def mean_lanes(x):
    weight = jnp.full((2 * LANES, LANES), 1.0 / LANES, BF16)
    return dot(cat(split(x), 1), weight, NN)


def norm(x):
    cent = x - mean_lanes(x)
    inv = lax.rsqrt(mean_lanes(cent * cent) + 1e-05)
    return cent * inv, inv


def norm_back(d, xhat, inv):
    return (d - mean_lanes(d) - xhat * mean_lanes(d * xhat)) * inv


def sigmoid(x):
    return 1.0 / (1.0 + jnp.exp(-x))


def column_sum(x):
    return jnp.sum(x, axis=0, keepdims=True)


def block_kernel(sizes, *refs):
    samples, rows, dpn, seqn, early, late = sizes
    nwin = rows // WQ
    flat = samples * rows
    nz = 4
    nx = seqn // (2 * nz)
    nxy = dpn * nx
    (
        count,
        gain_s,
        wpair_s,
        atoms,
        single,
        cot,
        p_s_gain1,
        p_w_scale1,
        p_b_scale1,
        p_w_shift1,
        p_w_query,
        p_b_query,
        p_w_key,
        p_w_value,
        p_w_gate,
        p_pair_gain,
        p_w_pair,
        p_w_out,
        p_w_zero1,
        p_b_zero1,
        p_s_gain2,
        p_w_scale2,
        p_b_scale2,
        p_w_shift2,
        p_w_hidden_gate,
        p_w_hidden_up,
        p_w_down,
        p_w_zero2,
        p_b_zero2,
        pair_hbm,
        out_hbm,
        g_atoms_hbm,
        g_single_hbm,
        g_pair_hbm,
        early_hbm,
        late_hbm,
        pair,
        bias,
        pmean,
        prs,
        prob,
        ds,
        kv,
        dkv,
        dhalo,
        kvh,
        kvl,
        w1h,
        w1l,
        wqh,
        wql,
        wzh,
        wzl,
        w2h,
        w2l,
        whh,
        whl,
        wdh,
        wdl,
        woh,
        wol,
        qh_s,
        ql_s,
        mh_s,
        ml_s,
        th_s,
        tl_s,
        mixed_s,
        ns_s,
        na_s,
        n1_s,
        sc1_s,
        sc2_s,
        sh2_s,
        gate_s,
        z1_s,
        z2_s,
        rs_s,
        ra_s,
        dq_s,
        dfirst_s,
        dz1_s,
        dz2_s,
        dn2_s,
        dsc2_s,
        gpre_s,
        out,
        g_atoms,
        g_single,
        gacc,
        acc_e,
        res_e,
        acc_l,
        res_l,
        recv_ec,
        recv_exy,
        recv_ez,
        recv_lc,
        recv_lxy,
        recv_lz,
        pair_sem,
        out_sem,
        h_send,
        h_recv,
        ec_send,
        ec_recv,
        exy_send,
        exy_recv,
        ez_send,
        ez_recv,
        lc_send,
        lc_recv,
        lxy_send,
        lxy_recv,
        lz_send,
        lz_recv,
    ) = refs
    dp = lax.axis_index("dp")
    me = lax.axis_index("seq")
    core = lax.rem(me, 2)
    x = lax.rem(me // 2, nx)
    z = me // (2 * nx)
    k = dp * nx + x
    left = (dp, lax.rem(me + seqn - 1, seqn))
    right = (dp, lax.rem(me + 1, seqn))
    other = (dp, me + 1 - 2 * core)

    def xy_peer(o):
        kk = lax.rem(k + o, nxy)
        return kk, (kk // nx, (z * nx + lax.rem(kk, nx)) * 2 + core)

    def z_peer(o):
        zz = lax.rem(z + o, nz)
        return zz, (dp, (zz * nx + x) * 2 + core)

    for s in range(samples):
        pltpu.make_async_copy(pair_hbm.at[s], pair.at[s], pair_sem.at[s]).start()

    barrier = pltpu.get_barrier_semaphore()
    greeted = [left, right, other]
    greeted += [xy_peer(o)[1] for o in range(1, nxy)]
    greeted += [z_peer(o)[1] for o in range(1, nz)]
    for device in greeted:
        pl.semaphore_signal(barrier, inc=1, device_id=device, device_id_type=MESH)

    def remote(src, dst, send, recv, device):
        return pltpu.make_async_remote_copy(
            src_ref=src, dst_ref=dst, send_sem=send, recv_sem=recv, device_id=device, device_id_type=MESH
        )

    def start(copies):
        for copy in copies:
            copy.start()
        return copies

    def wait(copies):
        for copy in copies:
            copy.wait()

    def span(first, size):
        return pl.ds(pl.multiple_of(first, 8), size)

    def hold(high, low, *weights):
        for c, w in enumerate(weights):
            width = w.shape[1]
            high[:, c * width : (c + 1) * width], low[:, c * width : (c + 1) * width] = split(w[...])

    hold(w1h, w1l, p_w_scale1, p_w_shift1)
    hold(wqh, wql, p_w_query, p_w_key, p_w_value, p_w_gate)
    ns, rs = norm(single[...])
    na, ra = norm(atoms[...])
    ns_s[...] = ns
    na_s[...] = na
    rs_s[...] = rs
    ra_s[...] = ra
    first1 = nn(split(ns * p_s_gain1[...]), (w1h[...], w1l[...]))
    sc1 = sigmoid(first1[:, :LANES] + p_b_scale1[...])
    sc1_s[...] = sc1
    n1 = sc1 * na + first1[:, LANES:]
    n1_s[...] = n1
    n1_split = split(n1)
    keys_values = nn(n1_split, (wqh[:, LANES : 3 * LANES], wql[:, LANES : 3 * LANES]))
    for s in range(samples):
        kv[s, HALO : HALO + rows] = keys_values[s * rows : (s + 1) * rows]

    pl.semaphore_wait(barrier, len(greeted))
    halos = start(
        [
            remote(kv.at[:, rows : rows + HALO], kv.at[:, 0:HALO], h_send.at[0], h_recv.at[0], right),
            remote(
                kv.at[:, HALO : 2 * HALO], kv.at[:, HALO + rows : 2 * HALO + rows], h_send.at[1], h_recv.at[1], left
            ),
        ]
    )

    hold(wzh, wzl, p_w_zero1, p_w_zero2)
    hold(w2h, w2l, p_w_scale2, p_w_shift2)
    hold(whh, whl, p_w_hidden_gate, p_w_hidden_up)
    hold(wdh, wdl, p_w_down)
    hold(woh, wol, p_w_out)
    scale = 1.0 / math.sqrt(32)
    query = (nn(n1_split, (wqh[:, :LANES], wql[:, :LANES])) + p_b_query[...]) * scale
    qh_s[...], ql_s[...] = split(query)
    gate_s[...] = sigmoid(nn(n1_split, (wqh[:, 3 * LANES :], wql[:, 3 * LANES :])))
    first2 = nn(split(ns * p_s_gain2[...]), (w2h[...], w2l[...]))
    sc2_s[...] = sigmoid(first2[:, :LANES] + p_b_scale2[...])
    sh2_s[...] = first2[:, LANES:]
    zeros = nn(split(single[...]), (wzh[...], wzl[...]))
    z1_s[...] = sigmoid(zeros[:, :LANES] + p_b_zero1[...])
    z2_s[...] = sigmoid(zeros[:, LANES:] + p_b_zero2[...])

    channels = gain_s.shape[0]
    heads = wpair_s.shape[0]
    wg = [[gain_s[p] * wpair_s[h, p] for h in range(heads)] for p in range(channels)]
    wsum = [functools.reduce(lambda a, b: a + b, [wg[p][h] for p in range(channels)]) for h in range(heads)]

    for s in range(samples):
        pltpu.make_async_copy(pair_hbm.at[s], pair.at[s], pair_sem.at[s]).wait()

    key_lane = lax.broadcasted_iota(jnp.int32, (WQ, KW), 1)
    same = key_lane == lax.broadcasted_iota(jnp.int32, (WQ, KW), 0) + HALO

    def pair_bias(t, carry):
        s, w = t // nwin, lax.rem(t, nwin)
        first = pair[s, w, 0]
        total, square = first, first * first
        b = [first * wg[0][h] for h in range(heads)]
        for p in range(1, channels):
            v = pair[s, w, p]
            total = total + v
            square = square + v * v
            b = [b[h] + v * wg[p][h] for h in range(heads)]
        mean = total * (1.0 / channels)
        var = square * (1.0 / channels) - mean * mean
        inv = lax.rsqrt(jnp.maximum(var, 0.25))
        pmean[t] = mean
        live = jnp.where(var > 0.25, 1.0, jnp.where(var == 0.25, 0.5, 0.0))
        prs[t, 0] = inv
        prs[t, 1] = inv * inv * live * (1.0 / channels)
        begin = me * rows + w * WQ - HALO
        valid = ((key_lane >= -begin) & (key_lane < count[s] - begin)) | same
        for h in range(heads):
            bias[t, h * WQ : (h + 1) * WQ] = jnp.where(valid, inv * (b[h] - mean * wsum[h]), -1e9)
        return carry

    lax.fori_loop(0, samples * nwin, pair_bias, 0)

    wait(halos)
    for s in range(samples):
        kv[s, 0:HALO] = jnp.where(me == 0, 0.0, kv[s, 0:HALO])
        kv[s, HALO + rows :] = jnp.where(me == seqn - 1, 0.0, kv[s, HALO + rows :])
    kvh[...], kvl[...] = split(kv[...])

    lane = lax.broadcasted_iota(jnp.int32, (heads * WQ, LANES), 1)
    row = lax.broadcasted_iota(jnp.int32, (heads * WQ, LANES), 0)
    own = (lane // 32 == row // WQ).astype(F32)
    own_low = own.astype(BF16)
    ones = jnp.ones((KW, LANES), BF16)
    nothing = jnp.zeros((KW, LANES), BF16)

    def heads_in(ref, at):
        return cat([ref[pl.ds(at, WQ), :]] * heads, 0) * own_low

    def heads_out(v):
        v = v * own
        return (v[0:WQ] + v[WQ : 2 * WQ]) + (v[2 * WQ : 3 * WQ] + v[3 * WQ : 4 * WQ])

    def attend(s, carry):
        for w in range(nwin):
            t = s * nwin + w
            at = pl.multiple_of(s * rows + w * WQ, WQ)
            keys = slice(w * WQ, w * WQ + KW)
            queries = heads_in(qh_s, at), heads_in(ql_s, at)
            scores = nt(queries, (kvh[s, keys, :LANES], kvl[s, keys, :LANES])) + bias[t]
            expo = jnp.exp(scores - jnp.max(scores, axis=-1, keepdims=True))
            eh, el = split(expo)
            vh, vl = kvh[s, keys, LANES:], kvl[s, keys, LANES:]
            high = cat([vh, ones], 1)
            both = dot(cat([eh, el, eh], 1), cat([high, high, cat([vl, nothing], 1)], 0), NN)
            inv = 1.0 / both[:, LANES:]
            prob[t] = expo * inv
            mixed_s[pl.ds(at, WQ), :] = heads_out(both[:, :LANES] * inv)
        return carry

    lax.fori_loop(0, samples, attend, 0)

    gated = gate_s[...] * mixed_s[...]
    gated_split = split(gated)
    projected = nn(gated_split, (woh[...], wol[...]))
    first = atoms[...] + z1_s[...] * projected
    nf, rf = norm(first)
    n2 = sc2_s[...] * nf + sh2_s[...]
    n2_split = split(n2)
    up = nn(n2_split, (whh[...], whl[...]))
    hidden_width = up.shape[1] // 2
    hg, hu = up[:, :hidden_width], up[:, hidden_width:]
    sg = sigmoid(hg)
    silu = hg * sg
    hidden = silu * hu
    hidden_split = split(hidden)
    down = nn(hidden_split, (wdh[...], wdl[...]))
    z2 = z2_s[...]
    g = cot[...]
    out[...] = first + z2 * down
    outputs = start([pltpu.make_async_copy(out, out_hbm, out_sem.at[0])])

    def put(acc, names, value):
        at = 0
        for name in names:
            base = PLACE[name]
            for b in range(dict((n, c) for n, _, c in EARLY + LATE)[name]):
                acc[base + b * value.shape[0] : base + (b + 1) * value.shape[0]] = value[:, at : at + LANES]
                at += LANES

    d_down = g * z2
    dz2 = g * down * z2 * (1.0 - z2)
    dz2_s[...] = dz2
    d_down_split = split(d_down)
    put(acc_e, ["w_down"], tn(hidden_split, d_down_split))
    d_hidden = nt(d_down_split, (wdh[...], wdl[...]))
    d_up = cat([d_hidden * hu * (sg * (1.0 + hg * (1.0 - sg))), d_hidden * silu], 1)
    d_up_split = split(d_up)
    put(acc_e, ["w_hidden_gate", "w_hidden_up"], tn(n2_split, d_up_split))
    d_n2 = nt(d_up_split, (whh[...], whl[...]))
    dn2_s[...] = d_n2
    sc2 = sc2_s[...]
    dsc2 = d_n2 * nf * sc2 * (1.0 - sc2)
    dsc2_s[...] = dsc2
    cond2_split = split(ns_s[...] * p_s_gain2[...])
    put(acc_e, ["w_scale2", "w_shift2"], tn(cond2_split, split(cat([dsc2, d_n2], 1))))
    d_first = g + norm_back(d_n2 * sc2, nf, rf)
    dfirst_s[...] = d_first
    z1 = z1_s[...]
    d_proj = d_first * z1
    d_proj_split = split(d_proj)
    dz1 = d_first * projected * z1 * (1.0 - z1)
    dz1_s[...] = dz1
    put(acc_e, ["w_out"], tn(gated_split, d_proj_split))
    put(acc_e, ["w_zero1", "w_zero2"], tn(split(single[...]), split(cat([dz1, dz2], 1))))
    d_gated = nt(d_proj_split, (woh[...], wol[...]))
    gate = gate_s[...]
    mixed = mixed_s[...]
    d_gate = d_gated * mixed * gate * (1.0 - gate)
    gpre_s[...] = d_gate
    put(acc_e, ["w_gate"], tn(split(n1_s[...]), split(d_gate)))
    d_mixed = d_gated * gate
    mh_s[...], ml_s[...] = split(d_mixed)
    th_s[...], tl_s[...] = split(d_mixed * mixed)
    if early > EARLY_ROWS:
        acc_e[EARLY_ROWS:] = jnp.zeros((early - EARLY_ROWS, LANES), F32)

    def scatter_core(acc, size, recv, sems):
        half = size // 2
        return [remote(acc.at[span((1 - core) * half, half)], recv, sems[0].at[0], sems[1].at[0], other)]

    def add_core(acc, size, recv):
        mine = span(core * (size // 2), size // 2)
        acc[mine, :] += recv[...]

    def scatter_xy(acc, size, recv, sems):
        half = size // 2
        part = half // nxy
        copies = []
        for o in range(1, nxy):
            kk, device = xy_peer(o)
            source = acc.at[span(core * half + kk * part, part)]
            copies.append(remote(source, recv.at[o - 1], sems[0].at[o - 1], sems[1].at[o - 1], device))
        return copies

    def add_xy(acc, size, recv):
        half = size // 2
        part = half // nxy
        mine = span(core * half + k * part, part)
        value = acc[mine, :]
        for o in range(1, nxy):
            value = value + recv[o - 1]
        acc[mine, :] = value

    def gather_xy(res, size, sems):
        half = size // 2
        part = half // nxy
        mine = span(core * half + k * part, part)
        copies = []
        for o in range(1, nxy):
            at = nxy - 2 + o
            copies.append(remote(res.at[mine], res.at[mine], sems[0].at[at], sems[1].at[at], xy_peer(o)[1]))
        return copies

    def gather_core(res, size, hbm, sems):
        mine = span(core * (size // 2), size // 2)
        return [remote(res.at[mine], hbm.at[mine], sems[0].at[1], sems[1].at[1], other)]

    def keep(res, size, hbm, sem):
        mine = span(core * (size // 2), size // 2)
        return [pltpu.make_async_copy(res.at[mine], hbm.at[mine], sem)]

    ec, exy, ez = (ec_send, ec_recv), (exy_send, exy_recv), (ez_send, ez_recv)
    lc, lxy, lz = (lc_send, lc_recv), (lxy_send, lxy_recv), (lz_send, lz_recv)
    part_e = early // (2 * nxy)
    chunk_e = part_e // nz
    at_e = core * (early // 2) + k * part_e
    part_l = late // (2 * nxy)
    at_l = core * (late // 2) + k * part_l

    e1 = start(scatter_core(acc_e, early, recv_ec, ec))

    dkv[...] = jnp.zeros_like(dkv)
    less = -jnp.ones((KW, LANES), BF16)

    def attend_back(s):
        for w in range(nwin):
            t = s * nwin + w
            at = s * rows + w * WQ
            keys = slice(w * WQ, w * WQ + KW)
            queries = heads_in(qh_s, at), heads_in(ql_s, at)
            mh, ml = heads_in(mh_s, at), heads_in(ml_s, at)
            th, tl = heads_in(th_s, at), heads_in(tl_s, at)
            vh, vl = kvh[s, keys, LANES:], kvl[s, keys, LANES:]
            weights = prob[t]
            d_scores = weights * dot(cat([mh, ml, mh, th, tl], 1), cat([vh, vh, vl, less, less], 1), NT)
            ds[t] = d_scores
            d_split = split(d_scores)
            dq_s[pl.ds(at, WQ), :] = heads_out(nn(d_split, (kvh[s, keys, :LANES], kvl[s, keys, :LANES]))) * scale
            dkv[s, keys, :LANES] += tn(d_split, queries)
            dkv[s, keys, LANES:] += tn(split(weights), (mh, ml))

    for s in range(samples):
        attend_back(s)
        if s == 0:
            wait(e1)
            add_core(acc_e, early, recv_ec)
            e2 = start(scatter_xy(acc_e, early, recv_exy, exy))

    halos = start(
        [
            remote(dkv.at[:, 0:HALO], dhalo.at[1], h_send.at[2], h_recv.at[2], left),
            remote(dkv.at[:, HALO + rows : 2 * HALO + rows], dhalo.at[0], h_send.at[3], h_recv.at[3], right),
        ]
    )

    gacc[...] = jnp.zeros_like(gacc)

    def pair_back(t, carry):
        s, w = t // nwin, lax.rem(t, nwin)
        inv, live = prs[t, 0], prs[t, 1]
        mean = pmean[t]
        u, along, level = [], None, None
        for h in range(heads):
            d = ds[t, h * WQ : (h + 1) * WQ]
            u.append(d * inv)
            a = d * bias[t, h * WQ : (h + 1) * WQ]
            b = u[h] * (wsum[h] * (1.0 / channels))
            along = a if along is None else along + a
            level = b if level is None else level + b
        c1 = along * live
        c0 = mean * c1 - level
        mu = [mean * u[h] for h in range(heads)]
        for p in range(channels):
            v = pair[s, w, p]
            d = c0 - v * c1
            for h in range(heads):
                d = d + u[h] * wg[p][h]
                term = v * u[h] - mu[h]
                gacc[h * channels + p] += (term[0:8] + term[8:16]) + (term[16:24] + term[24:32])
            pair[s, w, p] = d
        return carry

    lax.fori_loop(0, samples * nwin, pair_back, 0)
    outputs += start([pltpu.make_async_copy(pair, g_pair_hbm, out_sem.at[1])])

    wait(halos)
    for s in range(samples):
        dkv[s, HALO : 2 * HALO] += dhalo[0, s]
        dkv[s, rows : rows + HALO] += dhalo[1, s]

    dq = dq_s[...]
    d_keys_values = cat([dkv[s, HALO : HALO + rows] for s in range(samples)], 0)
    d_all = split(cat([dq, d_keys_values, gpre_s[...]], 1))
    d_n1 = nt(d_all, (wqh[...], wql[...]))
    na = na_s[...]
    sc1 = sc1_s[...]
    dsc1 = d_n1 * na * sc1 * (1.0 - sc1)
    d_first1 = split(cat([dsc1, d_n1], 1))
    ns = ns_s[...]
    put(
        acc_l,
        ["w_query", "w_key", "w_value"],
        tn(split(n1_s[...]), (d_all[0][:, : 3 * LANES], d_all[1][:, : 3 * LANES])),
    )
    put(acc_l, ["w_scale1", "w_shift1"], tn(split(ns * p_s_gain1[...]), d_first1))
    d_cond1 = nt(d_first1, (w1h[...], w1l[...]))
    d_cond2 = nt(split(cat([dsc2_s[...], dn2_s[...]], 1)), (w2h[...], w2l[...]))

    eye = (
        lax.broadcasted_iota(jnp.int32, (channels, LANES), 0) == lax.broadcasted_iota(jnp.int32, (channels, LANES), 1)
    ).astype(F32)
    gsum = jnp.sum(jnp.sum(gacc[...], axis=1), axis=-1, keepdims=True)
    rows_g = [column_sum(gsum[h * channels : (h + 1) * channels] * eye) for h in range(heads)]
    blank = jnp.zeros((1, LANES - channels), F32)
    gain_row = cat([p_pair_gain[...], blank], 1)
    pair_row = jnp.zeros((1, LANES), F32)
    for h in range(heads):
        pair_row = pair_row + rows_g[h] * cat([p_w_pair[h : h + 1, :], blank], 1)
    pair_grad = cat([v * gain_row for v in rows_g] + [jnp.zeros((8 - heads, LANES), F32)], 0)
    small = {
        "b_scale1": column_sum(dsc1),
        "b_query": column_sum(dq),
        "b_scale2": column_sum(dsc2_s[...]),
        "b_zero1": column_sum(dz1_s[...]),
        "b_zero2": column_sum(dz2_s[...]),
        "s_gain1": column_sum(d_cond1 * ns),
        "s_gain2": column_sum(d_cond2 * ns),
        "pair_gain": pair_row,
    }
    acc_l[PLACE["vectors"] : PLACE["vectors"] + 8] = cat([small[name] for name in VECTORS], 0)
    acc_l[PLACE["w_pair"] : PLACE["w_pair"] + 8] = pair_grad
    if late > LATE_ROWS:
        acc_l[LATE_ROWS:] = jnp.zeros((late - LATE_ROWS, LANES), F32)

    l1 = start(scatter_core(acc_l, late, recv_lc, lc))
    wait(e2)
    add_xy(acc_e, early, recv_exy)
    copies = []
    for o in range(1, nz):
        zz, device = z_peer(o)
        source = acc_e.at[span(at_e + zz * chunk_e, chunk_e)]
        copies.append(remote(source, recv_ez.at[o - 1], ez_send.at[o - 1], ez_recv.at[o - 1], device))
    e3 = start(copies)
    wait(l1)
    add_core(acc_l, late, recv_lc)
    l2 = start(scatter_xy(acc_l, late, recv_lxy, lxy))

    g_atoms[...] = dfirst_s[...] + norm_back(d_n1 * sc1, na, ra_s[...])
    outputs += start([pltpu.make_async_copy(g_atoms, g_atoms_hbm, out_sem.at[2])])

    wait(e3)
    mine = span(at_e + z * chunk_e, chunk_e)
    value = acc_e[mine, :]
    for o in range(1, nz):
        value = value + recv_ez[o - 1]
    res_e[mine, :] = value
    copies = []
    for o in range(1, nz):
        at = nz - 2 + o
        copies.append(remote(res_e.at[mine], res_e.at[mine], ez_send.at[at], ez_recv.at[at], z_peer(o)[1]))
    e4 = start(copies)

    d_ns = d_cond1 * p_s_gain1[...] + d_cond2 * p_s_gain2[...]
    g_single[...] = norm_back(d_ns, ns, rs_s[...]) + nt(
        split(cat([dz1_s[...], dz2_s[...]], 1)), (wzh[...], wzl[...])
    )
    outputs += start([pltpu.make_async_copy(g_single, g_single_hbm, out_sem.at[3])])

    wait(l2)
    add_xy(acc_l, late, recv_lxy)
    copies = []
    for o in range(1, nz):
        copies.append(
            remote(
                acc_l.at[span(at_l, part_l)], recv_lz.at[z], lz_send.at[o - 1], lz_recv.at[o - 1], z_peer(o)[1]
            )
        )
    l3 = start(copies)
    wait(e4)
    e5 = start(gather_xy(res_e, early, exy))
    recv_lz[z] = acc_l[span(at_l, part_l), :]
    wait(l3)
    value = recv_lz[0]
    for i in range(1, nz):
        value = value + recv_lz[i]
    res_l[span(at_l, part_l), :] = value
    l4 = start(gather_xy(res_l, late, lxy))
    wait(e5)
    e6 = start(gather_core(res_e, early, early_hbm, ec) + keep(res_e, early, early_hbm, out_sem.at[4]))
    wait(l4)
    l5 = start(gather_core(res_l, late, late_hbm, lc) + keep(res_l, late, late_hbm, out_sem.at[5]))
    wait(e6)
    wait(l5)
    wait(outputs)


def unpack_kernel(*refs):
    n, v = len(EARLY) + len(LATE), len(VECTORS)
    ins, refs = refs[:6], refs[6:]
    outs, mats, rows, wp, refs = refs[:4], refs[4 : 4 + n], refs[4 + n : 4 + n + v], refs[4 + n + v], refs[5 + n + v :]
    stage, (in_sems, out_sems) = refs[:6], refs[6:]
    loads, stores = [], []

    def load(a, b):
        loads.append(pltpu.make_async_copy(a, b, in_sems.at[len(loads)]))
        loads[-1].start()
        return loads[-1]

    def store(a, b):
        stores.append(pltpu.make_async_copy(a, b, out_sems.at[len(stores)]))
        stores[-1].start()

    early, late = load(ins[4], stage[4]), load(ins[5], stage[5])
    big = [
        (load(a.at[c], mid.at[c]), mid.at[c], b.at[c])
        for a, mid, b in zip(ins[:4], stage[:4], outs)
        for c in range(a.shape[0])
    ]
    at = 0
    for group, arrived, packed in ((EARLY, early, stage[4]), (LATE, late, stage[5])):
        arrived.wait()
        for name, _, columns in group:
            base, height = PLACE[name], mats[at].shape[0]
            for b in range(columns):
                store(packed.at[pl.ds(base + b * height, height)], mats[at].at[:, pl.ds(b * LANES, LANES)])
            at += 1
    base = PLACE["vectors"]
    for i, ref in enumerate(rows):
        ref[...] = stage[5][base + i : base + i + 1, 0 : ref.shape[1]]
    base = PLACE["w_pair"]
    wp[...] = stage[5][base : base + wp.shape[0], 0 : wp.shape[1]]
    for arrived, mid, b in big:
        arrived.wait()
        store(mid, b)
    for copy in stores:
        copy.wait()


def shards(dpn, seqn, atoms, single_cond, pair_block, atom_count, *rest):
    params, cotangent = dict(zip(PARAMS, rest[:-1])), rest[-1]
    params["w_pair"] = params["w_pair"].T
    samples, rows, width = atoms.shape
    nwin, channels = pair_block.shape[1:3]
    heads = params["w_pair"].shape[0]
    flat = samples * rows
    nz, nx = 4, seqn // 8
    nxy = dpn * nx
    grain_e, grain_l = 8 * 2 * nxy * nz, 8 * 2 * nxy
    early = -(-EARLY_ROWS // grain_e) * grain_e
    late = -(-LATE_ROWS // grain_l) * grain_l
    windows = samples * nwin
    hidden = params["w_down"].shape[0]

    def row(v):
        return v.reshape(1, -1) if v.ndim == 1 else v

    vmem = pl.BlockSpec(memory_space=pltpu.VMEM)
    smem = pl.BlockSpec(memory_space=pltpu.SMEM)
    anyw = pl.BlockSpec(memory_space=pl.ANY)

    def buf(*shape):
        return pltpu.VMEM(shape, F32)

    def low(*shape):
        return [pltpu.VMEM(shape, BF16), pltpu.VMEM(shape, BF16)]

    def sems(n):
        return [pltpu.SemaphoreType.DMA((n,)), pltpu.SemaphoreType.DMA((n,))]

    tall = (flat, width)
    extended = (samples, rows + 2 * HALO, 2 * width)
    scratch = [
        buf(*pair_block.shape),
        buf(windows, heads * WQ, KW),
        buf(windows, WQ, KW),
        buf(windows, 2, WQ, KW),
        buf(windows, heads * WQ, KW),
        buf(windows, heads * WQ, KW),
        buf(*extended),
        buf(*extended),
        buf(2, samples, HALO, 2 * width),
    ]
    scratch += low(*extended)
    scratch += low(width, 2 * width)
    scratch += low(width, 4 * width)
    scratch += low(width, 2 * width)
    scratch += low(width, 2 * width)
    scratch += low(width, 2 * hidden)
    scratch += low(hidden, width)
    scratch += low(width, width)
    scratch += low(*tall) + low(*tall) + low(*tall)
    scratch += [buf(*tall) for _ in range(22)]
    scratch += [
        buf(heads * channels, 8, KW),
        buf(early, LANES),
        buf(early, LANES),
        buf(late, LANES),
        buf(late, LANES),
        buf(early // 2, LANES),
        buf(nxy - 1, early // (2 * nxy), LANES),
        buf(nz - 1, early // (2 * nxy * nz), LANES),
        buf(late // 2, LANES),
        buf(nxy - 1, late // (2 * nxy), LANES),
        buf(nz, late // (2 * nxy), LANES),
        pltpu.SemaphoreType.DMA((samples,)),
        pltpu.SemaphoreType.DMA((6,)),
    ]
    scratch += sems(4) + sems(2) + sems(2 * (nxy - 1)) + sems(2 * (nz - 1))
    scratch += sems(2) + sems(2 * (nxy - 1)) + sems(nz - 1)
    sizes = (samples, rows, dpn, seqn, early, late)
    big = pl.pallas_call(
        functools.partial(block_kernel, sizes),
        out_shape=[
            jax.ShapeDtypeStruct(tall, F32),
            jax.ShapeDtypeStruct(tall, F32),
            jax.ShapeDtypeStruct(tall, F32),
            jax.ShapeDtypeStruct(pair_block.shape, F32),
            jax.ShapeDtypeStruct((early, LANES), F32),
            jax.ShapeDtypeStruct((late, LANES), F32),
        ],
        in_specs=[smem] * 3 + [vmem] * (3 + len(PARAMS)) + [anyw],
        out_specs=[anyw] * 6,
        scratch_shapes=scratch,
        compiler_params=pltpu.CompilerParams(
            collective_id=0, has_side_effects=True, vmem_limit_bytes=60 * 2**20
        ),
        name="block",
    )(
        atom_count,
        params["pair_gain"],
        params["w_pair"],
        atoms.reshape(tall),
        single_cond.reshape(tall),
        cotangent.reshape(tall),
        *[row(params[name]) for name in PARAMS],
        pair_block,
    )

    names = [name for name, _, _ in EARLY + LATE]
    mats = [jax.ShapeDtypeStruct(params[name].shape, F32) for name in names]
    vecs = [jax.ShapeDtypeStruct((1, params[name].shape[0]), F32) for name in VECTORS]
    big = list(big)
    for i in range(3):
        big[i] = big[i].reshape(1, *tall)
    big[3] = big[3].reshape((windows,) + pair_block.shape[2:])
    results = pl.pallas_call(
        unpack_kernel,
        out_shape=[jax.ShapeDtypeStruct(v.shape, F32) for v in big[:4]]
        + mats
        + vecs
        + [jax.ShapeDtypeStruct((heads, channels), F32)],
        in_specs=[anyw] * 6,
        out_specs=[anyw] * (4 + len(mats)) + [vmem] * (len(vecs) + 1),
        scratch_shapes=[buf(*v.shape) for v in big]
        + [
            pltpu.SemaphoreType.DMA((2 + sum(v.shape[0] for v in big[:4]),)),
            pltpu.SemaphoreType.DMA((sum(c for _, _, c in EARLY + LATE) + sum(v.shape[0] for v in big[:4]),)),
        ],
        compiler_params=pltpu.CompilerParams(vmem_limit_bytes=60 * 2**20),
        name="unpack",
    )(*big)
    grads = dict(zip(names, results[4:]))
    for name, value in zip(VECTORS, results[4 + len(mats) :]):
        grads[name] = value.reshape(-1)
    grads["w_pair"] = results[-1].T
    out, g_atoms, g_single, g_pair = results[:4]
    return (
        out.reshape(atoms.shape),
        g_atoms.reshape(atoms.shape),
        g_single.reshape(atoms.shape),
        g_pair.reshape(pair_block.shape),
    ) + tuple(grads[name] for name in PARAMS)


def solution(mesh):
    data = P("dp", "seq", None)
    pairs = P("dp", "seq", None, None, None)
    return jax.shard_map(
        functools.partial(shards, mesh.shape["dp"], mesh.shape["seq"]),
        mesh=mesh,
        in_specs=(data, data, pairs, P("dp")) + (P(),) * len(PARAMS) + (data,),
        out_specs=(data, data, data, pairs) + (P(),) * len(PARAMS),
        check_vma=False,
    )
```

time: 82.2 us -> 55.9 us (0.68)
  Pallas kernels: 74.8 us -> 55.1 us
  local copies, waits for them, and re-layouts: 6.3 us -> 0 us
    pallas_call x1, Pallas kernels: 69.9 us -> 48.8 us  [shards(): pl.pallas_call(functools.partial(block_kernel, sizes), out_shape=[jax.Sha...]
    unnamed x10 -> x0, local copies, waits for them, and re-layouts: 6.3 us -> none
    pallas_call x1, Pallas kernels: 4.99 us -> 6.26 us  [shards(): pl.pallas_call(unpack_kernel, out_shape=[jax.ShapeDtypeStruct(v.shape, F3...]
where the time goes in v2:
time: 55.9 us; the launch traced here: 55.8 us
  Pallas kernels  55.1 us (99%)
  between operations  0.69 us (1%)
    pallas_call x1, Pallas kernels, shards(): pl.pallas_call(functools.partial(block_kernel, sizes), out_shape=[jax.Sha...  48.8 us
    pallas_call x1, Pallas kernels, shards(): pl.pallas_call(unpack_kernel, out_shape=[jax.ShapeDtypeStruct(v.shape, F3...  6.26 us

profile of v2, /device:TPU:0, one launch (start us, length us, event | category | flops | bytes accessed | tf_op | source)
XLA Modules:
  0.0 55.8 jit_solution(4606639206634898609)
XLA Ops:
  0.7 48.8 %block.1 = (f32[512,128]{1,0:T(8,128)}, f32[512,128]{1,0:T(8,128)}, f32[512,128]{1,0:T(8,128)}, f32[2,8,16,32,128]{4,3,2,1,0:T(8,128)}, f32[1536,128]{1,0:T(8,128)}, /*index=5*/f32[704,128]{1,0:T(8,128)}) custom-call(s32[2]{0:T(128)} %refs_0_.1, f32[16]{0:T(128)} %refs_1_.1, f32[4,16]{1,0:T(4,128)} %bitcast.36, f32[512,128]{1,0:T(8,128)} %bitcast.30, ...), custom_call_target="tpu_custom_call" | custom-call | tf_op jit(solution)/shard_map/block/pallas_call | solution.py:841
  49.5 6.3 %unpack.1 = (f32[1,512,128]{2,1,0:T(8,128)}, f32[1,512,128]{2,1,0:T(8,128)}, f32[1,512,128]{2,1,0:T(8,128)}, f32[16,16,32,128]{3,2,1,0:T(8,128)}, f32[256,128]{1...) custom-call(f32[1,512,128]{2,1,0:T(8,128)} %bitcast.33, ...), custom_call_target="tpu_custom_call" | custom-call | tf_op jit(solution)/shard_map/unpack/pallas_call | solution.py:876

commit v3 on v2

--- a/solution.py
+++ b/solution.py
@@ -138,10 +138,14 @@
 def block_kernel(sizes, *refs):
     samples, rows, dpn, seqn, early, late = sizes
     nwin = rows // WQ
+    windows = samples * nwin
     flat = samples * rows
     nz = 4
     nx = seqn // (2 * nz)
     nxy = dpn * nx
+    n_in = 6 + len(PARAMS)
+    given, refs = refs[:n_in], refs[n_in:]
+    held, refs = refs[-n_in - 1 : -1], refs[:-n_in - 1] + refs[-1:]
     (
         count,
         gain_s,
@@ -172,13 +176,15 @@
         p_w_down,
         p_w_zero2,
         p_b_zero2,
+    ) = held
+    (
         pair_hbm,
-        out_hbm,
-        g_atoms_hbm,
-        g_single_hbm,
-        g_pair_hbm,
-        early_hbm,
-        late_hbm,
+        out,
+        g_atoms,
+        g_single,
+        g_pair,
+        res_e,
+        res_l,
         pair,
         bias,
         pmean,
@@ -229,14 +235,9 @@
         dn2_s,
         dsc2_s,
         gpre_s,
-        out,
-        g_atoms,
-        g_single,
         gacc,
         acc_e,
-        res_e,
         acc_l,
-        res_l,
         recv_ec,
         recv_exy,
         recv_ez,
@@ -244,7 +245,6 @@
         recv_lxy,
         recv_lz,
         pair_sem,
-        out_sem,
         h_send,
         h_recv,
         ec_send,
@@ -259,6 +259,7 @@
         lxy_recv,
         lz_send,
         lz_recv,
+        in_sem,
     ) = refs
     dp = lax.axis_index("dp")
     me = lax.axis_index("seq")
@@ -278,8 +279,27 @@
         zz = lax.rem(z + o, nz)
         return zz, (dp, (zz * nx + x) * 2 + core)
 
+    def load(ref):
+        i = [ref is h for h in held].index(True)
+        return pltpu.make_async_copy(given[i], ref, in_sem.at[i])
+
+    def bring(*which):
+        for ref in which:
+            load(ref).start()
+
+    def ready(*which):
+        for ref in which:
+            load(ref).wait()
+
+    norms = (single, atoms, p_s_gain1, p_w_scale1, p_w_shift1, p_b_scale1)
+    projections = (p_w_query, p_w_key, p_w_value, p_w_gate, p_b_query)
+    scalars = (count, gain_s, wpair_s)
+    conditions = (p_w_zero1, p_w_zero2, p_w_scale2, p_w_shift2, p_s_gain2, p_b_scale2, p_b_zero1, p_b_zero2)
+    transition = (p_w_hidden_gate, p_w_hidden_up, p_w_down, p_w_out, cot, p_pair_gain, p_w_pair)
+    bring(*norms, *projections, *scalars)
     for s in range(samples):
         pltpu.make_async_copy(pair_hbm.at[s], pair.at[s], pair_sem.at[s]).start()
+    bring(*conditions, *transition)
 
     barrier = pltpu.get_barrier_semaphore()
     greeted = [left, right, other]
@@ -310,8 +330,8 @@
             width = w.shape[1]
             high[:, c * width : (c + 1) * width], low[:, c * width : (c + 1) * width] = split(w[...])
 
+    ready(*norms)
     hold(w1h, w1l, p_w_scale1, p_w_shift1)
-    hold(wqh, wql, p_w_query, p_w_key, p_w_value, p_w_gate)
     ns, rs = norm(single[...])
     na, ra = norm(atoms[...])
     ns_s[...] = ns
@@ -324,6 +344,8 @@
     n1 = sc1 * na + first1[:, LANES:]
     n1_s[...] = n1
     n1_split = split(n1)
+    ready(*projections)
+    hold(wqh, wql, p_w_query, p_w_key, p_w_value, p_w_gate)
     keys_values = nn(n1_split, (wqh[:, LANES : 3 * LANES], wql[:, LANES : 3 * LANES]))
     for s in range(samples):
         kv[s, HALO : HALO + rows] = keys_values[s * rows : (s + 1) * rows]
@@ -338,6 +360,7 @@
         ]
     )
 
+    ready(*conditions, *transition)
     hold(wzh, wzl, p_w_zero1, p_w_zero2)
     hold(w2h, w2l, p_w_scale2, p_w_shift2)
     hold(whh, whl, p_w_hidden_gate, p_w_hidden_up)
@@ -354,6 +377,7 @@
     z1_s[...] = sigmoid(zeros[:, :LANES] + p_b_zero1[...])
     z2_s[...] = sigmoid(zeros[:, LANES:] + p_b_zero2[...])
 
+    ready(*scalars)
     channels = gain_s.shape[0]
     heads = wpair_s.shape[0]
     wg = [[gain_s[p] * wpair_s[h, p] for h in range(heads)] for p in range(channels)]
@@ -404,30 +428,31 @@
     nothing = jnp.zeros((KW, LANES), BF16)
 
     def heads_in(ref, at):
-        return cat([ref[pl.ds(at, WQ), :]] * heads, 0) * own_low
+        return cat([ref[at, :]] * heads, 0) * own_low
 
     def heads_out(v):
         v = v * own
         return (v[0:WQ] + v[WQ : 2 * WQ]) + (v[2 * WQ : 3 * WQ] + v[3 * WQ : 4 * WQ])
 
-    def attend(s, carry):
-        for w in range(nwin):
-            t = s * nwin + w
-            at = pl.multiple_of(s * rows + w * WQ, WQ)
-            keys = slice(w * WQ, w * WQ + KW)
-            queries = heads_in(qh_s, at), heads_in(ql_s, at)
-            scores = nt(queries, (kvh[s, keys, :LANES], kvl[s, keys, :LANES])) + bias[t]
-            expo = jnp.exp(scores - jnp.max(scores, axis=-1, keepdims=True))
-            eh, el = split(expo)
-            vh, vl = kvh[s, keys, LANES:], kvl[s, keys, LANES:]
-            high = cat([vh, ones], 1)
-            both = dot(cat([eh, el, eh], 1), cat([high, high, cat([vl, nothing], 1)], 0), NN)
-            inv = 1.0 / both[:, LANES:]
-            prob[t] = expo * inv
-            mixed_s[pl.ds(at, WQ), :] = heads_out(both[:, :LANES] * inv)
-        return carry
-
-    lax.fori_loop(0, samples, attend, 0)
+    def window(t):
+        s, w = divmod(t, nwin)
+        return s, slice(s * rows + w * WQ, s * rows + (w + 1) * WQ), slice(w * WQ, w * WQ + KW)
+
+    for t in range(windows):
+        s, at, keys = window(t)
+        queries = heads_in(qh_s, at), heads_in(ql_s, at)
+        prob[t] = nt(queries, (kvh[s, keys, :LANES], kvl[s, keys, :LANES])) + bias[t]
+    for t in range(windows):
+        s, at, keys = window(t)
+        scores = prob[t]
+        expo = jnp.exp(scores - jnp.max(scores, axis=-1, keepdims=True))
+        eh, el = split(expo)
+        vh, vl = kvh[s, keys, LANES:], kvl[s, keys, LANES:]
+        high = cat([vh, ones], 1)
+        both = dot(cat([eh, el, eh], 1), cat([high, high, cat([vl, nothing], 1)], 0), NN)
+        inv = 1.0 / both[:, LANES:]
+        prob[t] = expo * inv
+        mixed_s[at, :] = heads_out(both[:, :LANES] * inv)
 
     gated = gate_s[...] * mixed_s[...]
     gated_split = split(gated)
@@ -447,7 +472,6 @@
     z2 = z2_s[...]
     g = cot[...]
     out[...] = first + z2 * down
-    outputs = start([pltpu.make_async_copy(out, out_hbm, out_sem.at[0])])
 
     def put(acc, names, value):
         at = 0
@@ -531,13 +555,9 @@
             copies.append(remote(res.at[mine], res.at[mine], sems[0].at[at], sems[1].at[at], xy_peer(o)[1]))
         return copies
 
-    def gather_core(res, size, hbm, sems):
+    def gather_core(res, size, sems):
         mine = span(core * (size // 2), size // 2)
-        return [remote(res.at[mine], hbm.at[mine], sems[0].at[1], sems[1].at[1], other)]
-
-    def keep(res, size, hbm, sem):
-        mine = span(core * (size // 2), size // 2)
-        return [pltpu.make_async_copy(res.at[mine], hbm.at[mine], sem)]
+        return [remote(res.at[mine], res.at[mine], sems[0].at[1], sems[1].at[1], other)]
 
     ec, exy, ez = (ec_send, ec_recv), (exy_send, exy_recv), (ez_send, ez_recv)
     lc, lxy, lz = (lc_send, lc_recv), (lxy_send, lxy_recv), (lz_send, lz_recv)
@@ -552,29 +572,23 @@
     dkv[...] = jnp.zeros_like(dkv)
     less = -jnp.ones((KW, LANES), BF16)
 
-    def attend_back(s):
-        for w in range(nwin):
-            t = s * nwin + w
-            at = s * rows + w * WQ
-            keys = slice(w * WQ, w * WQ + KW)
-            queries = heads_in(qh_s, at), heads_in(ql_s, at)
-            mh, ml = heads_in(mh_s, at), heads_in(ml_s, at)
-            th, tl = heads_in(th_s, at), heads_in(tl_s, at)
-            vh, vl = kvh[s, keys, LANES:], kvl[s, keys, LANES:]
-            weights = prob[t]
-            d_scores = weights * dot(cat([mh, ml, mh, th, tl], 1), cat([vh, vh, vl, less, less], 1), NT)
-            ds[t] = d_scores
-            d_split = split(d_scores)
-            dq_s[pl.ds(at, WQ), :] = heads_out(nn(d_split, (kvh[s, keys, :LANES], kvl[s, keys, :LANES]))) * scale
-            dkv[s, keys, :LANES] += tn(d_split, queries)
-            dkv[s, keys, LANES:] += tn(split(weights), (mh, ml))
-
-    for s in range(samples):
-        attend_back(s)
-        if s == 0:
-            wait(e1)
-            add_core(acc_e, early, recv_ec)
-            e2 = start(scatter_xy(acc_e, early, recv_exy, exy))
+    for t in range(windows):
+        s, at, keys = window(t)
+        mh, ml = heads_in(mh_s, at), heads_in(ml_s, at)
+        th, tl = heads_in(th_s, at), heads_in(tl_s, at)
+        vh, vl = kvh[s, keys, LANES:], kvl[s, keys, LANES:]
+        ds[t] = prob[t] * dot(cat([mh, ml, mh, th, tl], 1), cat([vh, vh, vl, less, less], 1), NT)
+
+    wait(e1)
+    add_core(acc_e, early, recv_ec)
+    e2 = start(scatter_xy(acc_e, early, recv_exy, exy))
+
+    for t in range(windows):
+        s, at, keys = window(t)
+        dkv[s, keys, :LANES] += tn(split(ds[t]), (heads_in(qh_s, at), heads_in(ql_s, at)))
+    for t in range(windows):
+        s, at, keys = window(t)
+        dkv[s, keys, LANES:] += tn(split(prob[t]), (heads_in(mh_s, at), heads_in(ml_s, at)))
 
     halos = start(
         [
@@ -582,6 +596,10 @@
             remote(dkv.at[:, HALO + rows : 2 * HALO + rows], dhalo.at[0], h_send.at[3], h_recv.at[3], right),
         ]
     )
+
+    for t in range(windows):
+        s, at, keys = window(t)
+        dq_s[at, :] = heads_out(nn(split(ds[t]), (kvh[s, keys, :LANES], kvl[s, keys, :LANES]))) * scale
 
     gacc[...] = jnp.zeros_like(gacc)
 
@@ -607,11 +625,10 @@
                 d = d + u[h] * wg[p][h]
                 term = v * u[h] - mu[h]
                 gacc[h * channels + p] += (term[0:8] + term[8:16]) + (term[16:24] + term[24:32])
-            pair[s, w, p] = d
+            g_pair[s, w, p] = d
         return carry
 
     lax.fori_loop(0, samples * nwin, pair_back, 0)
-    outputs += start([pltpu.make_async_copy(pair, g_pair_hbm, out_sem.at[1])])
 
     wait(halos)
     for s in range(samples):
@@ -676,7 +693,6 @@
     l2 = start(scatter_xy(acc_l, late, recv_lxy, lxy))
 
     g_atoms[...] = dfirst_s[...] + norm_back(d_n1 * sc1, na, ra_s[...])
-    outputs += start([pltpu.make_async_copy(g_atoms, g_atoms_hbm, out_sem.at[2])])
 
     wait(e3)
     mine = span(at_e + z * chunk_e, chunk_e)
@@ -694,7 +710,6 @@
     g_single[...] = norm_back(d_ns, ns, rs_s[...]) + nt(
         split(cat([dz1_s[...], dz2_s[...]], 1)), (wzh[...], wzl[...])
     )
-    outputs += start([pltpu.make_async_copy(g_single, g_single_hbm, out_sem.at[3])])
 
     wait(l2)
     add_xy(acc_l, late, recv_lxy)
@@ -716,53 +731,39 @@
     res_l[span(at_l, part_l), :] = value
     l4 = start(gather_xy(res_l, late, lxy))
     wait(e5)
-    e6 = start(gather_core(res_e, early, early_hbm, ec) + keep(res_e, early, early_hbm, out_sem.at[4]))
+    e6 = start(gather_core(res_e, early, ec))
     wait(l4)
-    l5 = start(gather_core(res_l, late, late_hbm, lc) + keep(res_l, late, late_hbm, out_sem.at[5]))
+    l5 = start(gather_core(res_l, late, lc))
     wait(e6)
     wait(l5)
-    wait(outputs)
 
 
 def unpack_kernel(*refs):
     n, v = len(EARLY) + len(LATE), len(VECTORS)
     ins, refs = refs[:6], refs[6:]
-    outs, mats, rows, wp, refs = refs[:4], refs[4 : 4 + n], refs[4 + n : 4 + n + v], refs[4 + n + v], refs[5 + n + v :]
-    stage, (in_sems, out_sems) = refs[:6], refs[6:]
-    loads, stores = [], []
-
-    def load(a, b):
-        loads.append(pltpu.make_async_copy(a, b, in_sems.at[len(loads)]))
-        loads[-1].start()
-        return loads[-1]
-
-    def store(a, b):
-        stores.append(pltpu.make_async_copy(a, b, out_sems.at[len(stores)]))
-        stores[-1].start()
-
-    early, late = load(ins[4], stage[4]), load(ins[5], stage[5])
-    big = [
-        (load(a.at[c], mid.at[c]), mid.at[c], b.at[c])
-        for a, mid, b in zip(ins[:4], stage[:4], outs)
-        for c in range(a.shape[0])
-    ]
+    outs, mats, rows, wp, sems = refs[:4], refs[4 : 4 + n], refs[4 + n : 4 + n + v], refs[4 + n + v], refs[5 + n + v]
+    copies = []
+
+    def move(a, b):
+        copies.append(pltpu.make_async_copy(a, b, sems.at[len(copies)]))
+        copies[-1].start()
+
+    for a, b in zip(ins[3::-1], outs[::-1]):
+        for c in range(a.shape[0]):
+            move(a.at[c], b.at[c])
     at = 0
-    for group, arrived, packed in ((EARLY, early, stage[4]), (LATE, late, stage[5])):
-        arrived.wait()
+    for group, packed in ((EARLY, ins[4]), (LATE, ins[5])):
         for name, _, columns in group:
             base, height = PLACE[name], mats[at].shape[0]
             for b in range(columns):
-                store(packed.at[pl.ds(base + b * height, height)], mats[at].at[:, pl.ds(b * LANES, LANES)])
+                move(packed.at[pl.ds(base + b * height, height)], mats[at].at[:, pl.ds(b * LANES, LANES)])
             at += 1
     base = PLACE["vectors"]
     for i, ref in enumerate(rows):
-        ref[...] = stage[5][base + i : base + i + 1, 0 : ref.shape[1]]
+        ref[...] = ins[5][base + i : base + i + 1, 0 : ref.shape[1]]
     base = PLACE["w_pair"]
-    wp[...] = stage[5][base : base + wp.shape[0], 0 : wp.shape[1]]
-    for arrived, mid, b in big:
-        arrived.wait()
-        store(mid, b)
-    for copy in stores:
+    wp[...] = ins[5][base : base + wp.shape[0], 0 : wp.shape[1]]
+    for copy in copies:
         copy.wait()
 
 
@@ -785,7 +786,6 @@
         return v.reshape(1, -1) if v.ndim == 1 else v
 
     vmem = pl.BlockSpec(memory_space=pltpu.VMEM)
-    smem = pl.BlockSpec(memory_space=pltpu.SMEM)
     anyw = pl.BlockSpec(memory_space=pl.ANY)
 
     def buf(*shape):
@@ -819,12 +819,10 @@
     scratch += low(hidden, width)
     scratch += low(width, width)
     scratch += low(*tall) + low(*tall) + low(*tall)
-    scratch += [buf(*tall) for _ in range(22)]
+    scratch += [buf(*tall) for _ in range(19)]
     scratch += [
         buf(heads * channels, 8, KW),
         buf(early, LANES),
-        buf(early, LANES),
-        buf(late, LANES),
         buf(late, LANES),
         buf(early // 2, LANES),
         buf(nxy - 1, early // (2 * nxy), LANES),
@@ -833,29 +831,10 @@
         buf(nxy - 1, late // (2 * nxy), LANES),
         buf(nz, late // (2 * nxy), LANES),
         pltpu.SemaphoreType.DMA((samples,)),
-        pltpu.SemaphoreType.DMA((6,)),
     ]
     scratch += sems(4) + sems(2) + sems(2 * (nxy - 1)) + sems(2 * (nz - 1))
     scratch += sems(2) + sems(2 * (nxy - 1)) + sems(nz - 1)
-    sizes = (samples, rows, dpn, seqn, early, late)
-    big = pl.pallas_call(
-        functools.partial(block_kernel, sizes),
-        out_shape=[
-            jax.ShapeDtypeStruct(tall, F32),
-            jax.ShapeDtypeStruct(tall, F32),
-            jax.ShapeDtypeStruct(tall, F32),
-            jax.ShapeDtypeStruct(pair_block.shape, F32),
-            jax.ShapeDtypeStruct((early, LANES), F32),
-            jax.ShapeDtypeStruct((late, LANES), F32),
-        ],
-        in_specs=[smem] * 3 + [vmem] * (3 + len(PARAMS)) + [anyw],
-        out_specs=[anyw] * 6,
-        scratch_shapes=scratch,
-        compiler_params=pltpu.CompilerParams(
-            collective_id=0, has_side_effects=True, vmem_limit_bytes=60 * 2**20
-        ),
-        name="block",
-    )(
+    arrays = [
         atom_count,
         params["pair_gain"],
         params["w_pair"],
@@ -864,7 +843,22 @@
         cotangent.reshape(tall),
         *[row(params[name]) for name in PARAMS],
         pair_block,
-    )
+    ]
+    scratch += [pltpu.SMEM(v.shape, v.dtype) for v in arrays[:3]]
+    scratch += [buf(*v.shape) for v in arrays[3:-1]]
+    scratch += [pltpu.SemaphoreType.DMA((len(arrays) - 1,))]
+    sizes = (samples, rows, dpn, seqn, early, late)
+    big = pl.pallas_call(
+        functools.partial(block_kernel, sizes),
+        out_shape=[buf(*shape) for shape in (tall, tall, tall, pair_block.shape, (early, LANES), (late, LANES))],
+        in_specs=[anyw] * (7 + len(PARAMS)),
+        out_specs=[vmem] * 6,
+        scratch_shapes=scratch,
+        compiler_params=pltpu.CompilerParams(
+            collective_id=0, has_side_effects=True, vmem_limit_bytes=40 * 2**20
+        ),
+        name="block",
+    )(*[pltpu.with_memory_space_constraint(v, pltpu.HBM) for v in arrays])
 
     names = [name for name, _, _ in EARLY + LATE]
     mats = [jax.ShapeDtypeStruct(params[name].shape, F32) for name in names]
@@ -872,23 +866,20 @@
     big = list(big)
     for i in range(3):
         big[i] = big[i].reshape(1, *tall)
-    big[3] = big[3].reshape((windows,) + pair_block.shape[2:])
     results = pl.pallas_call(
         unpack_kernel,
         out_shape=[jax.ShapeDtypeStruct(v.shape, F32) for v in big[:4]]
         + mats
         + vecs
         + [jax.ShapeDtypeStruct((heads, channels), F32)],
-        in_specs=[anyw] * 6,
+        in_specs=[vmem] * 6,
         out_specs=[anyw] * (4 + len(mats)) + [vmem] * (len(vecs) + 1),
-        scratch_shapes=[buf(*v.shape) for v in big]
-        + [
-            pltpu.SemaphoreType.DMA((2 + sum(v.shape[0] for v in big[:4]),)),
+        scratch_shapes=[
             pltpu.SemaphoreType.DMA((sum(c for _, _, c in EARLY + LATE) + sum(v.shape[0] for v in big[:4]),)),
         ],
-        compiler_params=pltpu.CompilerParams(vmem_limit_bytes=60 * 2**20),
+        compiler_params=pltpu.CompilerParams(vmem_limit_bytes=16 * 2**20),
         name="unpack",
-    )(*big)
+    )(*[pltpu.with_memory_space_constraint(v, pltpu.VMEM) for v in big])
     grads = dict(zip(names, results[4:]))
     for name, value in zip(VECTORS, results[4 + len(mats) :]):
         grads[name] = value.reshape(-1)

time: 55.9 us -> 47.3 us (0.85)
  Pallas kernels: 55.1 us -> 46.5 us
    pallas_call x1, Pallas kernels: 48.8 us -> 43 us  [shards(): pl.pallas_call(functools.partial(block_kernel, sizes), out_shape=[buf(*sh...]
    pallas_call x1, Pallas kernels: 6.26 us -> 3.41 us  [shards(): pl.pallas_call(unpack_kernel, out_shape=[jax.ShapeDtypeStruct(v.shape, F3...]
where the time goes in v3:
time: 47.3 us; the launch traced here: 47.1 us
  Pallas kernels  46.5 us (98%)
  between operations  0.69 us (1%)
    pallas_call x1, Pallas kernels, shards(): pl.pallas_call(functools.partial(block_kernel, sizes), out_shape=[buf(*sh...  43 us
    pallas_call x1, Pallas kernels, shards(): pl.pallas_call(unpack_kernel, out_shape=[jax.ShapeDtypeStruct(v.shape, F3...  3.41 us

profile of v3, /device:TPU:0, one launch (start us, length us, event | category | flops | bytes accessed | tf_op | source)
XLA Modules:
  0.0 47.1 jit_solution(6655383532234847168)
XLA Ops:
  0.7 43.0 %block.1 = (f32[512,128]{1,0:T(8,128)S(1)}, f32[512,128]{1,0:T(8,128)S(1)}, f32[512,128]{1,0:T(8,128)S(1)}, f32[2,8,16,32,128]{4,3,2,1,0:T(8,128)S(1)}, f32[1536,128]{1,0:T(8,128)S(1)}, /*index=5*/f32[704,128]{1,0:T(8,128)S(1)}) custom-call(s32[2]{0:T(128)} %refs_0_.1, f32[16]{0:T(128)} %refs_1_.1, f32[4,16]{1,0:T(4,128)} %bitcast.33, f32[512,128]{1,0:T(8,128)} %bitcast.30, ...), custom_call_target="tpu_custom_call" | custom-call | tf_op jit(solution)/shard_map/block/pallas_call | solution.py:851
  43.7 3.4 %unpack.1 = (f32[1,512,128]{2,1,0:T(8,128)}, f32[1,512,128]{2,1,0:T(8,128)}, f32[1,512,128]{2,1,0:T(8,128)}, f32[2,8,16,32,128]{4,3,2,1,0:T(8,128)}, f32[256,128...) custom-call(f32[1,512,128]{2,1,0:T(8,128)S(1)} %bitcast.27, ...), custom_call_target="tpu_custom_call" | custom-call | tf_op jit(solution)/shard_map/unpack/pallas_call | solution.py:869

commit v4 on v3

--- a/solution.py
+++ b/solution.py
@@ -69,9 +69,7 @@
             place[name] = row
             row += rows * columns * LANES
         used.append(row)
-    place["vectors"] = used[1]
-    place["w_pair"] = used[1] + 8
-    return place, used[0], used[1] + 16
+    return place, used[0], used[1]
 
 
 PLACE, EARLY_ROWS, LATE_ROWS = offsets()
@@ -146,6 +144,8 @@
     n_in = 6 + len(PARAMS)
     given, refs = refs[:n_in], refs[n_in:]
     held, refs = refs[-n_in - 1 : -1], refs[:-n_in - 1] + refs[-1:]
+    n_e, n_l = 1 + 2 * len(early.parts), 1 + 2 * len(late.parts)
+    landing_e, landing_l, refs = refs[-n_e - n_l - 1 : -n_l - 1], refs[-n_l - 1 : -1], refs[: -n_e - n_l - 1] + refs[-1:]
     (
         count,
         gain_s,
@@ -185,6 +185,7 @@
         g_pair,
         res_e,
         res_l,
+        res_s,
         pair,
         bias,
         pmean,
@@ -238,27 +239,19 @@
         gacc,
         acc_e,
         acc_l,
-        recv_ec,
-        recv_exy,
-        recv_ez,
-        recv_lc,
-        recv_lxy,
-        recv_lz,
+        acc_s,
+        recv_sc,
+        recv_sxy,
+        recv_sz,
         pair_sem,
         h_send,
         h_recv,
-        ec_send,
-        ec_recv,
-        exy_send,
-        exy_recv,
-        ez_send,
-        ez_recv,
-        lc_send,
-        lc_recv,
-        lxy_send,
-        lxy_recv,
-        lz_send,
-        lz_recv,
+        e_send,
+        e_recv,
+        l_send,
+        l_recv,
+        s_send,
+        s_recv,
         in_sem,
     ) = refs
     dp = lax.axis_index("dp")
@@ -348,16 +341,38 @@
     hold(wqh, wql, p_w_query, p_w_key, p_w_value, p_w_gate)
     keys_values = nn(n1_split, (wqh[:, LANES : 3 * LANES], wql[:, LANES : 3 * LANES]))
     for s in range(samples):
-        kv[s, HALO : HALO + rows] = keys_values[s * rows : (s + 1) * rows]
+        block = keys_values[s * rows : (s + 1) * rows]
+        kv[s, HALO : HALO + rows] = block
+        kvh[s, HALO : HALO + rows], kvl[s, HALO : HALO + rows] = split(block)
+
+    def swap(leftward, rightward):
+        def begin():
+            @pl.when(me > 0)
+            def _():
+                leftward.start()
+
+            @pl.when(me < seqn - 1)
+            def _():
+                rightward.start()
+
+        def end():
+            @pl.when(me > 0)
+            def _():
+                leftward.wait_send()
+                rightward.wait_recv()
+
+            @pl.when(me < seqn - 1)
+            def _():
+                rightward.wait_send()
+                leftward.wait_recv()
+
+        begin()
+        return end
 
     pl.semaphore_wait(barrier, len(greeted))
-    halos = start(
-        [
-            remote(kv.at[:, rows : rows + HALO], kv.at[:, 0:HALO], h_send.at[0], h_recv.at[0], right),
-            remote(
-                kv.at[:, HALO : 2 * HALO], kv.at[:, HALO + rows : 2 * HALO + rows], h_send.at[1], h_recv.at[1], left
-            ),
-        ]
+    halos_here = swap(
+        remote(kv.at[:, HALO : 2 * HALO], kv.at[:, HALO + rows : 2 * HALO + rows], h_send.at[1], h_recv.at[1], left),
+        remote(kv.at[:, rows : rows + HALO], kv.at[:, 0:HALO], h_send.at[0], h_recv.at[0], right),
     )
 
     ready(*conditions, *transition)
@@ -414,12 +429,6 @@
 
     lax.fori_loop(0, samples * nwin, pair_bias, 0)
 
-    wait(halos)
-    for s in range(samples):
-        kv[s, 0:HALO] = jnp.where(me == 0, 0.0, kv[s, 0:HALO])
-        kv[s, HALO + rows :] = jnp.where(me == seqn - 1, 0.0, kv[s, HALO + rows :])
-    kvh[...], kvl[...] = split(kv[...])
-
     lane = lax.broadcasted_iota(jnp.int32, (heads * WQ, LANES), 1)
     row = lax.broadcasted_iota(jnp.int32, (heads * WQ, LANES), 0)
     own = (lane // 32 == row // WQ).astype(F32)
@@ -438,21 +447,36 @@
         s, w = divmod(t, nwin)
         return s, slice(s * rows + w * WQ, s * rows + (w + 1) * WQ), slice(w * WQ, w * WQ + KW)
 
-    for t in range(windows):
-        s, at, keys = window(t)
-        queries = heads_in(qh_s, at), heads_in(ql_s, at)
-        prob[t] = nt(queries, (kvh[s, keys, :LANES], kvl[s, keys, :LANES])) + bias[t]
-    for t in range(windows):
-        s, at, keys = window(t)
-        scores = prob[t]
-        expo = jnp.exp(scores - jnp.max(scores, axis=-1, keepdims=True))
-        eh, el = split(expo)
-        vh, vl = kvh[s, keys, LANES:], kvl[s, keys, LANES:]
-        high = cat([vh, ones], 1)
-        both = dot(cat([eh, el, eh], 1), cat([high, high, cat([vl, nothing], 1)], 0), NN)
-        inv = 1.0 / both[:, LANES:]
-        prob[t] = expo * inv
-        mixed_s[at, :] = heads_out(both[:, :LANES] * inv)
+    def inner(t):
+        w = t % nwin
+        return w * WQ >= HALO and w * WQ + KW <= HALO + rows
+
+    middle = [t for t in range(windows) if inner(t)]
+    border = [t for t in range(windows) if not inner(t)]
+
+    def attend(ts):
+        for t in ts:
+            s, at, keys = window(t)
+            queries = heads_in(qh_s, at), heads_in(ql_s, at)
+            prob[t] = nt(queries, (kvh[s, keys, :LANES], kvl[s, keys, :LANES])) + bias[t]
+        for t in ts:
+            s, at, keys = window(t)
+            scores = prob[t]
+            expo = jnp.exp(scores - jnp.max(scores, axis=-1, keepdims=True))
+            eh, el = split(expo)
+            vh, vl = kvh[s, keys, LANES:], kvl[s, keys, LANES:]
+            high = cat([vh, ones], 1)
+            both = dot(cat([eh, el, eh], 1), cat([high, high, cat([vl, nothing], 1)], 0), NN)
+            inv = 1.0 / both[:, LANES:]
+            prob[t] = expo * inv
+            mixed_s[at, :] = heads_out(both[:, :LANES] * inv)
+
+    attend(middle)
+    halos_here()
+    for s in range(samples):
+        for absent, at in ((me == 0, slice(0, HALO)), (me == seqn - 1, slice(HALO + rows, 2 * HALO + rows))):
+            kvh[s, at], kvl[s, at] = split(jnp.where(absent, 0.0, kv[s, at]))
+    attend(border)
 
     gated = gate_s[...] * mixed_s[...]
     gated_split = split(gated)
@@ -515,88 +539,143 @@
     d_mixed = d_gated * gate
     mh_s[...], ml_s[...] = split(d_mixed)
     th_s[...], tl_s[...] = split(d_mixed * mixed)
-    if early > EARLY_ROWS:
-        acc_e[EARLY_ROWS:] = jnp.zeros((early - EARLY_ROWS, LANES), F32)
-
-    def scatter_core(acc, size, recv, sems):
-        half = size // 2
-        return [remote(acc.at[span((1 - core) * half, half)], recv, sems[0].at[0], sems[1].at[0], other)]
-
-    def add_core(acc, size, recv):
-        mine = span(core * (size // 2), size // 2)
-        acc[mine, :] += recv[...]
-
-    def scatter_xy(acc, size, recv, sems):
-        half = size // 2
-        part = half // nxy
-        copies = []
-        for o in range(1, nxy):
-            kk, device = xy_peer(o)
-            source = acc.at[span(core * half + kk * part, part)]
-            copies.append(remote(source, recv.at[o - 1], sems[0].at[o - 1], sems[1].at[o - 1], device))
-        return copies
-
-    def add_xy(acc, size, recv):
-        half = size // 2
-        part = half // nxy
-        mine = span(core * half + k * part, part)
-        value = acc[mine, :]
-        for o in range(1, nxy):
-            value = value + recv[o - 1]
-        acc[mine, :] = value
-
-    def gather_xy(res, size, sems):
-        half = size // 2
-        part = half // nxy
-        mine = span(core * half + k * part, part)
-        copies = []
-        for o in range(1, nxy):
-            at = nxy - 2 + o
-            copies.append(remote(res.at[mine], res.at[mine], sems[0].at[at], sems[1].at[at], xy_peer(o)[1]))
-        return copies
-
-    def gather_core(res, size, sems):
-        mine = span(core * (size // 2), size // 2)
-        return [remote(res.at[mine], res.at[mine], sems[0].at[1], sems[1].at[1], other)]
-
-    ec, exy, ez = (ec_send, ec_recv), (exy_send, exy_recv), (ez_send, ez_recv)
-    lc, lxy, lz = (lc_send, lc_recv), (lxy_send, lxy_recv), (lz_send, lz_recv)
-    part_e = early // (2 * nxy)
-    chunk_e = part_e // nz
-    at_e = core * (early // 2) + k * part_e
-    part_l = late // (2 * nxy)
-    at_l = core * (late // 2) + k * part_l
-
-    e1 = start(scatter_core(acc_e, early, recv_ec, ec))
+    if early.size > EARLY_ROWS:
+        acc_e[EARLY_ROWS:] = jnp.zeros((early.size - EARLY_ROWS, LANES), F32)
+
+    groups = {"plane": (nxy, k, xy_peer), "line": (nz, z, z_peer)}
+
+    def travelling(plan, acc, res, landing, sems):
+        half = plan.size // 2
+        base = core * half
+        used = [0]
+
+        def send(src, dst, device):
+            i = used[0]
+            used[0] += 1
+            return remote(src, dst, sems[0].at[i], sems[1].at[i], device)
+
+        def gathers(name, where):
+            n, _, peer = groups[name]
+            return [send(res.at[where], res.at[where], peer(o)[1]) for o in range(1, n)]
+
+        places = []
+        for i, (first, rows_at, rows_in) in enumerate(plan.parts):
+            second = "line" if first == "plane" else "plane"
+            here = base + rows_at
+            one = rows_in // groups[first][0]
+            two = one // groups[second][0]
+            mine = here + groups[first][1] * one
+            places.append((first, second, here, one, two, mine, landing[1 + 2 * i], landing[2 + 2 * i]))
+
+        def run():
+            copies = start([send(acc.at[span((1 - core) * half, half)], landing[0], other)])
+            yield
+            wait(copies)
+            acc[span(base, half), :] += landing[0][...]
+            copies = []
+            for first, _, here, one, _, _, land, _ in places:
+                n, _, peer = groups[first]
+                for o in range(1, n):
+                    index, device = peer(o)
+                    copies.append(send(acc.at[span(here + index * one, one)], land.at[o - 1], device))
+            start(copies)
+            yield
+            wait(copies)
+            copies = []
+            for first, second, _, one, two, mine, land, land2 in places:
+                value = acc[span(mine, one), :]
+                for o in range(1, groups[first][0]):
+                    value = value + land[o - 1]
+                acc[span(mine, one), :] = value
+                n, own_index, peer = groups[second]
+                for o in range(1, n):
+                    index, device = peer(o)
+                    if plan.whole:
+                        copies.append(send(acc.at[span(mine, one)], land2.at[own_index], device))
+                    else:
+                        copies.append(send(acc.at[span(mine + index * two, two)], land2.at[o - 1], device))
+            start(copies)
+            if plan.whole:
+                for _, second, _, one, _, mine, _, land2 in places:
+                    land2[groups[second][1]] = acc[span(mine, one), :]
+            yield
+            wait(copies)
+            copies = []
+            for first, second, _, one, two, mine, _, land2 in places:
+                n, own_index, _ = groups[second]
+                if plan.whole:
+                    res[span(mine, one), :] = add_up(land2, n)
+                    copies += gathers(first, span(mine, one))
+                else:
+                    at = mine + own_index * two
+                    value = acc[span(at, two), :]
+                    for o in range(1, n):
+                        value = value + land2[o - 1]
+                    res[span(at, two), :] = value
+                    copies += gathers(second, span(at, two))
+            start(copies)
+            yield
+            if not plan.whole:
+                wait(copies)
+                copies = []
+                for first, _, _, one, _, mine, _, _ in places:
+                    copies += gathers(first, span(mine, one))
+                start(copies)
+                yield
+            wait(copies)
+            copies = start([send(res.at[span(base, half)], res.at[span(base, half)], other)])
+            yield
+            wait(copies)
+            yield
+
+        steps = run()
+        return lambda: next(steps)
+
+    def add_up(slots, count):
+        value = slots[0]
+        for i in range(1, count):
+            value = value + slots[i]
+        return value
+
+    go_early = travelling(early, acc_e, res_e, landing_e, (e_send, e_recv))
+    go_late = travelling(late, acc_l, res_l, landing_l, (l_send, l_recv))
+    go_early()
 
     dkv[...] = jnp.zeros_like(dkv)
     less = -jnp.ones((KW, LANES), BF16)
 
-    for t in range(windows):
+    def back_values(ts):
+        for t in ts:
+            s, at, keys = window(t)
+            dkv[s, keys, LANES:] += tn(split(prob[t]), (heads_in(mh_s, at), heads_in(ml_s, at)))
+
+    def back_keys(ts):
+        for t in ts:
+            s, at, keys = window(t)
+            dkv[s, keys, :LANES] += tn(split(ds[t]), (heads_in(qh_s, at), heads_in(ql_s, at)))
+
+    def swap_back(lanes, i):
+        ends = slice(0, HALO), slice(HALO + rows, 2 * HALO + rows)
+        return swap(
+            remote(dkv.at[:, ends[0], lanes], dhalo.at[1, :, :, lanes], h_send.at[i], h_recv.at[i], left),
+            remote(dkv.at[:, ends[1], lanes], dhalo.at[0, :, :, lanes], h_send.at[i + 1], h_recv.at[i + 1], right),
+        )
+
+    back_values(border)
+    values_here = swap_back(slice(LANES, 2 * LANES), 2)
+    for t in border + middle:
         s, at, keys = window(t)
         mh, ml = heads_in(mh_s, at), heads_in(ml_s, at)
         th, tl = heads_in(th_s, at), heads_in(tl_s, at)
         vh, vl = kvh[s, keys, LANES:], kvl[s, keys, LANES:]
         ds[t] = prob[t] * dot(cat([mh, ml, mh, th, tl], 1), cat([vh, vh, vl, less, less], 1), NT)
-
-    wait(e1)
-    add_core(acc_e, early, recv_ec)
-    e2 = start(scatter_xy(acc_e, early, recv_exy, exy))
-
-    for t in range(windows):
-        s, at, keys = window(t)
-        dkv[s, keys, :LANES] += tn(split(ds[t]), (heads_in(qh_s, at), heads_in(ql_s, at)))
-    for t in range(windows):
-        s, at, keys = window(t)
-        dkv[s, keys, LANES:] += tn(split(prob[t]), (heads_in(mh_s, at), heads_in(ml_s, at)))
-
-    halos = start(
-        [
-            remote(dkv.at[:, 0:HALO], dhalo.at[1], h_send.at[2], h_recv.at[2], left),
-            remote(dkv.at[:, HALO + rows : 2 * HALO + rows], dhalo.at[0], h_send.at[3], h_recv.at[3], right),
-        ]
-    )
-
+    back_keys(border)
+    keys_here = swap_back(slice(0, LANES), 4)
+
+    go_early()
+
+    back_keys(middle)
+    back_values(middle)
     for t in range(windows):
         s, at, keys = window(t)
         dq_s[at, :] = heads_out(nn(split(ds[t]), (kvh[s, keys, :LANES], kvl[s, keys, :LANES]))) * scale
@@ -628,12 +707,14 @@
             g_pair[s, w, p] = d
         return carry
 
-    lax.fori_loop(0, samples * nwin, pair_back, 0)
-
-    wait(halos)
+    ahead = windows // 2
+    lax.fori_loop(0, ahead, pair_back, 0)
+
+    values_here()
+    keys_here()
     for s in range(samples):
-        dkv[s, HALO : 2 * HALO] += dhalo[0, s]
-        dkv[s, rows : rows + HALO] += dhalo[1, s]
+        dkv[s, HALO : 2 * HALO] += jnp.where(me == 0, 0.0, dhalo[0, s])
+        dkv[s, rows : rows + HALO] += jnp.where(me == seqn - 1, 0.0, dhalo[1, s])
 
     dq = dq_s[...]
     d_keys_values = cat([dkv[s, HALO : HALO + rows] for s in range(samples)], 0)
@@ -650,6 +731,15 @@
         tn(split(n1_s[...]), (d_all[0][:, : 3 * LANES], d_all[1][:, : 3 * LANES])),
     )
     put(acc_l, ["w_scale1", "w_shift1"], tn(split(ns * p_s_gain1[...]), d_first1))
+    if late.size > LATE_ROWS:
+        acc_l[LATE_ROWS:] = jnp.zeros((late.size - LATE_ROWS, LANES), F32)
+    go_late()
+
+    g_atoms[...] = dfirst_s[...] + norm_back(d_n1 * sc1, na, ra_s[...])
+    go_late()
+    go_early()
+    lax.fori_loop(ahead, windows, pair_back, 0)
+
     d_cond1 = nt(d_first1, (w1h[...], w1l[...]))
     d_cond2 = nt(split(cat([dsc2_s[...], dn2_s[...]], 1)), (w2h[...], w2l[...]))
 
@@ -674,73 +764,65 @@
         "s_gain2": column_sum(d_cond2 * ns),
         "pair_gain": pair_row,
     }
-    acc_l[PLACE["vectors"] : PLACE["vectors"] + 8] = cat([small[name] for name in VECTORS], 0)
-    acc_l[PLACE["w_pair"] : PLACE["w_pair"] + 8] = pair_grad
-    if late > LATE_ROWS:
-        acc_l[LATE_ROWS:] = jnp.zeros((late - LATE_ROWS, LANES), F32)
-
-    l1 = start(scatter_core(acc_l, late, recv_lc, lc))
-    wait(e2)
-    add_xy(acc_e, early, recv_exy)
-    copies = []
-    for o in range(1, nz):
-        zz, device = z_peer(o)
-        source = acc_e.at[span(at_e + zz * chunk_e, chunk_e)]
-        copies.append(remote(source, recv_ez.at[o - 1], ez_send.at[o - 1], ez_recv.at[o - 1], device))
-    e3 = start(copies)
-    wait(l1)
-    add_core(acc_l, late, recv_lc)
-    l2 = start(scatter_xy(acc_l, late, recv_lxy, lxy))
-
-    g_atoms[...] = dfirst_s[...] + norm_back(d_n1 * sc1, na, ra_s[...])
-
-    wait(e3)
-    mine = span(at_e + z * chunk_e, chunk_e)
-    value = acc_e[mine, :]
-    for o in range(1, nz):
-        value = value + recv_ez[o - 1]
-    res_e[mine, :] = value
-    copies = []
-    for o in range(1, nz):
-        at = nz - 2 + o
-        copies.append(remote(res_e.at[mine], res_e.at[mine], ez_send.at[at], ez_recv.at[at], z_peer(o)[1]))
-    e4 = start(copies)
-
+    acc_s[...] = cat([small[name] for name in VECTORS] + [pair_grad], 0)
+    s1 = start([remote(acc_s, recv_sc, s_send.at[0], s_recv.at[0], other)])
     d_ns = d_cond1 * p_s_gain1[...] + d_cond2 * p_s_gain2[...]
     g_single[...] = norm_back(d_ns, ns, rs_s[...]) + nt(
         split(cat([dz1_s[...], dz2_s[...]], 1)), (wzh[...], wzl[...])
     )
 
-    wait(l2)
-    add_xy(acc_l, late, recv_lxy)
-    copies = []
-    for o in range(1, nz):
-        copies.append(
-            remote(
-                acc_l.at[span(at_l, part_l)], recv_lz.at[z], lz_send.at[o - 1], lz_recv.at[o - 1], z_peer(o)[1]
-            )
+    def spread(slots, mine, peers, first):
+        slots[mine] = acc_s[...]
+        return start(
+            [
+                remote(acc_s, slots.at[mine], s_send.at[first + i], s_recv.at[first + i], device)
+                for i, device in enumerate(peers)
+            ]
         )
-    l3 = start(copies)
-    wait(e4)
-    e5 = start(gather_xy(res_e, early, exy))
-    recv_lz[z] = acc_l[span(at_l, part_l), :]
-    wait(l3)
-    value = recv_lz[0]
-    for i in range(1, nz):
-        value = value + recv_lz[i]
-    res_l[span(at_l, part_l), :] = value
-    l4 = start(gather_xy(res_l, late, lxy))
-    wait(e5)
-    e6 = start(gather_core(res_e, early, ec))
-    wait(l4)
-    l5 = start(gather_core(res_l, late, lc))
-    wait(e6)
-    wait(l5)
+
+    go_late()
+    go_early()
+    wait(s1)
+    acc_s[...] = acc_s[...] + recv_sc[...]
+    s2 = spread(recv_sxy, k, [xy_peer(o)[1] for o in range(1, nxy)], 1)
+    wait(s2)
+    acc_s[...] = add_up(recv_sxy, nxy)
+    s3 = spread(recv_sz, z, [z_peer(o)[1] for o in range(1, nz)], nxy)
+    go_late()
+    go_early()
+    wait(s3)
+    res_s[...] = add_up(recv_sz, nz)
+    go_late()
+    go_early()
+    go_late()
+    go_early()
+
+
+class Plan:
+    def __init__(self, needed, nxy, nz, whole):
+        half = -(-needed // 2)
+        grains = (8 * nxy, 8 * nz) if whole else (8 * nxy * nz,) * 2
+        line = int(half * (0.4 if whole else 0.34)) // grains[1] * grains[1]
+        plane = -(-(half - line) // grains[0]) * grains[0]
+        self.whole, self.size = whole, 2 * (plane + line)
+        self.parts = [("plane", 0, plane)] + ([("line", plane, line)] if line else [])
+
+    def landing(self, nxy, nz):
+        count = {"plane": (nxy, nz), "line": (nz, nxy)}
+        shapes = [(self.size // 2, LANES)]
+        for first, _, rows in self.parts:
+            n, m = count[first]
+            shapes.append((n - 1, rows // n, LANES))
+            shapes.append((m, rows // n, LANES) if self.whole else (m - 1, rows // n // m, LANES))
+        return shapes
+
+    def copies(self, nxy, nz):
+        return 2 + 2 * len(self.parts) * (nxy + nz - 2)
 
 
 def unpack_kernel(*refs):
     n, v = len(EARLY) + len(LATE), len(VECTORS)
-    ins, refs = refs[:6], refs[6:]
+    ins, refs = refs[:7], refs[7:]
     outs, mats, rows, wp, sems = refs[:4], refs[4 : 4 + n], refs[4 + n : 4 + n + v], refs[4 + n + v], refs[5 + n + v]
     copies = []
 
@@ -758,11 +840,9 @@
             for b in range(columns):
                 move(packed.at[pl.ds(base + b * height, height)], mats[at].at[:, pl.ds(b * LANES, LANES)])
             at += 1
-    base = PLACE["vectors"]
     for i, ref in enumerate(rows):
-        ref[...] = ins[5][base + i : base + i + 1, 0 : ref.shape[1]]
-    base = PLACE["w_pair"]
-    wp[...] = ins[5][base : base + wp.shape[0], 0 : wp.shape[1]]
+        ref[...] = ins[6][i : i + 1, 0 : ref.shape[1]]
+    wp[...] = ins[6][v : v + wp.shape[0], 0 : wp.shape[1]]
     for copy in copies:
         copy.wait()
 
@@ -776,9 +856,8 @@
     flat = samples * rows
     nz, nx = 4, seqn // 8
     nxy = dpn * nx
-    grain_e, grain_l = 8 * 2 * nxy * nz, 8 * 2 * nxy
-    early = -(-EARLY_ROWS // grain_e) * grain_e
-    late = -(-LATE_ROWS // grain_l) * grain_l
+    early = Plan(EARLY_ROWS, nxy, nz, False)
+    late = Plan(LATE_ROWS, nxy, nz, True)
     windows = samples * nwin
     hidden = params["w_down"].shape[0]
 
@@ -822,18 +901,16 @@
     scratch += [buf(*tall) for _ in range(19)]
     scratch += [
         buf(heads * channels, 8, KW),
-        buf(early, LANES),
-        buf(late, LANES),
-        buf(early // 2, LANES),
-        buf(nxy - 1, early // (2 * nxy), LANES),
-        buf(nz - 1, early // (2 * nxy * nz), LANES),
-        buf(late // 2, LANES),
-        buf(nxy - 1, late // (2 * nxy), LANES),
-        buf(nz, late // (2 * nxy), LANES),
+        buf(early.size, LANES),
+        buf(late.size, LANES),
+        buf(16, LANES),
+        buf(16, LANES),
+        buf(nxy, 16, LANES),
+        buf(nz, 16, LANES),
         pltpu.SemaphoreType.DMA((samples,)),
     ]
-    scratch += sems(4) + sems(2) + sems(2 * (nxy - 1)) + sems(2 * (nz - 1))
-    scratch += sems(2) + sems(2 * (nxy - 1)) + sems(nz - 1)
+    scratch += sems(6) + sems(early.copies(nxy, nz)) + sems(late.copies(nxy, nz)) + sems(nxy + nz - 1)
+    scratch += [buf(*shape) for plan in (early, late) for shape in plan.landing(nxy, nz)]
     arrays = [
         atom_count,
         params["pair_gain"],
@@ -850,9 +927,9 @@
     sizes = (samples, rows, dpn, seqn, early, late)
     big = pl.pallas_call(
         functools.partial(block_kernel, sizes),
-        out_shape=[buf(*shape) for shape in (tall, tall, tall, pair_block.shape, (early, LANES), (late, LANES))],
+        out_shape=[buf(*shape) for shape in (tall, tall, tall, pair_block.shape, (early.size, LANES), (late.size, LANES), (16, LANES))],
         in_specs=[anyw] * (7 + len(PARAMS)),
-        out_specs=[vmem] * 6,
+        out_specs=[vmem] * 7,
         scratch_shapes=scratch,
         compiler_params=pltpu.CompilerParams(
             collective_id=0, has_side_effects=True, vmem_limit_bytes=40 * 2**20
@@ -872,7 +949,7 @@
         + mats
         + vecs
         + [jax.ShapeDtypeStruct((heads, channels), F32)],
-        in_specs=[vmem] * 6,
+        in_specs=[vmem] * 7,
         out_specs=[anyw] * (4 + len(mats)) + [vmem] * (len(vecs) + 1),
         scratch_shapes=[
             pltpu.SemaphoreType.DMA((sum(c for _, _, c in EARLY + LATE) + sum(v.shape[0] for v in big[:4]),)),

time: 47.3 us -> 43 us (0.909)
  Pallas kernels: 46.5 us -> 42.1 us
    pallas_call x1, Pallas kernels: 43 us -> 38.7 us  [shards(): pl.pallas_call(functools.partial(block_kernel, sizes), out_shape=[buf(*sh...]
where the time goes in v4:
time: 43 us; the launch traced here: 42.8 us
  Pallas kernels  42.1 us (98%)
  between operations  0.69 us (2%)
    pallas_call x1, Pallas kernels, shards(): pl.pallas_call(functools.partial(block_kernel, sizes), out_shape=[buf(*sh...  38.7 us
    pallas_call x1, Pallas kernels, shards(): pl.pallas_call(unpack_kernel, out_shape=[jax.ShapeDtypeStruct(v.shape, F3...  3.41 us

profile of v4, /device:TPU:0, one launch (start us, length us, event | category | flops | bytes accessed | tf_op | source)
XLA Modules:
  0.0 42.8 jit_solution(16122459468037659830)
XLA Ops:
  0.7 38.7 %block.1 = (f32[512,128]{1,0:T(8,128)S(1)}, f32[512,128]{1,0:T(8,128)S(1)}, f32[512,128]{1,0:T(8,128)S(1)}, f32[2,8,16,32,128]{4,3,2,1,0:T(8,128)S(1)}, f32[1536...) custom-call(s32[2]{0:T(128)} %refs_0_.1, f32[16]{0:T(128)} %refs_1_.1, f32[4,16]{1,0:T(4,128)} %bitcast.33, ...), custom_call_target="tpu_custom_call" | custom-call | tf_op jit(solution)/shard_map/block/pallas_call | solution.py:928
  39.4 3.4 %unpack.1 = (f32[1,512,128]{2,1,0:T(8,128)}, f32[1,512,128]{2,1,0:T(8,128)}, f32[1,512,128]{2,1,0:T(8,128)}, f32[2,8,16,32,128]{4,3,2,1,0:T(8,128)}, f32[256,128...) custom-call(f32[1,512,128]{2,1,0:T(8,128)S(1)} %bitcast.27, ...), custom_call_target="tpu_custom_call" | custom-call | tf_op jit(solution)/shard_map/unpack/pallas_call | solution.py:946

commit v5 on v4

--- a/solution.py
+++ b/solution.py
@@ -96,6 +96,14 @@
     (ah, al), (bh, bl) = a, b
     (ka,), (kb,) = dims[0]
     return dot(cat([ah, al, ah], ka), cat([bh, bh, bl], kb), dims)
+
+
+def beside(a, b, dims):
+    (ah, al), (bh, bl) = a, b
+    free = 1 - dims[0][1][0]
+    width = bh.shape[free]
+    both = dot(ah, cat([bh, bl], free), dims)
+    return both[:, :width] + (both[:, width:] + dot(al, bh, dims))
 
 
 def nn(a, b):
@@ -237,6 +245,7 @@
         dsc2_s,
         gpre_s,
         gacc,
+        gmid,
         acc_e,
         acc_l,
         acc_s,
@@ -272,27 +281,46 @@
         zz = lax.rem(z + o, nz)
         return zz, (dp, (zz * nx + x) * 2 + core)
 
-    def load(ref):
-        i = [ref is h for h in held].index(True)
-        return pltpu.make_async_copy(given[i], ref, in_sem.at[i])
+    norm_weights = (p_w_scale1, p_w_shift1)
+    projections = (p_w_key, p_w_value, p_w_query, p_w_gate)
+    conditions = (p_w_zero1, p_w_zero2, p_w_scale2, p_w_shift2)
+    transition = (p_w_hidden_gate, p_w_hidden_up, p_w_down, p_w_out)
+    together = (norm_weights, projections, conditions, transition)
+    sem_of = [[i for i, group in enumerate(together) if any(ref is r for r in group)] for ref in held]
+    used = len(together)
+    for found in sem_of:
+        if not found:
+            found.append(used)
+            used += 1
+
+    def where(ref):
+        return [ref is h for h in held].index(True)
 
     def bring(*which):
         for ref in which:
-            load(ref).start()
+            i = where(ref)
+            pltpu.make_async_copy(given[i], ref, in_sem.at[sem_of[i][0]]).start()
 
     def ready(*which):
         for ref in which:
-            load(ref).wait()
-
-    norms = (single, atoms, p_s_gain1, p_w_scale1, p_w_shift1, p_b_scale1)
-    projections = (p_w_query, p_w_key, p_w_value, p_w_gate, p_b_query)
+            if isinstance(ref, tuple):
+                total = sum(r.shape[0] * r.shape[1] for r in ref) // LANES
+                some = acc_e.at[0:total]
+                pltpu.make_async_copy(some, some, in_sem.at[sem_of[where(ref[0])][0]]).wait()
+            else:
+                i = where(ref)
+                pltpu.make_async_copy(given[i], ref, in_sem.at[sem_of[i][0]]).wait()
+
     scalars = (count, gain_s, wpair_s)
-    conditions = (p_w_zero1, p_w_zero2, p_w_scale2, p_w_shift2, p_s_gain2, p_b_scale2, p_b_zero1, p_b_zero2)
-    transition = (p_w_hidden_gate, p_w_hidden_up, p_w_down, p_w_out, cot, p_pair_gain, p_w_pair)
-    bring(*norms, *projections, *scalars)
-    for s in range(samples):
-        pltpu.make_async_copy(pair_hbm.at[s], pair.at[s], pair_sem.at[s]).start()
-    bring(*conditions, *transition)
+    bring(single, atoms, p_s_gain1, *norm_weights, p_b_scale1, *projections, p_b_query, *scalars)
+    bring(*conditions, p_s_gain2, p_b_scale2, p_b_zero1, p_b_zero2)
+
+    def pair_load(s, w):
+        return pltpu.make_async_copy(pair_hbm.at[s, w], pair.at[s, w], pair_sem.at[s])
+
+    for t in range(windows):
+        pair_load(t // nwin, t % nwin).start()
+    bring(*transition, cot, p_pair_gain, p_w_pair)
 
     barrier = pltpu.get_barrier_semaphore()
     greeted = [left, right, other]
@@ -323,10 +351,12 @@
             width = w.shape[1]
             high[:, c * width : (c + 1) * width], low[:, c * width : (c + 1) * width] = split(w[...])
 
-    ready(*norms)
+    ready(single, atoms, norm_weights, p_s_gain1, p_b_scale1)
     hold(w1h, w1l, p_w_scale1, p_w_shift1)
-    ns, rs = norm(single[...])
-    na, ra = norm(atoms[...])
+    xs, xa = single[...], atoms[...]
+    cs, ca = xs - mean_lanes(xs), xa - mean_lanes(xa)
+    rs, ra = lax.rsqrt(mean_lanes(cs * cs) + 1e-05), lax.rsqrt(mean_lanes(ca * ca) + 1e-05)
+    ns, na = cs * rs, ca * ra
     ns_s[...] = ns
     na_s[...] = na
     rs_s[...] = rs
@@ -337,9 +367,9 @@
     n1 = sc1 * na + first1[:, LANES:]
     n1_s[...] = n1
     n1_split = split(n1)
-    ready(*projections)
-    hold(wqh, wql, p_w_query, p_w_key, p_w_value, p_w_gate)
-    keys_values = nn(n1_split, (wqh[:, LANES : 3 * LANES], wql[:, LANES : 3 * LANES]))
+    ready(projections, p_b_query)
+    hold(wqh, wql, p_w_key, p_w_value, p_w_query, p_w_gate)
+    keys_values = nn(n1_split, (wqh[:, : 2 * LANES], wql[:, : 2 * LANES]))
     for s in range(samples):
         block = keys_values[s * rows : (s + 1) * rows]
         kv[s, HALO : HALO + rows] = block
@@ -375,16 +405,13 @@
         remote(kv.at[:, rows : rows + HALO], kv.at[:, 0:HALO], h_send.at[0], h_recv.at[0], right),
     )
 
-    ready(*conditions, *transition)
+    ready(conditions, p_s_gain2, p_b_scale2, p_b_zero1, p_b_zero2)
     hold(wzh, wzl, p_w_zero1, p_w_zero2)
     hold(w2h, w2l, p_w_scale2, p_w_shift2)
-    hold(whh, whl, p_w_hidden_gate, p_w_hidden_up)
-    hold(wdh, wdl, p_w_down)
-    hold(woh, wol, p_w_out)
     scale = 1.0 / math.sqrt(32)
-    query = (nn(n1_split, (wqh[:, :LANES], wql[:, :LANES])) + p_b_query[...]) * scale
-    qh_s[...], ql_s[...] = split(query)
-    gate_s[...] = sigmoid(nn(n1_split, (wqh[:, 3 * LANES :], wql[:, 3 * LANES :])))
+    query_gate = nn(n1_split, (wqh[:, 2 * LANES :], wql[:, 2 * LANES :]))
+    qh_s[...], ql_s[...] = split((query_gate[:, :LANES] + p_b_query[...]) * scale)
+    gate_s[...] = sigmoid(query_gate[:, LANES:])
     first2 = nn(split(ns * p_s_gain2[...]), (w2h[...], w2l[...]))
     sc2_s[...] = sigmoid(first2[:, :LANES] + p_b_scale2[...])
     sh2_s[...] = first2[:, LANES:]
@@ -396,10 +423,8 @@
     channels = gain_s.shape[0]
     heads = wpair_s.shape[0]
     wg = [[gain_s[p] * wpair_s[h, p] for h in range(heads)] for p in range(channels)]
-    wsum = [functools.reduce(lambda a, b: a + b, [wg[p][h] for p in range(channels)]) for h in range(heads)]
-
-    for s in range(samples):
-        pltpu.make_async_copy(pair_hbm.at[s], pair.at[s], pair_sem.at[s]).wait()
+    mid = [functools.reduce(lambda a, b: a + b, [wg[p][h] for p in range(channels)]) * (1.0 / channels) for h in range(heads)]
+    centred = [[wg[p][h] - mid[h] for h in range(heads)] for p in range(channels)]
 
     key_lane = lax.broadcasted_iota(jnp.int32, (WQ, KW), 1)
     same = key_lane == lax.broadcasted_iota(jnp.int32, (WQ, KW), 0) + HALO
@@ -408,12 +433,12 @@
         s, w = t // nwin, lax.rem(t, nwin)
         first = pair[s, w, 0]
         total, square = first, first * first
-        b = [first * wg[0][h] for h in range(heads)]
+        b = [first * centred[0][h] for h in range(heads)]
         for p in range(1, channels):
             v = pair[s, w, p]
             total = total + v
             square = square + v * v
-            b = [b[h] + v * wg[p][h] for h in range(heads)]
+            b = [b[h] + v * centred[p][h] for h in range(heads)]
         mean = total * (1.0 / channels)
         var = square * (1.0 / channels) - mean * mean
         inv = lax.rsqrt(jnp.maximum(var, 0.25))
@@ -424,10 +449,16 @@
         begin = me * rows + w * WQ - HALO
         valid = ((key_lane >= -begin) & (key_lane < count[s] - begin)) | same
         for h in range(heads):
-            bias[t, h * WQ : (h + 1) * WQ] = jnp.where(valid, inv * (b[h] - mean * wsum[h]), -1e9)
+            bias[t, h * WQ : (h + 1) * WQ] = jnp.where(valid, inv * b[h], -1e9)
         return carry
 
-    lax.fori_loop(0, samples * nwin, pair_bias, 0)
+    for s in range(samples):
+        pltpu.make_async_copy(pair_hbm.at[s], pair.at[s], pair_sem.at[s]).wait()
+        lax.fori_loop(s * nwin, (s + 1) * nwin, pair_bias, 0)
+    ready(transition, cot, p_pair_gain, p_w_pair)
+    hold(whh, whl, p_w_hidden_gate, p_w_hidden_up)
+    hold(wdh, wdl, p_w_down)
+    hold(woh, wol, p_w_out)
 
     lane = lax.broadcasted_iota(jnp.int32, (heads * WQ, LANES), 1)
     row = lax.broadcasted_iota(jnp.int32, (heads * WQ, LANES), 0)
@@ -478,25 +509,6 @@
             kvh[s, at], kvl[s, at] = split(jnp.where(absent, 0.0, kv[s, at]))
     attend(border)
 
-    gated = gate_s[...] * mixed_s[...]
-    gated_split = split(gated)
-    projected = nn(gated_split, (woh[...], wol[...]))
-    first = atoms[...] + z1_s[...] * projected
-    nf, rf = norm(first)
-    n2 = sc2_s[...] * nf + sh2_s[...]
-    n2_split = split(n2)
-    up = nn(n2_split, (whh[...], whl[...]))
-    hidden_width = up.shape[1] // 2
-    hg, hu = up[:, :hidden_width], up[:, hidden_width:]
-    sg = sigmoid(hg)
-    silu = hg * sg
-    hidden = silu * hu
-    hidden_split = split(hidden)
-    down = nn(hidden_split, (wdh[...], wdl[...]))
-    z2 = z2_s[...]
-    g = cot[...]
-    out[...] = first + z2 * down
-
     def put(acc, names, value):
         at = 0
         for name in names:
@@ -505,40 +517,54 @@
                 acc[base + b * value.shape[0] : base + (b + 1) * value.shape[0]] = value[:, at : at + LANES]
                 at += LANES
 
-    d_down = g * z2
-    dz2 = g * down * z2 * (1.0 - z2)
-    dz2_s[...] = dz2
-    d_down_split = split(d_down)
+    gated = gate_s[...] * mixed_s[...]
+    gated_split = split(gated)
+    projected = beside(gated_split, (woh[...], wol[...]), NN)
+    z2 = z2_s[...]
+    g = cot[...]
+    d_down_split = split(g * z2)
+    d_hidden = nt(d_down_split, (wdh[...], wdl[...]))
+    first = atoms[...] + z1_s[...] * projected
+    nf, rf = norm(first)
+    sc2 = sc2_s[...]
+    n2_split = split(sc2 * nf + sh2_s[...])
+    up = nn(n2_split, (whh[...], whl[...]))
+    hidden_width = up.shape[1] // 2
+    hg, hu = up[:, :hidden_width], up[:, hidden_width:]
+    sg = sigmoid(hg)
+    silu = hg * sg
+    hidden_split = split(silu * hu)
+    d_up_split = split(cat([d_hidden * hu * (sg + silu * (1.0 - sg)), d_hidden * silu], 1))
+
+    d_n2 = beside(d_up_split, (whh[...], whl[...]), NT)
+    down = beside(hidden_split, (wdh[...], wdl[...]), NN)
+    dn2_s[...] = d_n2
+    d_first = g + norm_back(d_n2 * sc2, nf, rf)
+    dfirst_s[...] = d_first
     put(acc_e, ["w_down"], tn(hidden_split, d_down_split))
-    d_hidden = nt(d_down_split, (wdh[...], wdl[...]))
-    d_up = cat([d_hidden * hu * (sg * (1.0 + hg * (1.0 - sg))), d_hidden * silu], 1)
-    d_up_split = split(d_up)
     put(acc_e, ["w_hidden_gate", "w_hidden_up"], tn(n2_split, d_up_split))
-    d_n2 = nt(d_up_split, (whh[...], whl[...]))
-    dn2_s[...] = d_n2
-    sc2 = sc2_s[...]
+    z1 = z1_s[...]
+    d_proj_split = split(d_first * z1)
+    d_gated = beside(d_proj_split, (woh[...], wol[...]), NT)
     dsc2 = d_n2 * nf * sc2 * (1.0 - sc2)
     dsc2_s[...] = dsc2
     cond2_split = split(ns_s[...] * p_s_gain2[...])
     put(acc_e, ["w_scale2", "w_shift2"], tn(cond2_split, split(cat([dsc2, d_n2], 1))))
-    d_first = g + norm_back(d_n2 * sc2, nf, rf)
-    dfirst_s[...] = d_first
-    z1 = z1_s[...]
-    d_proj = d_first * z1
-    d_proj_split = split(d_proj)
+    out[...] = first + z2 * down
+    dz2 = g * down * z2 * (1.0 - z2)
+    dz2_s[...] = dz2
     dz1 = d_first * projected * z1 * (1.0 - z1)
     dz1_s[...] = dz1
-    put(acc_e, ["w_out"], tn(gated_split, d_proj_split))
-    put(acc_e, ["w_zero1", "w_zero2"], tn(split(single[...]), split(cat([dz1, dz2], 1))))
-    d_gated = nt(d_proj_split, (woh[...], wol[...]))
     gate = gate_s[...]
     mixed = mixed_s[...]
     d_gate = d_gated * mixed * gate * (1.0 - gate)
     gpre_s[...] = d_gate
-    put(acc_e, ["w_gate"], tn(split(n1_s[...]), split(d_gate)))
     d_mixed = d_gated * gate
     mh_s[...], ml_s[...] = split(d_mixed)
     th_s[...], tl_s[...] = split(d_mixed * mixed)
+    put(acc_e, ["w_out"], tn(gated_split, d_proj_split))
+    put(acc_e, ["w_zero1", "w_zero2"], tn(split(single[...]), split(cat([dz1, dz2], 1))))
+    put(acc_e, ["w_gate"], tn(split(n1_s[...]), split(d_gate)))
     if early.size > EARLY_ROWS:
         acc_e[EARLY_ROWS:] = jnp.zeros((early.size - EARLY_ROWS, LANES), F32)
 
@@ -547,12 +573,15 @@
     def travelling(plan, acc, res, landing, sems):
         half = plan.size // 2
         base = core * half
-        used = [0]
+        step = [0]
 
         def send(src, dst, device):
-            i = used[0]
-            used[0] += 1
-            return remote(src, dst, sems[0].at[i], sems[1].at[i], device)
+            return remote(src, dst, sems[0].at[step[0]], sems[1].at[step[0]], device)
+
+        def arrived(rows_in):
+            some = acc_e.at[0:rows_in]
+            remote(some, some, sems[0].at[step[0]], sems[1].at[step[0]], other).wait()
+            step[0] += 1
 
         def gathers(name, where):
             n, _, peer = groups[name]
@@ -570,7 +599,7 @@
         def run():
             copies = start([send(acc.at[span((1 - core) * half, half)], landing[0], other)])
             yield
-            wait(copies)
+            arrived(half)
             acc[span(base, half), :] += landing[0][...]
             copies = []
             for first, _, here, one, _, _, land, _ in places:
@@ -580,7 +609,7 @@
                     copies.append(send(acc.at[span(here + index * one, one)], land.at[o - 1], device))
             start(copies)
             yield
-            wait(copies)
+            arrived(sum((groups[p[0]][0] - 1) * p[3] for p in places))
             copies = []
             for first, second, _, one, two, mine, land, land2 in places:
                 value = acc[span(mine, one), :]
@@ -599,7 +628,7 @@
                 for _, second, _, one, _, mine, _, land2 in places:
                     land2[groups[second][1]] = acc[span(mine, one), :]
             yield
-            wait(copies)
+            arrived(sum((groups[p[1]][0] - 1) * (p[3] if plan.whole else p[4]) for p in places))
             copies = []
             for first, second, _, one, two, mine, _, land2 in places:
                 n, own_index, _ = groups[second]
@@ -616,16 +645,16 @@
             start(copies)
             yield
             if not plan.whole:
-                wait(copies)
+                arrived(sum((groups[p[1]][0] - 1) * p[4] for p in places))
                 copies = []
                 for first, _, _, one, _, mine, _, _ in places:
                     copies += gathers(first, span(mine, one))
                 start(copies)
                 yield
-            wait(copies)
+            arrived(sum((groups[p[0]][0] - 1) * p[3] for p in places))
             copies = start([send(res.at[span(base, half)], res.at[span(base, half)], other)])
             yield
-            wait(copies)
+            arrived(half)
             yield
 
         steps = run()
@@ -661,17 +690,20 @@
             remote(dkv.at[:, ends[1], lanes], dhalo.at[0, :, :, lanes], h_send.at[i + 1], h_recv.at[i + 1], right),
         )
 
+    def back_scores(ts):
+        for t in ts:
+            s, at, keys = window(t)
+            mh, ml = heads_in(mh_s, at), heads_in(ml_s, at)
+            th, tl = heads_in(th_s, at), heads_in(tl_s, at)
+            vh, vl = kvh[s, keys, LANES:], kvl[s, keys, LANES:]
+            ds[t] = prob[t] * dot(cat([mh, ml, mh, th, tl], 1), cat([vh, vh, vl, less, less], 1), NT)
+
     back_values(border)
     values_here = swap_back(slice(LANES, 2 * LANES), 2)
-    for t in border + middle:
-        s, at, keys = window(t)
-        mh, ml = heads_in(mh_s, at), heads_in(ml_s, at)
-        th, tl = heads_in(th_s, at), heads_in(tl_s, at)
-        vh, vl = kvh[s, keys, LANES:], kvl[s, keys, LANES:]
-        ds[t] = prob[t] * dot(cat([mh, ml, mh, th, tl], 1), cat([vh, vh, vl, less, less], 1), NT)
+    back_scores(border)
     back_keys(border)
     keys_here = swap_back(slice(0, LANES), 4)
-
+    back_scores(middle)
     go_early()
 
     back_keys(middle)
@@ -680,34 +712,41 @@
         s, at, keys = window(t)
         dq_s[at, :] = heads_out(nn(split(ds[t]), (kvh[s, keys, :LANES], kvl[s, keys, :LANES]))) * scale
 
+    dq = dq_s[...]
+    rest = split(cat([dq, gpre_s[...]], 1))
+    n1_split = split(n1_s[...])
+    d_n1 = beside(rest, (wqh[:, 2 * LANES :], wql[:, 2 * LANES :]), NT)
+    put(acc_l, ["w_query"], tn(n1_split, (rest[0][:, :LANES], rest[1][:, :LANES])))
+
     gacc[...] = jnp.zeros_like(gacc)
+    gmid[...] = jnp.zeros_like(gmid)
+
+    def fold(v):
+        return (v[0:8] + v[8:16]) + (v[16:24] + v[24:32])
 
     def pair_back(t, carry):
         s, w = t // nwin, lax.rem(t, nwin)
         inv, live = prs[t, 0], prs[t, 1]
         mean = pmean[t]
-        u, along, level = [], None, None
+        u, along = [], None
         for h in range(heads):
             d = ds[t, h * WQ : (h + 1) * WQ]
             u.append(d * inv)
             a = d * bias[t, h * WQ : (h + 1) * WQ]
-            b = u[h] * (wsum[h] * (1.0 / channels))
             along = a if along is None else along + a
-            level = b if level is None else level + b
+            gmid[h] += fold(mean * u[h])
         c1 = along * live
-        c0 = mean * c1 - level
-        mu = [mean * u[h] for h in range(heads)]
+        c0 = mean * c1
         for p in range(channels):
             v = pair[s, w, p]
             d = c0 - v * c1
             for h in range(heads):
-                d = d + u[h] * wg[p][h]
-                term = v * u[h] - mu[h]
-                gacc[h * channels + p] += (term[0:8] + term[8:16]) + (term[16:24] + term[24:32])
+                d = d + u[h] * centred[p][h]
+                gacc[h * channels + p] += fold(v * u[h])
             g_pair[s, w, p] = d
         return carry
 
-    ahead = windows // 2
+    ahead = 3 * windows // 8
     lax.fori_loop(0, ahead, pair_back, 0)
 
     values_here()
@@ -716,20 +755,14 @@
         dkv[s, HALO : 2 * HALO] += jnp.where(me == 0, 0.0, dhalo[0, s])
         dkv[s, rows : rows + HALO] += jnp.where(me == seqn - 1, 0.0, dhalo[1, s])
 
-    dq = dq_s[...]
-    d_keys_values = cat([dkv[s, HALO : HALO + rows] for s in range(samples)], 0)
-    d_all = split(cat([dq, d_keys_values, gpre_s[...]], 1))
-    d_n1 = nt(d_all, (wqh[...], wql[...]))
+    d_keys_values = split(cat([dkv[s, HALO : HALO + rows] for s in range(samples)], 0))
+    d_n1 = d_n1 + beside(d_keys_values, (wqh[:, : 2 * LANES], wql[:, : 2 * LANES]), NT)
     na = na_s[...]
     sc1 = sc1_s[...]
     dsc1 = d_n1 * na * sc1 * (1.0 - sc1)
     d_first1 = split(cat([dsc1, d_n1], 1))
     ns = ns_s[...]
-    put(
-        acc_l,
-        ["w_query", "w_key", "w_value"],
-        tn(split(n1_s[...]), (d_all[0][:, : 3 * LANES], d_all[1][:, : 3 * LANES])),
-    )
+    put(acc_l, ["w_key", "w_value"], tn(n1_split, d_keys_values))
     put(acc_l, ["w_scale1", "w_shift1"], tn(split(ns * p_s_gain1[...]), d_first1))
     if late.size > LATE_ROWS:
         acc_l[LATE_ROWS:] = jnp.zeros((late.size - LATE_ROWS, LANES), F32)
@@ -740,14 +773,15 @@
     go_early()
     lax.fori_loop(ahead, windows, pair_back, 0)
 
-    d_cond1 = nt(d_first1, (w1h[...], w1l[...]))
-    d_cond2 = nt(split(cat([dsc2_s[...], dn2_s[...]], 1)), (w2h[...], w2l[...]))
+    d_cond1 = beside(d_first1, (w1h[...], w1l[...]), NT)
+    d_cond2 = beside(split(cat([dsc2_s[...], dn2_s[...]], 1)), (w2h[...], w2l[...]), NT)
 
     eye = (
         lax.broadcasted_iota(jnp.int32, (channels, LANES), 0) == lax.broadcasted_iota(jnp.int32, (channels, LANES), 1)
     ).astype(F32)
     gsum = jnp.sum(jnp.sum(gacc[...], axis=1), axis=-1, keepdims=True)
-    rows_g = [column_sum(gsum[h * channels : (h + 1) * channels] * eye) for h in range(heads)]
+    gless = jnp.sum(jnp.sum(gmid[...], axis=1, keepdims=True), axis=-1, keepdims=True)
+    rows_g = [column_sum((gsum[h * channels : (h + 1) * channels] - gless[h]) * eye) for h in range(heads)]
     blank = jnp.zeros((1, LANES - channels), F32)
     gain_row = cat([p_pair_gain[...], blank], 1)
     pair_row = jnp.zeros((1, LANES), F32)
@@ -771,26 +805,27 @@
         split(cat([dz1_s[...], dz2_s[...]], 1)), (wzh[...], wzl[...])
     )
 
-    def spread(slots, mine, peers, first):
+    def spread(slots, mine, peers, i):
         slots[mine] = acc_s[...]
-        return start(
-            [
-                remote(acc_s, slots.at[mine], s_send.at[first + i], s_recv.at[first + i], device)
-                for i, device in enumerate(peers)
-            ]
-        )
+        start([remote(acc_s, slots.at[mine], s_send.at[i], s_recv.at[i], device) for device in peers])
+
+        def end():
+            some = acc_e.at[0 : 16 * len(peers)]
+            remote(some, some, s_send.at[i], s_recv.at[i], other).wait()
+
+        return end
 
     go_late()
     go_early()
     wait(s1)
     acc_s[...] = acc_s[...] + recv_sc[...]
     s2 = spread(recv_sxy, k, [xy_peer(o)[1] for o in range(1, nxy)], 1)
-    wait(s2)
+    s2()
     acc_s[...] = add_up(recv_sxy, nxy)
-    s3 = spread(recv_sz, z, [z_peer(o)[1] for o in range(1, nz)], nxy)
+    s3 = spread(recv_sz, z, [z_peer(o)[1] for o in range(1, nz)], 2)
     go_late()
     go_early()
-    wait(s3)
+    s3()
     res_s[...] = add_up(recv_sz, nz)
     go_late()
     go_early()
@@ -816,8 +851,8 @@
             shapes.append((m, rows // n, LANES) if self.whole else (m - 1, rows // n // m, LANES))
         return shapes
 
-    def copies(self, nxy, nz):
-        return 2 + 2 * len(self.parts) * (nxy + nz - 2)
+    def steps(self):
+        return 5 if self.whole else 6
 
 
 def unpack_kernel(*refs):
@@ -901,6 +936,7 @@
     scratch += [buf(*tall) for _ in range(19)]
     scratch += [
         buf(heads * channels, 8, KW),
+        buf(heads, 8, KW),
         buf(early.size, LANES),
         buf(late.size, LANES),
         buf(16, LANES),
@@ -909,7 +945,7 @@
         buf(nz, 16, LANES),
         pltpu.SemaphoreType.DMA((samples,)),
     ]
-    scratch += sems(6) + sems(early.copies(nxy, nz)) + sems(late.copies(nxy, nz)) + sems(nxy + nz - 1)
+    scratch += sems(6) + sems(early.steps()) + sems(late.steps()) + sems(3)
     scratch += [buf(*shape) for plan in (early, late) for shape in plan.landing(nxy, nz)]
     arrays = [
         atom_count,
@@ -923,7 +959,7 @@
     ]
     scratch += [pltpu.SMEM(v.shape, v.dtype) for v in arrays[:3]]
     scratch += [buf(*v.shape) for v in arrays[3:-1]]
-    scratch += [pltpu.SemaphoreType.DMA((len(arrays) - 1,))]
+    scratch += [pltpu.SemaphoreType.DMA((4 + len(arrays) - 1 - 14,))]
     sizes = (samples, rows, dpn, seqn, early, late)
     big = pl.pallas_call(
         functools.partial(block_kernel, sizes),

time: 43 us -> 40.1 us (0.933)
  Pallas kernels: 42.1 us -> 39.2 us
    pallas_call x1, Pallas kernels: 38.7 us -> 35.8 us  [shards(): pl.pallas_call(functools.partial(block_kernel, sizes), out_shape=[buf(*sh...]
where the time goes in v5:
time: 40.1 us; the launch traced here: 39.9 us
  Pallas kernels  39.2 us (98%)
  between operations  0.69 us (2%)
    pallas_call x1, Pallas kernels, shards(): pl.pallas_call(functools.partial(block_kernel, sizes), out_shape=[buf(*sh...  35.8 us
    pallas_call x1, Pallas kernels, shards(): pl.pallas_call(unpack_kernel, out_shape=[jax.ShapeDtypeStruct(v.shape, F3...  3.41 us

profile of v5, /device:TPU:0, one launch (start us, length us, event | category | flops | bytes accessed | tf_op | source)
XLA Modules:
  0.0 39.9 jit_solution(4450593778486652239)
XLA Ops:
  0.7 35.8 %block.1 = (f32[512,128]{1,0:T(8,128)S(1)}, f32[512,128]{1,0:T(8,128)S(1)}, f32[512,128]{1,0:T(8,128)S(1)}, f32[2,8,16,32,128]{4,3,2,1,0:T(8,128)S(1)}, f32[1536...) custom-call(s32[2]{0:T(128)} %refs_0_.1, f32[16]{0:T(128)} %refs_1_.1, f32[4,16]{1,0:T(4,128)} %bitcast.33, ...), custom_call_target="tpu_custom_call" | custom-call | tf_op jit(solution)/shard_map/block/pallas_call | solution.py:964
  36.5 3.4 %unpack.1 = (f32[1,512,128]{2,1,0:T(8,128)}, f32[1,512,128]{2,1,0:T(8,128)}, f32[1,512,128]{2,1,0:T(8,128)}, f32[2,8,16,32,128]{4,3,2,1,0:T(8,128)}, f32[256,128...) custom-call(f32[1,512,128]{2,1,0:T(8,128)S(1)} %bitcast.27, ...), custom_call_target="tpu_custom_call" | custom-call | tf_op jit(solution)/shard_map/unpack/pallas_call | solution.py:982

commit v6 on v5

--- a/solution.py
+++ b/solution.py
@@ -273,12 +273,20 @@
     right = (dp, lax.rem(me + 1, seqn))
     other = (dp, me + 1 - 2 * core)
 
+    def flipped(index, o):
+        bit = 1
+        while bit <= o:
+            if o // bit % 2:
+                index = index + bit - 2 * bit * lax.rem(index // bit, 2)
+            bit *= 2
+        return index
+
     def xy_peer(o):
-        kk = lax.rem(k + o, nxy)
+        kk = flipped(k, o)
         return kk, (kk // nx, (z * nx + lax.rem(kk, nx)) * 2 + core)
 
     def z_peer(o):
-        zz = lax.rem(z + o, nz)
+        zz = flipped(z, o)
         return zz, (dp, (zz * nx + x) * 2 + core)
 
     norm_weights = (p_w_scale1, p_w_shift1)
@@ -405,20 +413,6 @@
         remote(kv.at[:, rows : rows + HALO], kv.at[:, 0:HALO], h_send.at[0], h_recv.at[0], right),
     )
 
-    ready(conditions, p_s_gain2, p_b_scale2, p_b_zero1, p_b_zero2)
-    hold(wzh, wzl, p_w_zero1, p_w_zero2)
-    hold(w2h, w2l, p_w_scale2, p_w_shift2)
-    scale = 1.0 / math.sqrt(32)
-    query_gate = nn(n1_split, (wqh[:, 2 * LANES :], wql[:, 2 * LANES :]))
-    qh_s[...], ql_s[...] = split((query_gate[:, :LANES] + p_b_query[...]) * scale)
-    gate_s[...] = sigmoid(query_gate[:, LANES:])
-    first2 = nn(split(ns * p_s_gain2[...]), (w2h[...], w2l[...]))
-    sc2_s[...] = sigmoid(first2[:, :LANES] + p_b_scale2[...])
-    sh2_s[...] = first2[:, LANES:]
-    zeros = nn(split(single[...]), (wzh[...], wzl[...]))
-    z1_s[...] = sigmoid(zeros[:, :LANES] + p_b_zero1[...])
-    z2_s[...] = sigmoid(zeros[:, LANES:] + p_b_zero2[...])
-
     ready(*scalars)
     channels = gain_s.shape[0]
     heads = wpair_s.shape[0]
@@ -430,7 +424,7 @@
     same = key_lane == lax.broadcasted_iota(jnp.int32, (WQ, KW), 0) + HALO
 
     def pair_bias(t, carry):
-        s, w = t // nwin, lax.rem(t, nwin)
+        s, w = divmod(t, nwin) if isinstance(t, int) else (t // nwin, lax.rem(t, nwin))
         first = pair[s, w, 0]
         total, square = first, first * first
         b = [first * centred[0][h] for h in range(heads)]
@@ -452,9 +446,28 @@
             bias[t, h * WQ : (h + 1) * WQ] = jnp.where(valid, inv * b[h], -1e9)
         return carry
 
-    for s in range(samples):
+    def pair_sample(s):
         pltpu.make_async_copy(pair_hbm.at[s], pair.at[s], pair_sem.at[s]).wait()
-        lax.fori_loop(s * nwin, (s + 1) * nwin, pair_bias, 0)
+        for t in range(s * nwin, (s + 1) * nwin):
+            pair_bias(t, 0)
+
+    ready(conditions, p_s_gain2, p_b_scale2, p_b_zero1, p_b_zero2)
+    pair_sample(0)
+    hold(wzh, wzl, p_w_zero1, p_w_zero2)
+    hold(w2h, w2l, p_w_scale2, p_w_shift2)
+    scale = 1.0 / math.sqrt(32)
+    query_gate = nn(n1_split, (wqh[:, 2 * LANES :], wql[:, 2 * LANES :]))
+    qh_s[...], ql_s[...] = split((query_gate[:, :LANES] + p_b_query[...]) * scale)
+    gate_s[...] = sigmoid(query_gate[:, LANES:])
+    first2 = nn(split(ns * p_s_gain2[...]), (w2h[...], w2l[...]))
+    sc2_s[...] = sigmoid(first2[:, :LANES] + p_b_scale2[...])
+    sh2_s[...] = first2[:, LANES:]
+    zeros = nn(split(single[...]), (wzh[...], wzl[...]))
+    z1_s[...] = sigmoid(zeros[:, :LANES] + p_b_zero1[...])
+    z2_s[...] = sigmoid(zeros[:, LANES:] + p_b_zero2[...])
+
+    for s in range(1, samples):
+        pair_sample(s)
     ready(transition, cot, p_pair_gain, p_w_pair)
     hold(whh, whl, p_w_hidden_gate, p_w_hidden_up)
     hold(wdh, wdl, p_w_down)
@@ -585,7 +598,7 @@
 
         def gathers(name, where):
             n, _, peer = groups[name]
-            return [send(res.at[where], res.at[where], peer(o)[1]) for o in range(1, n)]
+            return [send(res.at[where], res.at[where], peer(o)[1]) for o in range(n - 1, 0, -1)]
 
         places = []
         for i, (first, rows_at, rows_in) in enumerate(plan.parts):
@@ -604,7 +617,7 @@
             copies = []
             for first, _, here, one, _, _, land, _ in places:
                 n, _, peer = groups[first]
-                for o in range(1, n):
+                for o in range(n - 1, 0, -1):
                     index, device = peer(o)
                     copies.append(send(acc.at[span(here + index * one, one)], land.at[o - 1], device))
             start(copies)
@@ -617,13 +630,14 @@
                     value = value + land[o - 1]
                 acc[span(mine, one), :] = value
                 n, own_index, peer = groups[second]
-                for o in range(1, n):
+                for o in range(n - 1, 0, -1):
                     index, device = peer(o)
                     if plan.whole:
                         copies.append(send(acc.at[span(mine, one)], land2.at[own_index], device))
                     else:
                         copies.append(send(acc.at[span(mine + index * two, two)], land2.at[o - 1], device))
-            start(copies)
+                start(copies)
+                copies = []
             if plan.whole:
                 for _, second, _, one, _, mine, _, land2 in places:
                     land2[groups[second][1]] = acc[span(mine, one), :]
@@ -634,15 +648,14 @@
                 n, own_index, _ = groups[second]
                 if plan.whole:
                     res[span(mine, one), :] = add_up(land2, n)
-                    copies += gathers(first, span(mine, one))
+                    start(gathers(first, span(mine, one)))
                 else:
                     at = mine + own_index * two
                     value = acc[span(at, two), :]
                     for o in range(1, n):
                         value = value + land2[o - 1]
                     res[span(at, two), :] = value
-                    copies += gathers(second, span(at, two))
-            start(copies)
+                    start(gathers(second, span(at, two)))
             yield
             if not plan.whole:
                 arrived(sum((groups[p[1]][0] - 1) * p[4] for p in places))
@@ -819,10 +832,10 @@
     go_early()
     wait(s1)
     acc_s[...] = acc_s[...] + recv_sc[...]
-    s2 = spread(recv_sxy, k, [xy_peer(o)[1] for o in range(1, nxy)], 1)
+    s2 = spread(recv_sxy, k, [xy_peer(o)[1] for o in range(nxy - 1, 0, -1)], 1)
     s2()
     acc_s[...] = add_up(recv_sxy, nxy)
-    s3 = spread(recv_sz, z, [z_peer(o)[1] for o in range(1, nz)], 2)
+    s3 = spread(recv_sz, z, [z_peer(o)[1] for o in range(nz - 1, 0, -1)], 2)
     go_late()
     go_early()
     s3()
@@ -856,30 +869,32 @@
 
 
 def unpack_kernel(*refs):
-    n, v = len(EARLY) + len(LATE), len(VECTORS)
+    n, v = len(EARLY) + len(LATE), len(VECTORS) + 1
     ins, refs = refs[:7], refs[7:]
-    outs, mats, rows, wp, sems = refs[:4], refs[4 : 4 + n], refs[4 + n : 4 + n + v], refs[4 + n + v], refs[5 + n + v]
-    copies = []
-
-    def move(a, b):
-        copies.append(pltpu.make_async_copy(a, b, sems.at[len(copies)]))
-        copies[-1].start()
-
-    for a, b in zip(ins[3::-1], outs[::-1]):
-        for c in range(a.shape[0]):
-            move(a.at[c], b.at[c])
+    outs, mats, small, held, sems = refs[:4], refs[4 : 4 + n], refs[4 + n : 4 + n + v], refs[4 + n + v : -1], refs[-1]
+    for i, (a, b) in enumerate(zip(ins[3::-1], outs[::-1])):
+        pltpu.make_async_copy(a, b, sems.at[i]).start()
     at = 0
-    for group, packed in ((EARLY, ins[4]), (LATE, ins[5])):
+    for i, (group, packed) in enumerate(((EARLY, ins[4]), (LATE, ins[5]))):
         for name, _, columns in group:
             base, height = PLACE[name], mats[at].shape[0]
             for b in range(columns):
-                move(packed.at[pl.ds(base + b * height, height)], mats[at].at[:, pl.ds(b * LANES, LANES)])
+                pltpu.make_async_copy(
+                    packed.at[pl.ds(base + b * height, height)], mats[at].at[:, pl.ds(b * LANES, LANES)], sems.at[4 + i]
+                ).start()
             at += 1
-    for i, ref in enumerate(rows):
-        ref[...] = ins[6][i : i + 1, 0 : ref.shape[1]]
-    wp[...] = ins[6][v : v + wp.shape[0], 0 : wp.shape[1]]
-    for copy in copies:
-        copy.wait()
+    row = 0
+    for i, (mid, ref) in enumerate(zip(held, small)):
+        mid[...] = ins[6][row : row + mid.shape[0], 0 : mid.shape[1]]
+        pltpu.make_async_copy(mid, ref, sems.at[6 + i]).start()
+        row += 1
+    for i, a in enumerate(ins[3::-1]):
+        pltpu.make_async_copy(a, a, sems.at[i]).wait()
+    for i, packed in enumerate(ins[4:6]):
+        some = packed.at[0 : (EARLY_ROWS, LATE_ROWS)[i]]
+        pltpu.make_async_copy(some, some, sems.at[4 + i]).wait()
+    for i, mid in enumerate(held):
+        pltpu.make_async_copy(mid, mid, sems.at[6 + i]).wait()
 
 
 def shards(dpn, seqn, atoms, single_cond, pair_block, atom_count, *rest):
@@ -986,10 +1001,9 @@
         + vecs
         + [jax.ShapeDtypeStruct((heads, channels), F32)],
         in_specs=[vmem] * 7,
-        out_specs=[anyw] * (4 + len(mats)) + [vmem] * (len(vecs) + 1),
-        scratch_shapes=[
-            pltpu.SemaphoreType.DMA((sum(c for _, _, c in EARLY + LATE) + sum(v.shape[0] for v in big[:4]),)),
-        ],
+        out_specs=[anyw] * (5 + len(mats) + len(vecs)),
+        scratch_shapes=[buf(*v.shape) for v in vecs]
+        + [buf(heads, channels), pltpu.SemaphoreType.DMA((7 + len(vecs),))],
         compiler_params=pltpu.CompilerParams(vmem_limit_bytes=16 * 2**20),
         name="unpack",
     )(*[pltpu.with_memory_space_constraint(v, pltpu.VMEM) for v in big])

time: 40.1 us -> 39.7 us (0.990)
  Pallas kernels: 39.2 us -> 38.7 us
    pallas_call x1, Pallas kernels: 3.41 us -> 2.73 us  [shards(): pl.pallas_call(unpack_kernel, out_shape=[jax.ShapeDtypeStruct(v.shape, F3...]
where the time goes in v6:
time: 39.7 us; the launch traced here: 39.5 us
  Pallas kernels  38.7 us (97%)
  between operations  0.85 us (2%)
    pallas_call x1, Pallas kernels, shards(): pl.pallas_call(functools.partial(block_kernel, sizes), out_shape=[buf(*sh...  35.9 us
    pallas_call x1, Pallas kernels, shards(): pl.pallas_call(unpack_kernel, out_shape=[jax.ShapeDtypeStruct(v.shape, F3...  2.73 us

profile of v6, /device:TPU:0, one launch (start us, length us, event | category | flops | bytes accessed | tf_op | source)
XLA Modules:
  0.0 39.5 jit_solution(4516132480825928891)
XLA Ops:
  0.7 35.9 %block.1 = (f32[512,128]{1,0:T(8,128)S(1)}, f32[512,128]{1,0:T(8,128)S(1)}, f32[512,128]{1,0:T(8,128)S(1)}, f32[2,8,16,32,128]{4,3,2,1,0:T(8,128)S(1)}, f32[1536...) custom-call(s32[2]{0:T(128)} %refs_0_.1, f32[16]{0:T(128)} %refs_1_.1, f32[4,16]{1,0:T(4,128)} %bitcast.33, ...), custom_call_target="tpu_custom_call" | custom-call | tf_op jit(solution)/shard_map/block/pallas_call | solution.py:979
  36.6 2.7 %unpack.1 = (f32[1,512,128]{2,1,0:T(8,128)}, f32[1,512,128]{2,1,0:T(8,128)}, f32[1,512,128]{2,1,0:T(8,128)}, f32[2,8,16,32,128]{4,3,2,1,0:T(8,128)}, f32[256,128...) custom-call(f32[1,512,128]{2,1,0:T(8,128)S(1)} %bitcast.27, ...), custom_call_target="tpu_custom_call" | custom-call | tf_op jit(solution)/shard_map/unpack/pallas_call | solution.py:997

commit v7 on v6

--- a/solution.py
+++ b/solution.py
@@ -273,20 +273,12 @@
     right = (dp, lax.rem(me + 1, seqn))
     other = (dp, me + 1 - 2 * core)
 
-    def flipped(index, o):
-        bit = 1
-        while bit <= o:
-            if o // bit % 2:
-                index = index + bit - 2 * bit * lax.rem(index // bit, 2)
-            bit *= 2
-        return index
-
     def xy_peer(o):
-        kk = flipped(k, o)
+        kk = lax.rem(k + o, nxy)
         return kk, (kk // nx, (z * nx + lax.rem(kk, nx)) * 2 + core)
 
     def z_peer(o):
-        zz = flipped(z, o)
+        zz = lax.rem(z + o, nz)
         return zz, (dp, (zz * nx + x) * 2 + core)
 
     norm_weights = (p_w_scale1, p_w_shift1)
@@ -598,7 +590,7 @@
 
         def gathers(name, where):
             n, _, peer = groups[name]
-            return [send(res.at[where], res.at[where], peer(o)[1]) for o in range(n - 1, 0, -1)]
+            return [send(res.at[where], res.at[where], peer(o)[1]) for o in range(1, n)]
 
         places = []
         for i, (first, rows_at, rows_in) in enumerate(plan.parts):
@@ -617,7 +609,7 @@
             copies = []
             for first, _, here, one, _, _, land, _ in places:
                 n, _, peer = groups[first]
-                for o in range(n - 1, 0, -1):
+                for o in range(1, n):
                     index, device = peer(o)
                     copies.append(send(acc.at[span(here + index * one, one)], land.at[o - 1], device))
             start(copies)
@@ -630,7 +622,7 @@
                     value = value + land[o - 1]
                 acc[span(mine, one), :] = value
                 n, own_index, peer = groups[second]
-                for o in range(n - 1, 0, -1):
+                for o in range(1, n):
                     index, device = peer(o)
                     if plan.whole:
                         copies.append(send(acc.at[span(mine, one)], land2.at[own_index], device))
@@ -717,9 +709,9 @@
     back_keys(border)
     keys_here = swap_back(slice(0, LANES), 4)
     back_scores(middle)
+    back_keys(middle)
     go_early()
 
-    back_keys(middle)
     back_values(middle)
     for t in range(windows):
         s, at, keys = window(t)
@@ -759,7 +751,7 @@
             g_pair[s, w, p] = d
         return carry
 
-    ahead = 3 * windows // 8
+    ahead = 8 * windows // 16
     lax.fori_loop(0, ahead, pair_back, 0)
 
     values_here()
@@ -832,10 +824,10 @@
     go_early()
     wait(s1)
     acc_s[...] = acc_s[...] + recv_sc[...]
-    s2 = spread(recv_sxy, k, [xy_peer(o)[1] for o in range(nxy - 1, 0, -1)], 1)
+    s2 = spread(recv_sxy, k, [xy_peer(o)[1] for o in range(1, nxy)], 1)
     s2()
     acc_s[...] = add_up(recv_sxy, nxy)
-    s3 = spread(recv_sz, z, [z_peer(o)[1] for o in range(nz - 1, 0, -1)], 2)
+    s3 = spread(recv_sz, z, [z_peer(o)[1] for o in range(1, nz)], 2)
     go_late()
     go_early()
     s3()

time: 39.7 us -> 39.4 us (level)
  no operation moved by 1% of the time
where the time goes in v7:
time: 39.4 us; the launch traced here: 39.2 us
  Pallas kernels  38.4 us (97%)
  between operations  0.85 us (2%)
    pallas_call x1, Pallas kernels, shards(): pl.pallas_call(functools.partial(block_kernel, sizes), out_shape=[buf(*sh...  35.6 us
    pallas_call x1, Pallas kernels, shards(): pl.pallas_call(unpack_kernel, out_shape=[jax.ShapeDtypeStruct(v.shape, F3...  2.73 us

profile of v7, /device:TPU:0, one launch (start us, length us, event | category | flops | bytes accessed | tf_op | source)
XLA Modules:
  0.0 39.2 jit_solution(9388227489318075955)
XLA Ops:
  0.7 35.6 %block.1 = (f32[512,128]{1,0:T(8,128)S(1)}, f32[512,128]{1,0:T(8,128)S(1)}, f32[512,128]{1,0:T(8,128)S(1)}, f32[2,8,16,32,128]{4,3,2,1,0:T(8,128)S(1)}, f32[1536...) custom-call(s32[2]{0:T(128)} %refs_0_.1, f32[16]{0:T(128)} %refs_1_.1, f32[4,16]{1,0:T(4,128)} %bitcast.33, ...), custom_call_target="tpu_custom_call" | custom-call | tf_op jit(solution)/shard_map/block/pallas_call | solution.py:971
  36.3 2.7 %unpack.1 = (f32[1,512,128]{2,1,0:T(8,128)}, f32[1,512,128]{2,1,0:T(8,128)}, f32[1,512,128]{2,1,0:T(8,128)}, f32[2,8,16,32,128]{4,3,2,1,0:T(8,128)}, f32[256,128...) custom-call(f32[1,512,128]{2,1,0:T(8,128)S(1)} %bitcast.27, ...), custom_call_target="tpu_custom_call" | custom-call | tf_op jit(solution)/shard_map/unpack/pallas_call | solution.py:989

commit v8 on v7

--- a/solution.py
+++ b/solution.py
@@ -417,16 +417,17 @@
 
     def pair_bias(t, carry):
         s, w = divmod(t, nwin) if isinstance(t, int) else (t // nwin, lax.rem(t, nwin))
-        first = pair[s, w, 0]
-        total, square = first, first * first
-        b = [first * centred[0][h] for h in range(heads)]
+        total = pair[s, w, 0]
         for p in range(1, channels):
-            v = pair[s, w, p]
-            total = total + v
-            square = square + v * v
-            b = [b[h] + v * centred[p][h] for h in range(heads)]
+            total = total + pair[s, w, p]
         mean = total * (1.0 / channels)
-        var = square * (1.0 / channels) - mean * mean
+        square, b = None, None
+        for p in range(channels):
+            v = pair[s, w, p] - mean
+            terms = [v * centred[p][h] for h in range(heads)]
+            square = v * v if p == 0 else square + v * v
+            b = terms if p == 0 else [b[h] + terms[h] for h in range(heads)]
+        var = square * (1.0 / channels)
         inv = lax.rsqrt(jnp.maximum(var, 0.25))
         pmean[t] = mean
         live = jnp.where(var > 0.25, 1.0, jnp.where(var == 0.25, 0.5, 0.0))

time: 39.4 us -> 39.3 us (level)
  no operation moved by 1% of the time
where the time goes in v8:
time: 39.3 us; the launch traced here: 39.1 us
  Pallas kernels  38.3 us (97%)
  between operations  0.85 us (2%)
    pallas_call x1, Pallas kernels, shards(): pl.pallas_call(functools.partial(block_kernel, sizes), out_shape=[buf(*sh...  35.5 us
    pallas_call x1, Pallas kernels, shards(): pl.pallas_call(unpack_kernel, out_shape=[jax.ShapeDtypeStruct(v.shape, F3...  2.73 us

profile of v8, /device:TPU:0, one launch (start us, length us, event | category | flops | bytes accessed | tf_op | source)
XLA Modules:
  0.0 39.1 jit_solution(11450191981597154466)
XLA Ops:
  0.7 35.5 %block.1 = (f32[512,128]{1,0:T(8,128)S(1)}, f32[512,128]{1,0:T(8,128)S(1)}, f32[512,128]{1,0:T(8,128)S(1)}, f32[2,8,16,32,128]{4,3,2,1,0:T(8,128)S(1)}, f32[1536...) custom-call(s32[2]{0:T(128)} %refs_0_.1, f32[16]{0:T(128)} %refs_1_.1, f32[4,16]{1,0:T(4,128)} %bitcast.33, ...), custom_call_target="tpu_custom_call" | custom-call | tf_op jit(solution)/shard_map/block/pallas_call | solution.py:972
  36.2 2.7 %unpack.1 = (f32[1,512,128]{2,1,0:T(8,128)}, f32[1,512,128]{2,1,0:T(8,128)}, f32[1,512,128]{2,1,0:T(8,128)}, f32[2,8,16,32,128]{4,3,2,1,0:T(8,128)}, f32[256,128...) custom-call(f32[1,512,128]{2,1,0:T(8,128)S(1)} %bitcast.27, ...), custom_call_target="tpu_custom_call" | custom-call | tf_op jit(solution)/shard_map/unpack/pallas_call | solution.py:990
